TPU v7x, 32 devices: a whole 2x2x4 slice. The times are simulated.
32 devices in a mesh: dp: 8 (over y, x, core), expert: 4 (over z).
Axes of the slice: x: 2, y: 2, z: 4, core: 2. Of those that a mesh axis runs over, the one named last changes fastest.
Arguments:
- tokens: bfloat16 [10240, 2048], P(('dp', 'expert')), may hold values from -6 to 6
- cotangent: bfloat16 [10240, 2048], P(('dp', 'expert')), may hold values from -6 to 6
- norm_gains: bfloat16 [2, 2048], P(None, ('dp', 'expert')), may hold values from 0.25 to 1.75
- qkv_weight: bfloat16 [2048, 6144], P(('dp', 'expert')), may hold values from -0.125 to 0.125
- out_weight: bfloat16 [2048, 2048], P(('dp', 'expert')), may hold values from -1.5 to 1.5
- router_weight: bfloat16 [2048, 16], P(('dp', 'expert')), may hold values from -0.046875 to 0.046875
- adapter_down: bfloat16 [2048, 8, 3, 16], P(('dp', 'expert')), may hold values from -0.125 to 0.125
- adapter_qkv: bfloat16 [8, 16, 6144], P(None, None, ('dp', 'expert')), may hold values from -1.5 to 1.5
- adapter_out: bfloat16 [8, 16, 2048], P(None, None, ('dp', 'expert')), may hold values from -6 to 6
- adapter_router: bfloat16 [128, 16], P(('dp', 'expert')), may hold values from -0.5 to 0.5
- expert_input: bfloat16 [16, 2048, 2048], P('expert', 'dp'), may hold values from -0.125 to 0.125
- expert_output: bfloat16 [16, 1024, 2048], P('expert', 'dp'), may hold values from -5 to 5
- expert_down: bfloat16 [16, 2048, 8, 16], P('expert', 'dp'), may hold values from -0.125 to 0.125
- expert_lift: bfloat16 [16, 8, 16, 2048], P('expert', None, None, 'dp'), may hold values from -1.5 to 1.5
- routes: int32 [10240, 8], P(('dp', 'expert')), may hold values from 0 to 15, all different within a row; in each aligned block of 320 rows (0 to 319, 320 to 639, ...) at most 240 rows name the same one
- adapter_ids: int32 [8], P('dp'), may hold values from 0 to 7
- cont_lengths: int32 [8, 8], P('dp'), may hold values from 1 to 64, 256 in all within a row
Outputs:
- layer_output: bfloat16 [10240, 2048], P(('dp', 'expert'))
- input_grad: bfloat16 [10240, 2048], P(('dp', 'expert'))
- down_grad: float32 [2048, 8, 3, 16], P(('dp', 'expert'))
- qkv_grad: float32 [8, 16, 6144], P(None, None, ('dp', 'expert'))
- proj_grad: float32 [8, 16, 2048], P(None, None, ('dp', 'expert'))
- router_grad: float32 [128, 16], P(('dp', 'expert'))
- expdown_grad: float32 [16, 2048, 8, 16], P('expert', 'dp')
- explift_grad: float32 [16, 8, 16, 2048], P('expert', None, None, 'dp')
Inputs may be any that keep to these rules, and one draw needn't show every extreme that they name: `routes`: each row names 8 different experts; among the rows of one device no expert is named more than 240 times, a bound that some block reaches. `cont_lengths`: each group's lengths sum to 256, the longest exactly 64.
All inputs are finite; a program needn't handle non-finite values.
Results may differ from a plain program's by a relative error of at most 0.022.
Values may be sent and summed in bfloat16 or wider, within the bound.
A program may use at most 448 MiB of HBM per device.

v0:
```python
import jax
import jax.numpy as jnp
from jax import lax
from jax.sharding import PartitionSpec as P

D = 2048
HEAD = 128
FF = 1024
TOPK = 8
RANK = 16
ADAPTERS = 8
EXP_DEV = 4
PROMPT = 1024
GROUP_TOK = 1280


EPSILON = 1e-05
MASKED = -1e30


def dot_plain(left, right):
    return jnp.dot(left, right, preferred_element_type=jnp.float32)


def dot_left(left, right):
    return lax.dot_general(
        left, right, (((0,), (0,)), ((), ())), preferred_element_type=jnp.float32
    )


def dot_right(left, right):
    return lax.dot_general(
        left, right, (((1,), (1,)), ((), ())), preferred_element_type=jnp.float32
    )


def norm_forward(values, gain_row):
    inverse = lax.rsqrt(jnp.mean(values * values, axis=-1, keepdims=True) + EPSILON)
    return (values * inverse * gain_row, inverse)


def norm_backward(values, inverse, gain_row, upstream):
    scaled = upstream * gain_row
    return inverse * scaled - values * inverse**3 * jnp.mean(
        scaled * values, axis=-1, keepdims=True
    )


def segment_of(lengths, places):
    limits = PROMPT + jnp.cumsum(lengths)
    passed = jnp.sum((places[:, None] >= limits[None, :]).astype(jnp.int32), axis=1)
    return jnp.where(places < PROMPT, 0, 1 + passed)


def visible(query_segments, query_places, key_segments, key_places):
    from_prompt = (key_segments[None, :] == 0) & (query_segments[:, None] != 0)
    own_causal = (key_segments[None, :] == query_segments[:, None]) & (
        key_places[None, :] <= query_places[:, None]
    )
    return from_prompt | own_causal


def pick_dense(gathered, adapter):
    gain_rows, qkv_full, out_full, router_full, down_all, qkv_all, out_all, router_all = gathered
    down_pick = lax.dynamic_index_in_dim(down_all, adapter, 1, keepdims=False)
    router_lift = lax.dynamic_index_in_dim(
        router_all.reshape(ADAPTERS, RANK, -1), adapter, 0, keepdims=False
    )
    return (
        gain_rows.astype(jnp.float32),
        qkv_full,
        out_full,
        router_full,
        down_pick[:, 0],
        down_pick[:, 1],
        down_pick[:, 2],
        lax.dynamic_index_in_dim(qkv_all, adapter, 0, keepdims=False),
        lax.dynamic_index_in_dim(out_all, adapter, 0, keepdims=False),
        router_lift,
    )


def pick_expert(gathered, adapter):
    input_full, output_full, down_all, lift_all = gathered
    return (
        input_full,
        output_full,
        lax.dynamic_index_in_dim(down_all, adapter, 2, keepdims=False),
        lax.dynamic_index_in_dim(lift_all, adapter, 1, keepdims=False),
    )


def slot_index(routes, experts, capacity):
    flat_routes = routes.reshape(-1)
    onehot = (flat_routes[:, None] == jnp.arange(experts, dtype=jnp.int32)[None, :]).astype(
        jnp.int32
    )
    earlier = jnp.cumsum(onehot, axis=0) - onehot
    return flat_routes * capacity + jnp.sum(earlier * onehot, axis=1)


def spread_rows(rows, targets, total_slots):
    buffer = jnp.zeros((total_slots, rows.shape[-1]), rows.dtype)
    return buffer.at[targets].set(rows)


def masked_scores(queries, keys, allowed, scale):
    scores = jnp.einsum("thd,shd->hts", queries, keys, preferred_element_type=jnp.float32) * scale
    return jnp.where(allowed[None], scores, MASKED)


def body(
    tokens,
    cotangent,
    norm_gains,
    qkv_weight,
    out_weight,
    router_weight,
    adapter_down,
    adapter_qkv,
    adapter_out,
    adapter_router,
    expert_input,
    expert_output,
    expert_down,
    expert_lift,
    routes,
    adapter_ids,
    cont_lengths,
):
    piece = tokens.shape[0]
    heads = D // HEAD
    scale = HEAD ** (-0.5)
    parts = lax.axis_size("expert")
    experts = EXP_DEV * parts
    capacity = 3 * piece * TOPK // (2 * experts)
    total_slots = experts * capacity
    first = lax.axis_index("expert") * piece
    adapter = adapter_ids[0]
    places = jnp.arange(GROUP_TOK, dtype=jnp.int32)
    segments = segment_of(cont_lengths[0], places)
    query_places = first + jnp.arange(piece, dtype=jnp.int32)
    query_segments = lax.dynamic_slice_in_dim(segments, first, piece)
    allowed = visible(query_segments, query_places, segments, places)
    dense_full = (
        lax.all_gather(norm_gains, ("dp", "expert"), axis=1, tiled=True),
        lax.all_gather(qkv_weight, ("dp", "expert"), axis=0, tiled=True),
        lax.all_gather(out_weight, ("dp", "expert"), axis=0, tiled=True),
        lax.all_gather(router_weight, ("dp", "expert"), axis=0, tiled=True),
        lax.all_gather(adapter_down, ("dp", "expert"), axis=0, tiled=True),
        lax.all_gather(adapter_qkv, ("dp", "expert"), axis=2, tiled=True),
        lax.all_gather(adapter_out, ("dp", "expert"), axis=2, tiled=True),
        lax.all_gather(adapter_router, ("dp", "expert"), axis=0, tiled=True),
    )
    dense_pick = pick_dense(dense_full, adapter)
    expert_full = (
        lax.all_gather(expert_input, "dp", axis=1, tiled=True),
        lax.all_gather(expert_output, "dp", axis=1, tiled=True),
        lax.all_gather(expert_down, "dp", axis=1, tiled=True),
        lax.all_gather(expert_lift, "dp", axis=3, tiled=True),
    )
    expert_pick = pick_expert(expert_full, adapter)
    (
        gain_rows,
        qkv_matrix,
        out_matrix,
        router_matrix,
        down_query,
        down_mix,
        down_route,
        lift_query,
        lift_mix,
        lift_route,
    ) = dense_pick
    input_matrix, output_matrix, down_expert, lift_expert = expert_pick
    inputs = tokens.astype(jnp.float32)
    normed, inverse_first = norm_forward(inputs, gain_rows[0])
    normed_low = normed.astype(jnp.bfloat16)
    rank_query = dot_plain(normed_low, down_query).astype(jnp.bfloat16)
    qkv_low = (dot_plain(normed_low, qkv_matrix) + dot_plain(rank_query, lift_query)).astype(
        jnp.bfloat16
    )
    queries = qkv_low[:, :D].reshape(piece, heads, HEAD)
    keys_own = qkv_low[:, D : 2 * D]
    values_own = qkv_low[:, 2 * D :]
    keys_all, values_all = (
        lax.all_gather(keys_own, "expert", axis=0, tiled=True),
        lax.all_gather(values_own, "expert", axis=0, tiled=True),
    )
    key_heads = keys_all.reshape(GROUP_TOK, heads, HEAD)
    value_heads = values_all.reshape(GROUP_TOK, heads, HEAD)
    scores = masked_scores(queries, key_heads, allowed, scale)
    top_score = jnp.max(scores, axis=-1, keepdims=True)
    expd = jnp.exp(scores - top_score)
    total = jnp.sum(expd, axis=-1, keepdims=True)
    log_total = top_score + jnp.log(total)
    probs_low = (expd / total).astype(jnp.bfloat16)
    mixed_low = (
        jnp.einsum("hts,shd->thd", probs_low, value_heads, preferred_element_type=jnp.float32)
        .reshape(piece, D)
        .astype(jnp.bfloat16)
    )
    rank_mix = dot_plain(mixed_low, down_mix).astype(jnp.bfloat16)
    middle = inputs + dot_plain(mixed_low, out_matrix) + dot_plain(rank_mix, lift_mix)
    second, inverse_second = norm_forward(middle, gain_rows[1])
    second_low = second.astype(jnp.bfloat16)
    rank_route = dot_plain(second_low, down_route).astype(jnp.bfloat16)
    logits = dot_plain(second_low, router_matrix) + dot_plain(rank_route, lift_route)
    logit_top = jnp.max(logits, axis=-1, keepdims=True)
    logit_exp = jnp.exp(logits - logit_top)
    router_probs = logit_exp / jnp.sum(logit_exp, axis=-1, keepdims=True)
    gates = jnp.take_along_axis(router_probs, routes, axis=1)
    targets = slot_index(routes, experts, capacity)
    token_of = jnp.arange(piece * TOPK, dtype=jnp.int32) // TOPK
    outgoing = spread_rows(second_low[token_of], targets, total_slots).reshape(
        parts, EXP_DEV, capacity, D
    )
    arrived = lax.all_to_all(outgoing, "expert", split_axis=0, concat_axis=0, tiled=True)
    rank_expert = jnp.einsum(
        "sjcd,jdr->sjcr", arrived, down_expert, preferred_element_type=jnp.float32
    ).astype(jnp.bfloat16)
    gate_up = jnp.einsum(
        "sjcd,jdf->sjcf", arrived, input_matrix, preferred_element_type=jnp.float32
    )
    gate_up = gate_up + jnp.einsum(
        "sjcr,jrf->sjcf", rank_expert, lift_expert, preferred_element_type=jnp.float32
    )
    gate_part = gate_up[..., :FF]
    hidden = (gate_part * jax.nn.sigmoid(gate_part) * gate_up[..., FF:]).astype(jnp.bfloat16)
    result = jnp.einsum(
        "sjcf,jfd->sjcd", hidden, output_matrix, preferred_element_type=jnp.float32
    ).astype(jnp.bfloat16)
    result, gate_up, rank_expert, arrived = (result, gate_up, rank_expert, arrived)
    returned = lax.all_to_all(result, "expert", split_axis=0, concat_axis=0, tiled=True)
    picked = returned.reshape(total_slots, D)[targets].reshape(piece, TOPK, D)
    layer_output = (middle + jnp.sum(gates[:, :, None] * picked, axis=1)).astype(jnp.bfloat16)
    upstream = cotangent.astype(jnp.float32)
    gate_grad = jnp.sum(upstream[:, None, :] * picked, axis=2)
    slot_grad = (
        (gates[:, :, None] * upstream[:, None, :]).astype(jnp.bfloat16).reshape(piece * TOPK, D)
    )
    outgoing_grad = spread_rows(slot_grad, targets, total_slots).reshape(
        parts, EXP_DEV, capacity, D
    )
    arrived_grad = lax.all_to_all(outgoing_grad, "expert", split_axis=0, concat_axis=0, tiled=True)
    expert_back = pick_expert(
        (
            lax.all_gather(expert_input, "dp", axis=1, tiled=True),
            lax.all_gather(expert_output, "dp", axis=1, tiled=True),
            lax.all_gather(expert_down, "dp", axis=1, tiled=True),
            lax.all_gather(expert_lift, "dp", axis=3, tiled=True),
        ),
        adapter,
    )
    dense_back = pick_dense(
        (
            lax.all_gather(norm_gains, ("dp", "expert"), axis=1, tiled=True),
            lax.all_gather(qkv_weight, ("dp", "expert"), axis=0, tiled=True),
            lax.all_gather(out_weight, ("dp", "expert"), axis=0, tiled=True),
            lax.all_gather(router_weight, ("dp", "expert"), axis=0, tiled=True),
            lax.all_gather(adapter_down, ("dp", "expert"), axis=0, tiled=True),
            lax.all_gather(adapter_qkv, ("dp", "expert"), axis=2, tiled=True),
            lax.all_gather(adapter_out, ("dp", "expert"), axis=2, tiled=True),
            lax.all_gather(adapter_router, ("dp", "expert"), axis=0, tiled=True),
        ),
        adapter,
    )
    input_matrix, output_matrix, down_expert, lift_expert = expert_back
    (
        gain_rows,
        qkv_matrix,
        out_matrix,
        router_matrix,
        down_query,
        down_mix,
        down_route,
        lift_query,
        lift_mix,
        lift_route,
    ) = dense_back
    hidden_grad = jnp.einsum(
        "sjcd,jfd->sjcf", arrived_grad, output_matrix, preferred_element_type=jnp.float32
    )
    gate_part = gate_up[..., :FF]
    up_part = gate_up[..., FF:]
    sigma = jax.nn.sigmoid(gate_part)
    gate_up_grad = jnp.concatenate(
        [
            hidden_grad * up_part * sigma * (1.0 + gate_part * (1.0 - sigma)),
            hidden_grad * gate_part * sigma,
        ],
        axis=-1,
    ).astype(jnp.bfloat16)
    rank_expert_grad = jnp.einsum(
        "sjcf,jrf->sjcr", gate_up_grad, lift_expert, preferred_element_type=jnp.float32
    ).astype(jnp.bfloat16)
    slot_input_grad = jnp.einsum(
        "sjcf,jdf->sjcd", gate_up_grad, input_matrix, preferred_element_type=jnp.float32
    )
    slot_input_grad = (
        slot_input_grad
        + jnp.einsum(
            "sjcr,jdr->sjcd", rank_expert_grad, down_expert, preferred_element_type=jnp.float32
        )
    ).astype(jnp.bfloat16)
    lift_expert_grad = jnp.einsum(
        "sjcr,sjcf->jrf", rank_expert, gate_up_grad, preferred_element_type=jnp.float32
    )
    down_expert_grad = jnp.einsum(
        "sjcd,sjcr->jdr", arrived, rank_expert_grad, preferred_element_type=jnp.float32
    )
    returned_grad = lax.all_to_all(
        slot_input_grad, "expert", split_axis=0, concat_axis=0, tiled=True
    )
    expert_part = jnp.sum(
        returned_grad.reshape(total_slots, D)[targets].reshape(piece, TOPK, D).astype(jnp.float32),
        axis=1,
    )
    expert_ids = jnp.arange(experts, dtype=jnp.int32)
    prob_grad = jnp.sum(
        jnp.where(routes[:, :, None] == expert_ids[None, None, :], gate_grad[:, :, None], 0.0),
        axis=1,
    )
    logit_grad = (
        router_probs * (prob_grad - jnp.sum(router_probs * prob_grad, axis=1, keepdims=True))
    ).astype(jnp.bfloat16)
    rank_route_grad = dot_right(logit_grad, lift_route).astype(jnp.bfloat16)
    second_grad = (
        expert_part + dot_right(logit_grad, router_matrix) + dot_right(rank_route_grad, down_route)
    )
    lift_route_grad = dot_left(rank_route, logit_grad)
    down_route_grad = dot_left(second_low, rank_route_grad)
    middle_grad = upstream + norm_backward(middle, inverse_second, gain_rows[1], second_grad)
    branch_grad = middle_grad.astype(jnp.bfloat16)
    rank_mix_grad = dot_right(branch_grad, lift_mix).astype(jnp.bfloat16)
    mixed_grad = (dot_right(branch_grad, out_matrix) + dot_right(rank_mix_grad, down_mix)).astype(
        jnp.bfloat16
    )
    lift_mix_grad = dot_left(rank_mix, branch_grad)
    down_mix_grad = dot_left(mixed_low, rank_mix_grad)
    grad_heads = mixed_grad.reshape(piece, heads, HEAD)
    probs = jnp.exp(masked_scores(queries, key_heads, allowed, scale) - log_total)
    prob_back = jnp.einsum(
        "thd,shd->hts", grad_heads, value_heads, preferred_element_type=jnp.float32
    )
    delta = jnp.sum(probs * prob_back, axis=-1, keepdims=True)
    score_grad = (probs * (prob_back - delta)).astype(jnp.bfloat16)
    query_grad = (
        jnp.einsum(
            "hts,shd->thd", score_grad, key_heads, preferred_element_type=jnp.float32
        ).reshape(piece, D)
        * scale
    )
    key_terms = (
        jnp.einsum("hts,thd->shd", score_grad, queries, preferred_element_type=jnp.float32).reshape(
            GROUP_TOK, D
        )
        * scale
    )
    value_terms = jnp.einsum(
        "hts,thd->shd", probs.astype(jnp.bfloat16), grad_heads, preferred_element_type=jnp.float32
    ).reshape(GROUP_TOK, D)
    key_grad, value_grad = (
        lax.psum_scatter(
            key_terms.astype(jnp.bfloat16), "expert", scatter_dimension=0, tiled=True
        ).astype(jnp.float32),
        lax.psum_scatter(
            value_terms.astype(jnp.bfloat16), "expert", scatter_dimension=0, tiled=True
        ).astype(jnp.float32),
    )
    qkv_back = jnp.concatenate([query_grad, key_grad, value_grad], axis=1).astype(jnp.bfloat16)
    rank_query_grad = dot_right(qkv_back, lift_query).astype(jnp.bfloat16)
    first_grad = dot_right(qkv_back, qkv_matrix) + dot_right(rank_query_grad, down_query)
    lift_query_grad = dot_left(rank_query, qkv_back)
    down_query_grad = dot_left(normed_low, rank_query_grad)
    input_grad = (
        middle_grad + norm_backward(inputs, inverse_first, gain_rows[0], first_grad)
    ).astype(jnp.bfloat16)
    chosen = (jnp.arange(ADAPTERS, dtype=jnp.int32) == adapter).astype(jnp.float32)
    down_local = jnp.stack([down_query_grad, down_mix_grad, down_route_grad], axis=1)
    router_terms = (chosen[:, None, None] * lift_route_grad[None]).reshape(ADAPTERS * RANK, experts)
    down_terms = down_local[:, None] * chosen[None, :, None, None]
    qkv_terms = chosen[:, None, None] * lift_query_grad[None]
    proj_terms = chosen[:, None, None] * lift_mix_grad[None]
    down_grad, qkv_grad, proj_grad, router_grad = (
        lax.psum_scatter(down_terms, ("dp", "expert"), scatter_dimension=0, tiled=True),
        lax.psum_scatter(qkv_terms, ("dp", "expert"), scatter_dimension=2, tiled=True),
        lax.psum_scatter(proj_terms, ("dp", "expert"), scatter_dimension=2, tiled=True),
        lax.psum_scatter(router_terms, ("dp", "expert"), scatter_dimension=0, tiled=True),
    )
    expdown_terms = down_expert_grad[:, :, None, :] * chosen[None, None, :, None]
    explift_terms = lift_expert_grad[:, None] * chosen[None, :, None, None]
    expdown_grad, explift_grad = (
        lax.psum_scatter(
            expdown_terms.astype(jnp.bfloat16), "dp", scatter_dimension=1, tiled=True
        ).astype(jnp.float32),
        lax.psum_scatter(
            explift_terms.astype(jnp.bfloat16), "dp", scatter_dimension=3, tiled=True
        ).astype(jnp.float32),
    )
    return (
        layer_output,
        input_grad,
        down_grad,
        qkv_grad,
        proj_grad,
        router_grad,
        expdown_grad,
        explift_grad,
    )


def solution(mesh):
    placed = (
        P(("dp", "expert"), None),
        P(("dp", "expert"), None),
        P(None, ("dp", "expert")),
        P(("dp", "expert"), None),
        P(("dp", "expert"), None),
        P(("dp", "expert"), None),
        P(("dp", "expert"), None, None, None),
        P(None, None, ("dp", "expert")),
        P(None, None, ("dp", "expert")),
        P(("dp", "expert"), None),
        P("expert", "dp", None),
        P("expert", "dp", None),
        P("expert", "dp", None, None),
        P("expert", None, None, "dp"),
        P(("dp", "expert"), None),
        P("dp"),
        P("dp", None),
    )
    return jax.shard_map(
        body,
        mesh=mesh,
        in_specs=placed,
        out_specs=(
            P(("dp", "expert"), None),
            P(("dp", "expert"), None),
            P(("dp", "expert"), None, None, None),
            P(None, None, ("dp", "expert")),
            P(None, None, ("dp", "expert")),
            P(("dp", "expert"), None),
            P("expert", "dp", None, None),
            P("expert", None, None, "dp"),
        ),
        check_vma=False,
    )
```

profile of v0, /device:TPU:9, one launch (start us, length us, event | category | flops | bytes accessed | tf_op | source)
XLA Modules:
  0.0 3086.3 jit_solution(16722686251901488556)
XLA Ops:
  12.4 58.9 %all-gather = bf16[32,64,2]{1,2,0:T(2,128)(2,1)S(1)} all-gather(bf16[1,64,2]{1,2,0:T(2,128)(2,1)} %bitcast.326), channel_id=1, replica_groups=mesh['dp'=8,'expert'=4] {'dp','expert'}, dimensions={0}, use_global_device_ids=true | all-gather | bytes 8448 | tf_op jit(solution)/shard_map/all_gather | solution.py:146
  73.7 34.9 %all-gather.16.cloned.1.call-done = bf16[2048,8,3,16]{3,1,2,0:T(8,128)(2,1)} async-done(((bf16[64,8,3,16]{3,1,2,0:T(8,128)(2,1)}), bf16[2048,8,3,16]{3,1,2,0:T(8,128)(2,1)}) %all-gather.16.cloned.1.call-update) | async-done | bytes 1572880 | tf_op jit(solution)/shard_map/all_gather | solution.py:150
  119.4 87.0 %all-gather.18.cloned.1.call-done = bf16[8,16,6144]{1,0,2:T(8,128)(2,1)} async-done(((bf16[8,16,192]{1,0,2:T(8,128)(2,1)}), bf16[8,16,6144]{1,0,2:T(8,128)(2,1)}) %all-gather.18.cloned.1.call-update) | async-done | bytes 1572880 | tf_op jit(solution)/shard_map/all_gather | solution.py:151
  218.7 142.3 %all-gather.14.cloned.1.call-done = bf16[2048,6144]{1,0:T(8,128)(2,1)} async-done(((bf16[64,6144]{1,0:T(8,128)(2,1)}), bf16[2048,6144]{1,0:T(8,128)(2,1)}) %all-gather.14.cloned.1.call-update) | async-done | bytes 25165840 | tf_op jit(solution)/shard_map/all_gather | solution.py:147
  386.8 202.5 %all_gather.61 = bf16[8,16,2048]{1,0,2:T(8,128)(2,1)S(1)} all-gather(bf16[8,16,64]{1,0,2:T(8,128)(2,1)S(1)} %copy.207), channel_id=1, replica_groups=mesh['dp'=8,'expert'=4] {'dp','expert'}, dimensions={2}, use_global_device_ids=true | all-gather | bytes 540672 | tf_op jit(solution)/shard_map/all_gather | solution.py:152
  615.3 32.6 %all-gather.20.cloned.1.call-done = bf16[1280,2048]{1,0:T(8,128)(2,1)} async-done(((bf16[320,2048]{1,0:T(8,128)(2,1)}), bf16[1280,2048]{1,0:T(8,128)(2,1)}) %all-gather.20.cloned.1.call-update) | async-done | bytes 5242896 | tf_op jit(solution)/shard_map/all_gather | solution.py:188
  661.7 68.9 %all-gather.24.cloned.1.call-done = bf16[2048,2048]{1,0:T(8,128)(2,1)} async-done(((bf16[64,2048]{1,0:T(8,128)(2,1)}), bf16[2048,2048]{1,0:T(8,128)(2,1)}) %all-gather.24.cloned.1.call-update) | async-done | bytes 8388624 | tf_op jit(solution)/shard_map/all_gather | solution.py:148
  738.3 57.7 %scatter_custom_fusion = bf16[3840,2048]{1,0:T(8,128)(2,1)} fusion(s32[2560]{0:T(1024)S(1)} %fusion.131, bf16[320,2048]{1,0:T(8,128)(2,1)S(1)} %multiply_convert_fusion.7, s32[3072]{0:T(1024)S(1)} %pad_clamp_fusion.1, bf16[]{:T(256)} %constant.113.clone.1), kind=kCustom, calls=%fused_computation.51 | custom fusion | bytes 15728642 | tf_op jit(solution)/shard_map/scatter | solution.py:104
  804.7 388.7 %all-gather.1 = bf16[32,64,16]{1,2,0:T(8,128)(2,1)S(1)} all-gather(bf16[1,64,16]{1,2,0:T(8,128)(2,1)S(1)} %bitcast.324), channel_id=1, replica_groups=mesh['dp'=8,'expert'=4] {'dp','expert'}, dimensions={0}, use_global_device_ids=true | all-gather | bytes 67584 | tf_op jit(solution)/shard_map/all_gather | solution.py:149
  1195.6 68.0 %all-gather.2 = bf16[32,4,16]{2,1,0:T(4,128)(2,1)S(1)} all-gather(bf16[1,4,16]{2,1,0:T(4,128)(2,1)S(1)} %bitcast.325), channel_id=1, replica_groups=mesh['dp'=8,'expert'=4] {'dp','expert'}, dimensions={0}, use_global_device_ids=true | all-gather | bytes 4224 | tf_op jit(solution)/shard_map/all_gather | solution.py:153
  1345.0 45.4 %bitcast_add_fusion.1 = f32[4,4,240,2048]{3,2,0,1:T(8,128)} fusion(f32[4,2048,4,240]{1,3,2,0:T(8,128)} %fusion.111, bf16[4,2048,2048]{2,1,0:T(8,128)(2,1)} %all-gather.26.cloned.1.call-done, bf16[4,4,240,2048]{3,2,1,0:T(8,128)(2,1)} %all-to-all-done), kind=kOutput, calls=%fused_computation.12 | convolution fusion | flops 32220119040 | bytes 112197632 | tf_op jit(solution)/shard_map/sjcd,jdf->sjcf/dot_general | solution.py:222
  1390.4 28.4 convert_bitcast_fusion
  1432.3 221.2 %all-to-all-done.2 = bf16[4,4,240,2048]{3,2,1,0:T(8,128)(2,1)} async-done(((bf16[4,4,240,2048]{3,2,1,0:T(8,128)(2,1)}), bf16[4,4,240,2048]{3,2,1,0:T(8,128)(2,1)}, u32[]{:S(2)}, u32[]{:S(2)}) %all-to-all-start.2) | async-done | bytes 15728672 | tf_op jit(solution)/shard_map/all_to_all | solution.py:245
  1668.5 31.8 %fusion.20 = (bf16[4,4,240,1024]{3,2,0,1:T(8,128)(2,1)}, bf16[4,4,240,1024]{3,2,0,1:T(8,128)(2,1)}) fusion(f32[4,4,240,2048]{3,2,0,1:T(8,128)} %bitcast_add_fusion.1, bf16[4,1024,2048]{2,1,0:T(8,128)(2,1)} %all-gather.32.cloned.1.call-done, bf16[4,4,240,2048]{3,2,1,0:T(8,128)(2,1)} %all-to-all-done.2), kind=kOutput, calls=%fused_computation.37 | convolution fusion | flops 16157245440 | bytes 79691776 | tf_op jit(solution)/shard_map/sjcd,jfd->sjcf/dot_general | solution.py:281
  1722.5 41.4 %fusion.4 = bf16[4,4,240,2048]{3,2,0,1:T(8,128)(2,1)} fusion(f32[4,2048,4,240]{1,3,2,0:T(8,128)} %fusion.113, bf16[4,2048,2048]{2,1,0:T(8,128)(2,1)} %all-gather.26.cloned.1.call-done, bf16[4,4,240,1024]{3,2,0,1:T(8,128)(2,1)} %get-tuple-element.13, bf16[4,4,240,1024]{3,2,0,1:T(8,128)(2,1)S(1)} %bitcast.331), kind=kOutput, calls=%fused_computation.11 | convolution fusion | flops 32259440640 | bytes 96468992 | tf_op jit(solution)/shard_map/sjcf,jdf->sjcd/dot_general | solution.py:297
  1777.5 226.9 %all-to-all-done.1 = bf16[4,4,240,2048]{3,2,1,0:T(8,128)(2,1)} async-done(((bf16[4,4,240,2048]{3,2,1,0:T(8,128)(2,1)}), bf16[4,4,240,2048]{3,2,1,0:T(8,128)(2,1)}, u32[]{:S(2)}, u32[]{:S(2)}) %all-to-all-start.1) | async-done | bytes 15728672 | tf_op jit(solution)/shard_map/all_to_all | solution.py:234
  2055.4 295.7 %all-to-all-done.3 = bf16[4,4,240,2048]{3,2,1,0:T(8,128)(2,1)} async-done(((bf16[4,4,240,2048]{3,2,1,0:T(8,128)(2,1)}), bf16[4,4,240,2048]{3,2,1,0:T(8,128)(2,1)}, u32[]{:S(2)}, u32[]{:S(2)}) %all-to-all-start.3) | async-done | bytes 15728672 | tf_op jit(solution)/shard_map/all_to_all | solution.py:312
  2515.5 29.7 reduce-scatter.14.cloned.1.call-done
  2547.8 93.8 %reduce-scatter.16.cloned.1.call-done = bf16[320,2048]{1,0:T(8,128)(2,1)} async-done(((bf16[1280,2048]{1,0:T(8,128)(2,1)}), bf16[320,2048]{1,0:T(8,128)(2,1)}) %reduce-scatter.16.cloned.1.call-update) | async-done | bytes 1310736 | tf_op jit(solution)/shard_map/reduce_scatter | solution.py:367
  2688.5 42.9 %reduce-scatter.18.cloned.1.call-done = bf16[4,256,8,16]{1,3,2,0:T(8,128)(2,1)} async-done(((bf16[4,2048,8,16]{1,3,2,0:T(8,128)(2,1)}), bf16[4,256,8,16]{1,3,2,0:T(8,128)(2,1)}) %reduce-scatter.18.cloned.1.call-update) | async-done | bytes 262160 | tf_op jit(solution)/shard_map/reduce_scatter | solution.py:394
  2746.2 39.5 %all-reduce = f32[128,16]{1,0:T(8,128)S(1)} all-reduce(f32[128,16]{1,0:T(8,128)S(1)} %bitcast_multiply_fusion.3), channel_id=7, replica_groups=mesh['dp'=8,'expert'=4] {'dp','expert'}, use_global_device_ids=true, to_apply=%region_26.27.clone | all-reduce | flops 2048 | bytes 16384
  2786.4 73.2 %reduce-scatter.26.cloned.1.call-done = f32[64,128]{1,0:T(8,128)} async-done(((f32[2048,128]{1,0:T(8,128)}), f32[64,128]{1,0:T(8,128)}) %reduce-scatter.26.cloned.1.call-update) | async-done | bytes 32784
  2881.4 90.0 %reduce-scatter.24.cloned.1.call-done = f32[192,128]{1,0:T(8,128)} async-done(((f32[6144,128]{1,0:T(8,128)}), f32[192,128]{1,0:T(8,128)}) %reduce-scatter.24.cloned.1.call-update) | async-done | bytes 98320
  2973.5 104.5 %reduce-scatter.22.cloned.1.call-done = f32[64,384]{1,0:T(8,128)} async-done(((f32[2048,384]{1,0:T(8,128)}), f32[64,384]{1,0:T(8,128)}) %reduce-scatter.22.cloned.1.call-update) | async-done | bytes 98320
  (323 shorter events, 564.6 us)
Async XLA Ops:
  7.2 101.4 %all-gather.16.cloned.1.call-start = ((), (), s32[]{:S(2)}) async-start(), calls=%async_computation.12 | async-start | bytes 12976128 | tf_op jit(solution)/shard_map/all_gather | solution.py:150
  9.1 197.3 %all-gather.18.cloned.1.call-start = ((), (), s32[]{:S(2)}) async-start(), calls=%async_computation.13 | async-start | bytes 12976128 | tf_op jit(solution)/shard_map/all_gather | solution.py:151
  11.0 350.0 %all-gather.14.cloned.1.call-start = ((), (), s32[]{:S(2)}) async-start(), calls=%async_computation.11 | async-start | bytes 25952256 | tf_op jit(solution)/shard_map/all_gather | solution.py:147
  11.7 580.9 %all-gather.22.cloned.1.call-start = ((), (), s32[]{:S(2)}) async-start(), calls=%async_computation.15 | async-start | bytes 6553600 | tf_op jit(solution)/shard_map/all_gather | solution.py:187
  73.7 663.4 %copy-start.37 = (f32[1,2048]{1,0:T(1,128)}, f32[1,2048]{1,0:T(1,128)S(1)}, u32[]{:S(2)}) copy-start(f32[1,2048]{1,0:T(1,128)S(1)} %get-tuple-element.19) | copy-start | bytes 24580
  119.4 1144.2 %copy-start.19 = (bf16[2048,1,3,16]{0,3,2,1:T(8,128)(2,1)}, bf16[2048,1,3,16]{0,3,2,1:T(8,128)(2,1)S(1)}, u32[]{:S(2)}) copy-start(bf16[2048,1,3,16]{0,3,2,1:T(8,128)(2,1)S(1)} %copy.245) | copy-start | bytes 589828
  377.2 270.7 %all-gather.20.cloned.1.call-start = ((), (), s32[]{:S(2)}) async-start(), calls=%async_computation.14 | async-start | bytes 6553600 | tf_op jit(solution)/shard_map/all_gather | solution.py:188
  377.8 352.8 %all-gather.24.cloned.1.call-start = ((), (), s32[]{:S(2)}) async-start(), calls=%async_computation.16 | async-start | bytes 8650752 | tf_op jit(solution)/shard_map/all_gather | solution.py:148
  378.3 943.5 %all-gather.30.cloned.1.call-start = ((), (), s32[]{:S(2)}) async-start(), calls=%async_computation.19 | async-start | bytes 2359296 | tf_op jit(solution)/shard_map/all_gather | solution.py:159
  379.1 952.4 %all-gather.28.cloned.1.call-start = ((), (), s32[]{:S(2)}) async-start(), calls=%async_computation.18 | async-start | bytes 2359296 | tf_op jit(solution)/shard_map/all_gather | solution.py:160
  379.8 965.2 %all-gather.26.cloned.1.call-start = ((), (), s32[]{:S(2)}) async-start(), calls=%async_computation.17 | async-start | bytes 37748736 | tf_op jit(solution)/shard_map/all_gather | solution.py:157
  591.9 698.0 %copy-start.45 = (s32[2560]{0:T(1024)}, s32[2560]{0:T(1024)S(1)}, u32[]{:S(2)}) copy-start(s32[2560]{0:T(1024)S(1)} %fusion.131) | copy-start | bytes 30724
  796.0 518.7 %all-to-all-start = ((bf16[4,4,240,2048]{3,2,1,0:T(8,128)(2,1)}), bf16[4,4,240,2048]{3,2,1,0:T(8,128)(2,1)}, u32[]{:S(2)}, u32[]{:S(2)}) async-start(bf16[4,4,240,2048]{3,2,1,0:T(8,128)(2,1)} %bitcast.296), calls=%async_computation | async-start | bytes 31457280 | tf_op jit(solution)/shard_map/all_to_all | solution.py:218
  804.1 586.2 %all-gather.32.cloned.1.call-start = ((), (), s32[]{:S(2)}) async-start(), calls=%async_computation.20 | async-start | bytes 18874368 | tf_op jit(solution)/shard_map/all_gather | solution.py:158
  1314.7 338.9 %all-to-all-start.2 = ((bf16[4,4,240,2048]{3,2,1,0:T(8,128)(2,1)}), bf16[4,4,240,2048]{3,2,1,0:T(8,128)(2,1)}, u32[]{:S(2)}, u32[]{:S(2)}) async-start(bf16[4,4,240,2048]{3,2,1,0:T(8,128)(2,1)} %bitcast.297), calls=%async_computation.2 | async-start | bytes 31457280 | tf_op jit(solution)/shard_map/all_to_all | solution.py:245
  1653.5 350.9 %all-to-all-start.1 = ((bf16[4,4,240,2048]{3,2,1,0:T(8,128)(2,1)}), bf16[4,4,240,2048]{3,2,1,0:T(8,128)(2,1)}, u32[]{:S(2)}, u32[]{:S(2)}) async-start(bf16[4,4,240,2048]{3,2,1,0:T(8,128)(2,1)} %copy.218), calls=%async_computation.1 | async-start | bytes 31457280 | tf_op jit(solution)/shard_map/all_to_all | solution.py:234
  2004.4 346.7 %all-to-all-start.3 = ((bf16[4,4,240,2048]{3,2,1,0:T(8,128)(2,1)}), bf16[4,4,240,2048]{3,2,1,0:T(8,128)(2,1)}, u32[]{:S(2)}, u32[]{:S(2)}) async-start(bf16[4,4,240,2048]{3,2,1,0:T(8,128)(2,1)} %copy.221), calls=%async_computation.3 | async-start | bytes 31457280 | tf_op jit(solution)/shard_map/all_to_all | solution.py:312
  2015.2 530.0 %reduce-scatter.14.cloned.1.call-start = ((), (), s32[]{:S(2)}) async-start(), calls=%async_computation.21 | async-start | bytes 6553600 | tf_op jit(solution)/shard_map/reduce_scatter | solution.py:364
  2448.5 193.1 %reduce-scatter.16.cloned.1.call-start = ((), (), s32[]{:S(2)}) async-start(), calls=%async_computation.22 | async-start | bytes 6553600 | tf_op jit(solution)/shard_map/reduce_scatter | solution.py:367
  2470.5 216.2 %reduce-scatter.20.cloned.1.call-start = ((), (), s32[]{:S(2)}) async-start(), calls=%async_computation.24 | async-start | bytes 2359296 | tf_op jit(solution)/shard_map/reduce_scatter | solution.py:397
  2480.4 251.0 %reduce-scatter.18.cloned.1.call-start = ((), (), s32[]{:S(2)}) async-start(), calls=%async_computation.23 | async-start | bytes 2359296 | tf_op jit(solution)/shard_map/reduce_scatter | solution.py:394
  2490.1 369.5 %reduce-scatter.26.cloned.1.call-start = ((), (), s32[]{:S(2)}) async-start(), calls=%async_computation.27 | async-start | bytes 1081344
  2515.4 455.9 %reduce-scatter.24.cloned.1.call-start = ((), (), s32[]{:S(2)}) async-start(), calls=%async_computation.26 | async-start | bytes 3244032
  2678.9 399.1 %reduce-scatter.22.cloned.1.call-start = ((), (), s32[]{:S(2)}) async-start(), calls=%async_computation.25 | async-start | bytes 3244032
  (66 other events, 3337.4 us)
Sparse Core Ops, SparseCore 0:
  11.5 97.0 all-gather.15
  112.0 94.2 all-gather.17
  209.3 151.6 all-gather.13
  377.3 150.7 all-gather.21
  530.1 117.7 all-gather.19
  650.7 79.8 all-gather.23
  732.4 26.7 all-gather.29
  761.1 28.1 all-gather.27
  791.2 160.7 all-gather.25
  953.8 89.8 all-gather.31
  2448.7 96.4 reduce-scatter.13
  2547.4 94.2 reduce-scatter.15
  2644.9 41.6 reduce-scatter.19
  2690.1 41.2 reduce-scatter.17
  2733.5 126.0 reduce-scatter.25
  2865.8 105.5 reduce-scatter.23
  2977.5 100.4 reduce-scatter.21
where the time goes:
time: 3100 us; the launch traced here: 3090 us
  waiting for transfers between devices  1560 us (50%)
  blocking collectives  758 us (24%)
  matrix products  342 us (11%)
  local copies, waits for them, and re-layouts  274 us (9%)
  other arithmetic  99.6 us (3%)
  starting transfers between devices  41.8 us (1%)
    all_gather x1, blocking collectives, body(): lax.all_gather(router_weight, ('dp', 'expert'), axis=0, tiled=True)  389 us
    all_to_all x1, waiting for transfers between devices, body(): lax.all_to_all(slot_input_grad, 'expert', split_axis=0, concat_axis=0, ti...  296 us
    unnamed x20, waiting for transfers between devices  272 us
    all_to_all x1, waiting for transfers between devices, body(): lax.all_to_all(result, 'expert', split_axis=0, concat_axis=0, tiled=True)  227 us
    all_to_all x1, waiting for transfers between devices, body(): lax.all_to_all(outgoing_grad, 'expert', split_axis=0, concat_axis=0, tile...  221 us
    all_gather x1, blocking collectives, body(): lax.all_gather(adapter_out, ('dp', 'expert'), axis=2, tiled=True)  202 us
    all_gather x1, waiting for transfers between devices, body(): lax.all_gather(qkv_weight, ('dp', 'expert'), axis=0, tiled=True)  142 us
    reduce_scatter x1, waiting for transfers between devices, body(): lax.psum_scatter(value_terms.astype(jnp.bfloat16), 'expert', scatter_dime...  93.8 us
  transfers between devices with their start and end apart: 21, of which 15 were waited for; matrix products, arithmetic and copies ran while one was open for 19% of the time, Pallas kernels for 0%

commit v1 on v0

v1 whole, which is shorter than its diff:
```python
import functools
import jax
import jax.numpy as jnp
from jax import lax
from jax.experimental import pallas as pl
from jax.experimental.pallas import tpu as pltpu
from jax.sharding import PartitionSpec as P

D = 2048
HEAD = 128
FF = 1024
RANK = 16
ADAPTERS = 8
EXP_DEV = 4
PROMPT = 1024
EPSILON = 1e-05
MASKED = -1e30

MESH = pl.DeviceIdType.MESH
ANY = pl.BlockSpec(memory_space=pl.ANY)
VMEM = pl.BlockSpec(memory_space=pltpu.VMEM)


def greet_line(me, parts):
    barrier = pltpu.get_barrier_semaphore()

    @pl.when(me > 0)
    def _():
        pl.semaphore_signal(barrier, inc=1, device_id={"expert": me - 1}, device_id_type=MESH)

    @pl.when(me < parts - 1)
    def _():
        pl.semaphore_signal(barrier, inc=1, device_id={"expert": me + 1}, device_id_type=MESH)

    pl.semaphore_wait(barrier, jnp.where((me > 0) & (me < parts - 1), 2, 1))


def greet_all(me, parts):
    barrier = pltpu.get_barrier_semaphore()
    for k in range(1, parts):
        pl.semaphore_signal(
            barrier, inc=1, device_id={"expert": lax.rem(me + k, parts)}, device_id_type=MESH
        )
    pl.semaphore_wait(barrier, parts - 1)


def gather_kernel(parts, count, *refs):
    srcs, dsts = refs[:count], refs[count : 2 * count]
    own_sem, send_up, recv_up, send_down, recv_down = refs[2 * count :]
    me = lax.axis_index("expert")
    greet_line(me, parts)

    def block(i, origin):
        rows = srcs[i].shape[0]
        return dsts[i].at[pl.ds(pl.multiple_of(origin * rows, rows), rows)]

    def hop(i, src, origin, to, send, recv):
        return pltpu.make_async_remote_copy(
            src_ref=src,
            dst_ref=block(i, origin),
            send_sem=send,
            recv_sem=recv,
            device_id={"expert": to},
            device_id_type=MESH,
        )

    for step in range(parts - 1):
        for up in (True, False):
            origin = me - step if up else me + step
            to = me + 1 if up else me - 1
            send, recv = (send_up, recv_up) if up else (send_down, recv_down)
            has = (origin >= 0) & (origin < parts)
            for i in range(count):
                if step > 0:

                    @pl.when(has)
                    def _(i=i, origin=origin, send=send, recv=recv, step=step):
                        hop(i, block(i, origin), origin, me, send.at[i, step], recv.at[i, step - 1]).wait_recv()

                @pl.when(has & (to >= 0) & (to < parts))
                def _(i=i, origin=origin, to=to, send=send, recv=recv, step=step):
                    src = srcs[i] if step == 0 else block(i, origin)
                    hop(i, src, origin, to, send.at[i, step], recv.at[i, step]).start()

    for i in range(count):
        own = pltpu.make_async_copy(srcs[i], block(i, me), own_sem.at[i])
        own.start()
        own.wait()
    for up in (True, False):
        send, recv = (send_up, recv_up) if up else (send_down, recv_down)
        to = me + 1 if up else me - 1
        last = me - (parts - 1) if up else me + (parts - 1)
        for i in range(count):

            @pl.when((last >= 0) & (last < parts))
            def _(i=i, last=last, send=send, recv=recv):
                hop(i, block(i, last), last, me, send.at[i, 0], recv.at[i, parts - 2]).wait_recv()

            for step in range(parts - 1):
                origin = me - step if up else me + step

                @pl.when((origin >= 0) & (origin < parts) & (to >= 0) & (to < parts))
                def _(i=i, origin=origin, send=send, recv=recv, step=step):
                    hop(i, block(i, origin), origin, me, send.at[i, step], recv.at[i, step]).wait_send()


def line_gather(arrays, cid):
    parts = lax.axis_size("expert")
    n = len(arrays)
    sem = pltpu.SemaphoreType.DMA
    return pl.pallas_call(
        functools.partial(gather_kernel, parts, n),
        out_shape=[jax.ShapeDtypeStruct((parts * a.shape[0],) + a.shape[1:], a.dtype) for a in arrays],
        in_specs=[ANY] * n,
        out_specs=[ANY] * n,
        scratch_shapes=[sem((n,))] + [sem((n, parts - 1))] * 4,
        compiler_params=pltpu.CompilerParams(collective_id=cid, has_side_effects=True),
        name="line_gather_%d" % cid,
    )(*arrays)


def exchange_kernel(parts, count, stack, *refs):
    srcs, dsts = refs[:count], refs[count : 2 * count]
    own_sem, send, recv = refs[2 * count :]
    me = lax.axis_index("expert")
    greet_all(me, parts)

    def piece(i, owner):
        rows = srcs[i].shape[0] // parts
        return srcs[i].at[pl.ds(pl.multiple_of(owner * rows, rows), rows)]

    def place(i, origin):
        rows, cols = srcs[i].shape[0] // parts, srcs[i].shape[1]
        if stack:
            return dsts[i].at[pl.ds(pl.multiple_of(origin * rows, rows), rows)]
        return dsts[i].at[:, pl.ds(pl.multiple_of(origin * cols, cols), cols)]

    copies = []
    for k in list(range(parts - 1, 0, -1)):
        to = lax.rem(me + k, parts)
        for i in range(count):
            copy = pltpu.make_async_remote_copy(
                src_ref=piece(i, to),
                dst_ref=place(i, me),
                send_sem=send.at[i, k - 1],
                recv_sem=recv.at[i, k - 1],
                device_id={"expert": to},
                device_id_type=MESH,
            )
            copy.start()
            copies.append(copy)
    for i in range(count):
        own = pltpu.make_async_copy(piece(i, me), place(i, me), own_sem.at[i])
        own.start()
        own.wait()
    for copy in copies:
        copy.wait_send()
    for k in list(range(parts - 1, 0, -1)):
        origin = lax.rem(me + parts - k, parts)
        for i in range(count):
            pltpu.make_async_remote_copy(
                src_ref=piece(i, me),
                dst_ref=place(i, origin),
                send_sem=send.at[i, k - 1],
                recv_sem=recv.at[i, k - 1],
                device_id={"expert": origin},
                device_id_type=MESH,
            ).wait_recv()


def exchange(arrays, cid, stack=False):
    parts = lax.axis_size("expert")
    n = len(arrays)
    sem = pltpu.SemaphoreType.DMA
    return pl.pallas_call(
        functools.partial(exchange_kernel, parts, n, stack),
        out_shape=[
            jax.ShapeDtypeStruct(
                a.shape if stack else (a.shape[0] // parts, a.shape[1] * parts), a.dtype
            )
            for a in arrays
        ],
        in_specs=[ANY] * n,
        out_specs=[ANY] * n,
        scratch_shapes=[sem((n,)), sem((n, parts - 1)), sem((n, parts - 1))],
        compiler_params=pltpu.CompilerParams(collective_id=cid, has_side_effects=True),
        name="exchange_%d" % cid,
    )(*arrays)


def reduce_kernel(parts, src, out, slot_up, slot_down, send_up, recv_up, send_down, recv_down):
    me = lax.axis_index("expert")
    greet_line(me, parts)
    rows = out.shape[0]
    step_rows = 16

    def term(dest):
        return src.at[pl.ds(pl.multiple_of(dest * rows, rows), rows)]

    def add(into, dest):
        @pl.loop(0, rows // step_rows)
        def _(r):
            here = pl.ds(pl.multiple_of(r * step_rows, step_rows), step_rows)
            there = pl.ds(pl.multiple_of(dest * rows + r * step_rows, step_rows), step_rows)
            total = into[here, :].astype(jnp.float32) + src[there, :].astype(jnp.float32)
            into[here, :] = total.astype(jnp.bfloat16)

    def hop(ref, slot, step, to, send, recv):
        return pltpu.make_async_remote_copy(
            src_ref=ref,
            dst_ref=slot.at[step],
            send_sem=send.at[step],
            recv_sem=recv.at[step],
            device_id={"expert": to},
            device_id_type=MESH,
        )

    streams = ((True, slot_up, send_up, recv_up), (False, slot_down, send_down, recv_down))
    for step in range(parts - 1):
        for up, slot, send, recv in streams:
            line = me if up else parts - 1 - me
            dest_line = parts - 1 - step + line
            dest = dest_line if up else parts - 1 - dest_line
            to = me + 1 if up else me - 1

            @pl.when(line == 0)
            def _(dest=dest, slot=slot, step=step, to=to, send=send, recv=recv):
                hop(term(dest), slot, step, to, send, recv).start()

            if step > 0:

                @pl.when((line > 0) & (step >= line) & (line < parts - 1))
                def _(dest=dest, slot=slot, step=step, to=to, send=send, recv=recv):
                    hop(slot.at[step - 1], slot, step - 1, me, send, recv).wait_recv()
                    add(slot.at[step - 1], dest)
                    hop(slot.at[step - 1], slot, step, to, send, recv).start()

    @pl.loop(0, rows // step_rows)
    def _(r):
        here = pl.ds(pl.multiple_of(r * step_rows, step_rows), step_rows)
        there = pl.ds(pl.multiple_of(me * rows + r * step_rows, step_rows), step_rows)
        out[here, :] = src[there, :].astype(jnp.float32)

    last = parts - 2
    for up, slot, send, recv in streams:
        line = me if up else parts - 1 - me

        @pl.when(line > 0)
        def _(slot=slot, send=send, recv=recv):
            hop(slot.at[last], slot, last, me, send, recv).wait_recv()

            @pl.loop(0, rows // step_rows)
            def _(r):
                here = pl.ds(pl.multiple_of(r * step_rows, step_rows), step_rows)
                out[here, :] = out[here, :] + slot[last, here, :].astype(jnp.float32)

    for up, slot, send, recv in streams:
        line = me if up else parts - 1 - me
        for step in range(parts - 1):

            @pl.when((step >= line) & (line < parts - 1))
            def _(slot=slot, step=step, send=send, recv=recv):
                hop(slot.at[step], slot, step, me, send, recv).wait_send()


def line_reduce(terms, cid):
    parts = lax.axis_size("expert")
    rows, cols = terms.shape[0] // parts, terms.shape[1]
    sem = pltpu.SemaphoreType.DMA
    return pl.pallas_call(
        functools.partial(reduce_kernel, parts),
        out_shape=jax.ShapeDtypeStruct((rows, cols), jnp.float32),
        in_specs=[VMEM],
        out_specs=VMEM,
        scratch_shapes=[pltpu.VMEM((parts - 1, rows, cols), jnp.bfloat16)] * 2 + [sem((parts - 1,))] * 4,
        compiler_params=pltpu.CompilerParams(
            collective_id=cid, has_side_effects=True, vmem_limit_bytes=48 * 1024 * 1024
        ),
        name="line_reduce_%d" % cid,
    )(terms)


def dot_plain(left, right):
    return jnp.dot(left, right, preferred_element_type=jnp.float32)


def dot_left(left, right):
    return lax.dot_general(
        left, right, (((0,), (0,)), ((), ())), preferred_element_type=jnp.float32
    )


def dot_right(left, right):
    return lax.dot_general(
        left, right, (((1,), (1,)), ((), ())), preferred_element_type=jnp.float32
    )


def norm_inverse(values):
    return lax.rsqrt(jnp.mean(values * values, axis=-1, keepdims=True) + EPSILON)


def norm_backward(values, inverse, gain_row, upstream):
    scaled = upstream * gain_row
    return inverse * scaled - values * inverse**3 * jnp.mean(
        scaled * values, axis=-1, keepdims=True
    )


def segments_of(lengths, places):
    upto = jnp.arange(lengths.shape[0])
    limits = PROMPT + jnp.sum(
        jnp.where(upto[:, None] <= upto[None, :], lengths[:, None], 0), axis=0
    )
    passed = jnp.sum((places[:, None] >= limits[None, :]).astype(jnp.int32), axis=1)
    return jnp.where(places < PROMPT, 0, 1 + passed)


def pack_rows(arrays, lanes):
    flat = jnp.concatenate([a.reshape(-1) for a in arrays])
    rows = -(-flat.shape[0] // (16 * lanes)) * 16
    return jnp.pad(flat, (0, rows * lanes - flat.shape[0])).reshape(rows, lanes)


def body(
    tokens,
    cotangent,
    norm_gains,
    qkv_weight,
    out_weight,
    router_weight,
    adapter_down,
    adapter_qkv,
    adapter_out,
    adapter_router,
    expert_input,
    expert_output,
    expert_down,
    expert_lift,
    routes,
    adapter_ids,
    cont_lengths,
):
    low = jnp.bfloat16
    piece = tokens.shape[0]
    parts = lax.axis_size("expert")
    groups = lax.axis_size("dp")
    ways = parts * groups
    me = lax.axis_index("expert")
    total = parts * piece
    experts = EXP_DEV * parts
    width = D // parts
    heads = width // HEAD
    scale = HEAD ** (-0.5)
    share = D // ways
    first = me * piece
    adapter = adapter_ids[0]
    own_hot = (jnp.arange(ADAPTERS, dtype=jnp.int32) == adapter).astype(low)

    qkv_blocks = (
        qkv_weight.reshape(share, 3, parts, width).transpose(2, 0, 1, 3).reshape(parts * share, 3 * width)
    )
    smalls = (
        norm_gains.T,
        router_weight,
        adapter_down,
        adapter_qkv.transpose(2, 0, 1),
        adapter_out.transpose(2, 0, 1),
        adapter_router,
        own_hot,
    )
    small = pack_rows(smalls, 128)
    (qkv_line,) = exchange([qkv_blocks], 0, stack=True)
    small_line, out_line = line_gather([small, out_weight], 1)
    qkv_matrix = lax.all_gather(qkv_line, "dp", axis=0, tiled=True)
    small_all = lax.all_gather(small_line, "dp", axis=0, tiled=True).reshape(ways, -1)
    out_matrix = lax.all_gather(out_line, "dp", axis=0, tiled=True)
    down_rows = expert_down.reshape(EXP_DEV * expert_down.shape[1], ADAPTERS * RANK)
    lift_rows = expert_lift.reshape(EXP_DEV * ADAPTERS * RANK, expert_lift.shape[3])
    down_gathered = lax.all_gather(down_rows, "dp", axis=0, tiled=False)
    lift_gathered = lax.all_gather(lift_rows, "dp", axis=0, tiled=False)
    matrices = [
        (
            lax.all_gather(expert_input[j], "dp", axis=0, tiled=True),
            lax.all_gather(expert_output[j], "dp", axis=0, tiled=True),
        )
        for j in range(EXP_DEV)
    ]

    at = 0
    taken = []
    for a in smalls:
        taken.append(small_all[:, at : at + a.size])
        at += a.size
    gain_rows = taken[0].reshape(D, 2).T.astype(jnp.float32)
    router_matrix = taken[1].reshape(D, experts)
    down_pick = lax.dynamic_index_in_dim(
        taken[2].reshape(D, ADAPTERS, 3, RANK), adapter, 1, keepdims=False
    )
    lift_pick = lax.dynamic_index_in_dim(
        taken[3].reshape(3 * D, ADAPTERS, RANK), adapter, 1, keepdims=False
    )
    lift_own = (
        lax.dynamic_index_in_dim(lift_pick.reshape(3, parts, width, RANK), me, 1, keepdims=False)
        .reshape(3 * width, RANK)
    )
    lift_mix = lax.dynamic_index_in_dim(
        taken[4].reshape(D, ADAPTERS, RANK), adapter, 1, keepdims=False
    )
    lift_route = lax.dynamic_index_in_dim(
        taken[5].reshape(ADAPTERS, RANK, experts), adapter, 0, keepdims=False
    )
    group_hot = taken[6].reshape(groups, parts, ADAPTERS)[:, 0].astype(jnp.float32)
    down_query, down_mix, down_route = down_pick[:, 0], down_pick[:, 1], down_pick[:, 2]
    down_expert = (
        lax.dynamic_slice_in_dim(down_gathered, adapter * RANK, RANK, 2)
        .reshape(groups, EXP_DEV, -1, RANK)
        .transpose(1, 0, 2, 3)
        .reshape(EXP_DEV, D, RANK)
    )
    lift_expert = (
        lax.dynamic_index_in_dim(
            lift_gathered.reshape(groups, EXP_DEV, ADAPTERS, RANK, -1), adapter, 2, keepdims=False
        )
        .transpose(1, 2, 0, 3)
        .reshape(EXP_DEV, RANK, 2 * FF)
    )

    expert_ids = jnp.arange(128, dtype=jnp.int32)
    routed = jnp.any(routes[:, :, None] == expert_ids[None, None, :], axis=1).astype(low)
    tokens_all, routed_all = line_gather([tokens, routed], 2)
    inputs_all = tokens_all.astype(jnp.float32)
    normed_low = (inputs_all * norm_inverse(inputs_all) * gain_rows[0]).astype(low)
    rank_query = dot_plain(normed_low, down_query).astype(low)
    qkv_low = (dot_plain(normed_low, qkv_matrix) + dot_right(rank_query, lift_own)).astype(low)
    queries = qkv_low[:, :width].reshape(total, heads, HEAD)
    key_heads = qkv_low[:, width : 2 * width].reshape(total, heads, HEAD)
    value_heads = qkv_low[:, 2 * width :].reshape(total, heads, HEAD)
    places = jnp.arange(total, dtype=jnp.int32)
    segments = segments_of(cont_lengths[0], places)
    allowed = ((segments[None, :] == 0) & (segments[:, None] != 0)) | (
        (segments[None, :] == segments[:, None]) & (places[None, :] <= places[:, None])
    )
    scores = jnp.einsum("thd,shd->hts", queries, key_heads, preferred_element_type=jnp.float32)
    scores = jnp.where(allowed[None], scores * scale, MASKED)
    top_score = jnp.max(scores, axis=-1, keepdims=True)
    expd = jnp.exp(scores - top_score)
    total_exp = jnp.sum(expd, axis=-1, keepdims=True)
    log_total = top_score + jnp.log(total_exp)
    probs_low = (expd / total_exp).astype(low)
    mixed_heads = (
        jnp.einsum("hts,shd->thd", probs_low, value_heads, preferred_element_type=jnp.float32)
        .reshape(total, width)
        .astype(low)
    )
    (mixed_low,) = exchange([mixed_heads], 3)

    inputs = tokens.astype(jnp.float32)
    upstream = cotangent.astype(jnp.float32)
    rank_mix = dot_plain(mixed_low, down_mix).astype(low)
    middle = inputs + dot_plain(mixed_low, out_matrix) + dot_right(rank_mix, lift_mix)
    inverse_second = norm_inverse(middle)
    second_low = (middle * inverse_second * gain_rows[1]).astype(low)
    second_all, upstream_all = line_gather([second_low, cotangent], 4)

    rank_route_all = dot_plain(second_all, down_route).astype(low)
    logits = dot_plain(second_all, router_matrix) + dot_plain(rank_route_all, lift_route)
    logit_exp = jnp.exp(logits - jnp.max(logits, axis=-1, keepdims=True))
    probs_all = logit_exp / jnp.sum(logit_exp, axis=-1, keepdims=True)
    gates_all = probs_all * routed_all[:, :experts].astype(jnp.float32)
    gates_own = lax.dynamic_slice_in_dim(gates_all, me * EXP_DEV, EXP_DEV, 1)

    output_terms = 0.0
    slot_terms = 0.0
    gate_grads, lift_terms, down_terms = [], [], []
    for j in range(EXP_DEV):
        input_matrix, output_matrix = matrices[j]
        gate_column = gates_own[:, j : j + 1]
        rank_expert = dot_plain(second_all, down_expert[j]).astype(low)
        gate_up = dot_plain(second_all, input_matrix) + dot_plain(rank_expert, lift_expert[j])
        gate_part, up_part = gate_up[:, :FF], gate_up[:, FF:]
        sigma = jax.nn.sigmoid(gate_part)
        hidden = gate_part * sigma * up_part
        output_terms = output_terms + dot_plain((gate_column * hidden).astype(low), output_matrix)
        hidden_grad = dot_right(upstream_all, output_matrix)
        gate_grads.append(jnp.sum(hidden_grad * hidden, axis=1, keepdims=True))
        hidden_grad = hidden_grad * gate_column
        gate_up_grad = jnp.concatenate(
            [
                hidden_grad * up_part * sigma * (1.0 + gate_part * (1.0 - sigma)),
                hidden_grad * gate_part * sigma,
            ],
            axis=-1,
        ).astype(low)
        rank_expert_grad = dot_right(gate_up_grad, lift_expert[j]).astype(low)
        slot_terms = (
            slot_terms
            + dot_right(gate_up_grad, input_matrix)
            + dot_right(rank_expert_grad, down_expert[j])
        )
        lift_terms.append(dot_left(rank_expert, gate_up_grad))
        down_terms.append(dot_left(rank_expert_grad, second_all))

    gate_grad = jnp.concatenate(gate_grads, axis=1)
    gate_grad_wide = lax.dynamic_update_slice(
        jnp.zeros((total, 64), jnp.float32), gate_grad, (0, me * EXP_DEV)
    )
    gate_high = gate_grad_wide.astype(low)
    gate_rest = (gate_grad_wide - gate_high.astype(jnp.float32)).astype(low)
    slot_sum = line_reduce(
        jnp.concatenate([slot_terms.astype(low), gate_high, gate_rest], axis=1), 5
    )
    output_sum = lax.psum_scatter(
        output_terms.astype(low), "expert", scatter_dimension=0, tiled=True
    )
    layer_output = (middle + output_sum.astype(jnp.float32)).astype(low)

    lift_sent = jnp.stack(lift_terms).astype(low).reshape(EXP_DEV * RANK, groups, -1)
    down_sent = jnp.stack(down_terms).astype(low).reshape(EXP_DEV * RANK, groups, -1)
    expert_sent = jnp.concatenate([lift_sent, down_sent], axis=0).transpose(1, 0, 2)
    expert_got = lax.all_to_all(expert_sent, "dp", split_axis=0, concat_axis=0, tiled=True)
    by_adapter = jnp.einsum(
        "ga,gkc->akc", group_hot, expert_got.astype(jnp.float32), precision=lax.Precision.HIGHEST
    ).reshape(ADAPTERS, 2, EXP_DEV, RANK, -1)
    explift_grad = by_adapter[:, 0].transpose(1, 0, 2, 3)
    expdown_grad = by_adapter[:, 1].transpose(1, 3, 0, 2)

    expert_part = slot_sum[:, :D]
    prob_grad = slot_sum[:, D : D + experts] + slot_sum[:, D + 64 : D + 64 + experts]
    router_probs = lax.dynamic_slice_in_dim(probs_all, first, piece, 0)
    rank_route = lax.dynamic_slice_in_dim(rank_route_all, first, piece, 0)
    prob_grad = jnp.where(routed[:, :experts] > 0, prob_grad, 0.0)
    logit_grad = (
        router_probs * (prob_grad - jnp.sum(router_probs * prob_grad, axis=1, keepdims=True))
    ).astype(low)
    rank_route_grad = dot_right(logit_grad, lift_route).astype(low)
    second_grad = (
        expert_part + dot_right(logit_grad, router_matrix) + dot_right(rank_route_grad, down_route)
    )
    lift_route_grad = dot_left(rank_route, logit_grad)
    down_route_grad = dot_left(rank_route_grad, second_low)
    middle_grad = upstream + norm_backward(middle, inverse_second, gain_rows[1], second_grad)
    branch_grad = middle_grad.astype(low)
    rank_mix_grad = dot_plain(branch_grad, lift_mix).astype(low)
    mixed_grad = (dot_right(branch_grad, out_matrix) + dot_right(rank_mix_grad, down_mix)).astype(
        low
    )
    lift_mix_grad = dot_left(rank_mix, branch_grad)
    down_mix_grad = dot_left(rank_mix_grad, mixed_low)

    (mixed_back,) = exchange(
        [mixed_grad.reshape(piece, parts, width).transpose(1, 0, 2).reshape(parts * piece, width)],
        6,
        stack=True,
    )
    grad_heads = mixed_back.reshape(total, heads, HEAD)
    scores = jnp.einsum("thd,shd->hts", queries, key_heads, preferred_element_type=jnp.float32)
    probs = jnp.exp(jnp.where(allowed[None], scores * scale, MASKED) - log_total)
    prob_back = jnp.einsum(
        "thd,shd->hts", grad_heads, value_heads, preferred_element_type=jnp.float32
    )
    delta = jnp.sum(probs * prob_back, axis=-1, keepdims=True)
    score_grad = (probs * (prob_back - delta)).astype(low)
    query_grad = jnp.einsum("hts,shd->thd", score_grad, key_heads, preferred_element_type=jnp.float32)
    key_grad = jnp.einsum("hts,thd->shd", score_grad, queries, preferred_element_type=jnp.float32)
    value_grad = jnp.einsum(
        "hts,thd->shd", probs.astype(low), grad_heads, preferred_element_type=jnp.float32
    )
    qkv_back = jnp.concatenate(
        [
            (query_grad * scale).reshape(total, width),
            (key_grad * scale).reshape(total, width),
            value_grad.reshape(total, width),
        ],
        axis=1,
    ).astype(low)
    rank_query_grad = dot_plain(qkv_back, lift_own).astype(low)
    first_terms = dot_right(qkv_back, qkv_matrix) + dot_right(rank_query_grad, down_query)
    lift_query_grad = dot_left(rank_query, qkv_back)
    down_query_grad = dot_left(rank_query_grad, normed_low)

    lift_query_wide = lax.dynamic_update_slice(
        jnp.zeros((RANK, 3, parts, width), jnp.float32),
        lift_query_grad.reshape(RANK, 3, 1, width),
        (0, 0, me, 0),
    ).reshape(RANK, groups, parts, 3 * share)

    def by_owner(grad):
        return grad.reshape(grad.shape[0], groups, parts, -1)

    def flat_owner(grad):
        return grad.transpose(2, 1, 0, 3).reshape(parts, groups, -1)

    route_flat = jnp.broadcast_to(
        lift_route_grad.reshape(1, 1, RANK * experts), (parts, groups, RANK * experts)
    )
    down_owner = flat_owner(
        by_owner(jnp.concatenate([down_query_grad, down_mix_grad, down_route_grad, lift_mix_grad]))
    )
    owned = jnp.concatenate([down_owner, flat_owner(lift_query_wide), route_flat], axis=2)
    per_group = owned.shape[2]
    owned = owned.reshape(parts, groups * per_group)
    rows = -(-owned.shape[1] // (16 * D)) * 16
    owned = jnp.pad(owned, ((0, 0), (0, rows * D - owned.shape[1]))).reshape(parts, rows, D)
    terms = jnp.concatenate(
        [first_terms.astype(low).reshape(parts, piece, D), owned.astype(low)], axis=1
    ).reshape(parts * (piece + rows), D)
    first_sum = line_reduce(terms, 7)
    first_grad = first_sum[:piece]
    inverse_first = norm_inverse(inputs)
    input_grad = (
        middle_grad + norm_backward(inputs, inverse_first, gain_rows[0], first_grad)
    ).astype(low)

    sent = first_sum[piece:].reshape(-1)[: groups * per_group].reshape(groups, per_group)
    got = lax.all_to_all(sent, "dp", split_axis=0, concat_axis=0, tiled=True)
    summed = jnp.einsum("ga,gk->ak", group_hot, got, precision=lax.Precision.HIGHEST)
    n_down = 4 * RANK * share
    downs = summed[:, :n_down].reshape(ADAPTERS, 4, RANK, share)
    down_grad = downs[:, :3].transpose(3, 0, 1, 2)
    proj_grad = downs[:, 3]
    n_qkv = RANK * 3 * share
    qkv_grad = summed[:, n_down : n_down + n_qkv].reshape(ADAPTERS, RANK, 3 * share)
    router_rows = summed[:, n_down + n_qkv :].reshape(ADAPTERS * RANK, experts)
    own_rows = ADAPTERS * RANK // ways
    router_grad = lax.dynamic_slice_in_dim(
        router_rows, (lax.axis_index("dp") * parts + me) * own_rows, own_rows, 0
    )
    return (
        layer_output,
        input_grad,
        down_grad,
        qkv_grad,
        proj_grad,
        router_grad,
        expdown_grad,
        explift_grad,
    )


def solution(mesh):
    placed = (
        P(("dp", "expert"), None),
        P(("dp", "expert"), None),
        P(None, ("dp", "expert")),
        P(("dp", "expert"), None),
        P(("dp", "expert"), None),
        P(("dp", "expert"), None),
        P(("dp", "expert"), None, None, None),
        P(None, None, ("dp", "expert")),
        P(None, None, ("dp", "expert")),
        P(("dp", "expert"), None),
        P("expert", "dp", None),
        P("expert", "dp", None),
        P("expert", "dp", None, None),
        P("expert", None, None, "dp"),
        P(("dp", "expert"), None),
        P("dp"),
        P("dp", None),
    )
    return jax.shard_map(
        body,
        mesh=mesh,
        in_specs=placed,
        out_specs=(
            P(("dp", "expert"), None),
            P(("dp", "expert"), None),
            P(("dp", "expert"), None, None, None),
            P(None, None, ("dp", "expert")),
            P(None, None, ("dp", "expert")),
            P(("dp", "expert"), None),
            P("expert", "dp", None, None),
            P("expert", None, None, "dp"),
        ),
        check_vma=False,
    )
```

time: 3100 us -> 1330 us (0.43)
  waiting for transfers between devices: 1560 us -> 6.73 us
  blocking collectives: 758 us -> 0 us
  Pallas kernels: 0 us -> 602 us
  matrix products: 342 us -> 464 us
  local copies, waits for them, and re-layouts: 274 us -> 153 us
  other arithmetic: 99.6 us -> 63 us
    all_to_all x4 -> x2, waiting for transfers between devices: 744 us -> 1.56 us  [the longest x1 1.56 us: body(): got = lax.all_to_all(sent, 'dp', split_axis=0, concat_axis=0, tiled=True)]
    all_gather x4 -> x0, blocking collectives: 718 us -> none  [the longest x1 389 us: body(): lax.all_gather(router_weight, ('dp', 'expert'), axis=0, tiled=True)]
    pallas_call x0 -> x8, Pallas kernels: none -> 602 us  [the longest x3 330 us: line_gather(): pl.pallas_call(functools.partial(gather_kernel, parts, n), out_shape=[jax...]
    all_gather x10 -> x13, waiting for transfers between devices: 366 us -> 0.04 us  [the longest x1 0.02 us: body(): lift_gathered = lax.all_gather(lift_rows, 'dp', axis=0, tiled=False)]
    unnamed x20 -> x14, waiting for transfers between devices: 272 us -> 5.13 us
    dot_general x12 -> x4, matrix products: 234 us -> 28.9 us  [the longest x1 14.6 us: body(): jnp.einsum('hts,thd->shd', probs.astype(low), grad_heads, preferred_eleme...]
    reduce_scatter x4 -> x1, waiting for transfers between devices: 174 us -> 0.01 us  [body(): lax.psum_scatter(output_terms.astype(low), 'expert', scatter_dimension=0,...]
    dot_general x9 -> x25, matrix products: 27.6 us -> 194 us  [dot_right(): lax.dot_general(left, right, (((1,), (1,)), ((), ())), preferred_element_...]
  transfers between devices with their start and end apart: 21 -> 16, of which waited for: 15 -> 1; matrix products, arithmetic and copies ran while one was open for 19% -> 38% of each run, Pallas kernels for 0% -> 36%
where the time goes in v1:
time: 1330 us; the launch traced here: 1320 us
  Pallas kernels  602 us (45%)
  matrix products  464 us (35%)
  local copies, waits for them, and re-layouts  153 us (12%)
  other arithmetic  63 us (5%)
  starting transfers between devices  18.6 us (1%)
  between operations  16.4 us (1%)
    pallas_call x3, Pallas kernels, line_gather(): pl.pallas_call(functools.partial(gather_kernel, parts, n), out_shape=[jax...  330 us
    dot_general x25, matrix products, dot_right(): lax.dot_general(left, right, (((1,), (1,)), ((), ())), preferred_element_...  194 us
    pallas_call x2, Pallas kernels, line_reduce(): pl.pallas_call(functools.partial(reduce_kernel, parts), out_shape=jax.Sha...  192 us
    dot_general x25, matrix products, dot_plain(): return jnp.dot(left, right, preferred_element_type=jnp.float32)  179 us
    pallas_call x3, Pallas kernels, exchange(): pl.pallas_call(functools.partial(exchange_kernel, parts, n, stack), out_s...  81.5 us
    unnamed x231, local copies, waits for them, and re-layouts  27.2 us
  transfers between devices with their start and end apart: 16, of which 1 were waited for; matrix products, arithmetic and copies ran while one was open for 38% of the time, Pallas kernels for 36%

profile of v1, /device:TPU:9, one launch (start us, length us, event | category | flops | bytes accessed | tf_op | source)
XLA Modules:
  0.0 1324.7 jit_solution(8445862819003360366)
XLA Ops:
  19.6 32.1 %line_gather_1.1 = (bf16[1856,128]{1,0:T(8,128)(2,1)}, bf16[256,2048]{1,0:T(8,128)(2,1)}) custom-call(bf16[464,128]{1,0:T(8,128)(2,1)} %pad_bitcast_fusion.refs_0_, bf16[64,2048]{1,0:T(8,128)(2,1)} %refs_1_.2), custom_call_target="tpu_custom_call" | custom-call | tf_op jit(solution)/shard_map/line_gather_1/pallas_call | solution.py:111
  53.9 19.2 %exchange_0.1 = bf16[256,1536]{1,0:T(8,128)(2,1)} custom-call(bf16[256,1536]{1,0:T(8,128)(2,1)} %bitcast.351), custom_call_target="tpu_custom_call" | custom-call | tf_op jit(solution)/shard_map/exchange_0/pallas_call | solution.py:175
  86.5 104.2 %line_gather_2.1 = (bf16[1280,2048]{1,0:T(8,128)(2,1)}, bf16[1280,128]{1,0:T(8,128)(2,1)}) custom-call(bf16[320,2048]{1,0:T(8,128)(2,1)} %refs_0_.1, bf16[320,128]{1,0:T(8,128)(2,1)} %convert_element_type.171.refs_1_), custom_call_target="tpu_custom_call" | custom-call | tf_op jit(solution)/shard_map/line_gather_2/pallas_call | solution.py:111
  215.9 18.5 %reshape.357 = bf16[2048,8,3,16]{3,2,1,0:T(4,128)(2,1)} reshape(bf16[32,24576]{1,0:T(8,128)(2,1)S(1)} %get-tuple-element.106) | data formatting | bytes 3145728 | tf_op jit(solution)/shard_map/reshape | solution.py:398
  341.6 33.5 %exchange_3.1 = bf16[320,2048]{1,0:T(8,128)(2,1)} custom-call(bf16[1280,512]{1,0:T(8,128)(2,1)} %copy.371.refs_0_), custom_call_target="tpu_custom_call" | custom-call | tf_op jit(solution)/shard_map/exchange_3/pallas_call | solution.py:175
  386.1 193.2 %line_gather_4.1 = (bf16[1280,2048]{1,0:T(8,128)(2,1)}, bf16[1280,2048]{1,0:T(8,128)(2,1)}) custom-call(bf16[320,2048]{1,0:T(8,128)(2,1)} %multiply_convert_fusion.17.refs_0_, bf16[320,2048]{1,0:T(8,128)(2,1)} %refs_1_.3), custom_call_target="tpu_custom_call" | custom-call | tf_op jit(solution)/shard_map/line_gather_4/pallas_call | solution.py:111
  596.3 15.7 %fusion.24 = f32[1280,2048]{1,0:T(8,128)S(1)} fusion(bf16[1280,2048]{1,0:T(8,128)(2,1)} %get-tuple-element.17, bf16[1,2048,2048]{2,1,0:T(8,128)(2,1)} %all-gather.32.cloned.1.call-done), kind=kOutput, calls=%fused_computation.39 | convolution fusion | flops 10737418240 | bytes 24117248 | tf_op jit(solution)/shard_map/dot_general | solution.py:284
  634.9 15.4 %fusion.20 = f32[1280,2048]{1,0:T(8,128)S(1)} fusion(bf16[1280,2048]{1,0:T(8,128)(2,1)} %get-tuple-element.17, bf16[1,2048,2048]{2,1,0:T(8,128)(2,1)} %all-gather.36.cloned.1.call-done), kind=kOutput, calls=%fused_computation.35 | convolution fusion | flops 10737418240 | bytes 24117248 | tf_op jit(solution)/shard_map/dot_general | solution.py:284
  655.8 15.2 %fusion.12 = f32[1280,2048]{1,0:T(8,128)S(1)} fusion(bf16[1280,2048]{1,0:T(8,128)(2,1)} %get-tuple-element.17, bf16[1,2048,2048]{2,1,0:T(8,128)(2,1)} %all-gather.44.cloned.1.call-done), kind=kOutput, calls=%fused_computation.27 | convolution fusion | flops 10737418240 | bytes 24117248 | tf_op jit(solution)/shard_map/dot_general | solution.py:284
  676.7 13.9 %multiply_convert_fusion.6 = (bf16[1280,1024]{1,0:T(8,128)(2,1)S(1)}, bf16[1280,1024]{1,0:T(8,128)(2,1)S(1)}, f32[1280]{0:T(1024)}) fusion(f32[1280,2048]{1,0:T(8,128)} %convolution_add_fusion.3, f32[1280]{0:T(1024)S(1)} %get-tuple-element.82, bf16[1280,2048]{1,0:T(8,128)(2,1)} %get-tuple-element.19, bf16[1,1024,2048]{2,1,0:T(8,128)(2,1)} %all-gather.38.cloned.1.call-done), kind=kOutput, calls=%fused_computation.59 | convolution fusion | flops 5392301056 | bytes 25176064 | tf_op jit(solution)/shard_map/dot_general | solution.py:294
  693.7 14.1 %multiply_convert_fusion.2 = (bf16[1280,1024]{1,0:T(8,128)(2,1)S(1)}, bf16[1280,1024]{1,0:T(8,128)(2,1)S(1)}, f32[1280]{0:T(1024)}) fusion(f32[1280,2048]{1,0:T(8,128)} %convolution_add_fusion.1, f32[1280]{0:T(1024)S(1)} %get-tuple-element.80, bf16[1280,2048]{1,0:T(8,128)(2,1)} %get-tuple-element.19, bf16[1,1024,2048]{2,1,0:T(8,128)(2,1)} %all-gather.46.cloned.1.call-done), kind=kOutput, calls=%fused_computation.55 | convolution fusion | flops 5392301056 | bytes 25176064 | tf_op jit(solution)/shard_map/dot_general | solution.py:294
  717.8 15.3 %fusion.16 = f32[1280,2048]{1,0:T(8,128)S(1)} fusion(bf16[1280,2048]{1,0:T(8,128)(2,1)} %get-tuple-element.17, bf16[1,2048,2048]{2,1,0:T(8,128)(2,1)} %all-gather.40.cloned.1.call-done), kind=kOutput, calls=%fused_computation.31 | convolution fusion | flops 10737418240 | bytes 24117248 | tf_op jit(solution)/shard_map/dot_general | solution.py:284
  821.1 19.6 %add_convert_fusion.2 = bf16[1280,2048]{1,0:T(8,128)(2,1)} fusion(f32[1280,2048]{1,0:T(8,128)} %fusion.34, f32[1280,2048]{1,0:T(8,128)} %fusion.42, f32[1280,2048]{1,0:T(8,128)} %fusion.38, bf16[1,1024,2048]{2,1,0:T(8,128)(2,1)} %all-gather.46.cloned.1.call-done, f32[1280]{0:T(1024)S(1)} %get-tuple-element.80, f32[1280,2048]{1,0:T(8,128)} %convolution_add_fusion.1), kind=kOutput, calls=%fused_computation.19 | convolution fusion | flops 5388369920 | bytes 51385344 | tf_op jit(solution)/shard_map/dot_general | solution.py:284
  848.1 18.5 %fusion.22 = f32[1280,2048]{1,0:T(8,128)} fusion(bf16[1,2048,2048]{2,1,0:T(8,128)(2,1)} %all-gather.32.cloned.1.call-done, bf16[1280,1024]{1,0:T(8,128)(2,1)} %copy-done.76, bf16[1280,1024]{1,0:T(8,128)(2,1)} %copy-done.74), kind=kOutput, calls=%fused_computation.37 | convolution fusion | flops 10747904000 | bytes 24117248 | tf_op jit(solution)/shard_map/dot_general | solution.py:294
  866.6 16.3 %fusion.18 = f32[1280,2048]{1,0:T(8,128)} fusion(bf16[1,2048,2048]{2,1,0:T(8,128)(2,1)} %all-gather.36.cloned.1.call-done, bf16[1280,1024]{1,0:T(8,128)(2,1)S(1)} %copy-done.83, bf16[1280,1024]{1,0:T(8,128)(2,1)S(1)} %copy-done.80), kind=kOutput, calls=%fused_computation.33 | convolution fusion | flops 10747904000 | bytes 24117248 | tf_op jit(solution)/shard_map/dot_general | solution.py:294
  882.9 17.1 %fusion.14 = f32[1280,2048]{1,0:T(8,128)} fusion(bf16[1,2048,2048]{2,1,0:T(8,128)(2,1)} %all-gather.40.cloned.1.call-done, bf16[1280,1024]{1,0:T(8,128)(2,1)} %copy-done.90, bf16[1280,1024]{1,0:T(8,128)(2,1)S(1)} %copy-done.89), kind=kOutput, calls=%fused_computation.29 | convolution fusion | flops 10747904000 | bytes 24117248 | tf_op jit(solution)/shard_map/dot_general | solution.py:294
  900.0 16.2 %fusion.10 = f32[1280,2048]{1,0:T(8,128)} fusion(bf16[1,2048,2048]{2,1,0:T(8,128)(2,1)} %all-gather.44.cloned.1.call-done, bf16[1280,1024]{1,0:T(8,128)(2,1)S(1)} %copy-done.87, bf16[1280,1024]{1,0:T(8,128)(2,1)S(1)} %copy-done.85), kind=kOutput, calls=%fused_computation.25 | convolution fusion | flops 10747904000 | bytes 24117248 | tf_op jit(solution)/shard_map/dot_general | solution.py:294
  916.2 22.9 %add_convert_fusion.1 = bf16[1280,2048]{1,0:T(8,128)(2,1)} fusion(f32[1280,2048]{1,0:T(8,128)} %fusion.10, f32[1280,2048]{1,0:T(8,128)} %fusion.126, f32[1280,2048]{1,0:T(8,128)} %fusion.14, f32[1280,2048]{1,0:T(8,128)} %fusion.125, f32[1280,2048]{1,0:T(8,128)} %fusion.18, f32[1280,2048]{1,0:T(8,128)} %fusion.22, f32[1280,2048]{1,0:T(8,128)S(1)} %bitcast.335, ...), kind=kOutput, calls=%fused_computation.18 | convolution fusion | flops 104857600 | bytes 78749696 | tf_op jit(solution)/shard_map/dot_general | solution.py:294
  948.3 95.5 %line_reduce_5.1 = f32[320,2176]{1,0:T(8,128)S(1)} custom-call(bf16[1280,2176]{1,0:T(8,128)(2,1)} %concatenate.49.src), custom_call_target="tpu_custom_call" | custom-call | tf_op jit(solution)/shard_map/line_reduce_5/pallas_call | solution.py:270
  1067.1 28.8 %exchange_6.1 = bf16[1280,512]{1,0:T(8,128)(2,1)} custom-call(bf16[1280,512]{1,0:T(8,128)(2,1)} %bitcast.347), custom_call_target="tpu_custom_call" | custom-call | tf_op jit(solution)/shard_map/exchange_6/pallas_call | solution.py:175
  1097.6 17.2 %multiply_reduce_fusion = (f32[4,1280]{1,0:T(4,128)S(1)}, f32[4,1280,1280]{1,2,0:T(8,128)}) fusion(f32[4,1280,1280]{1,2,0:T(8,128)} %get-tuple-element.130, f32[4,1280]{1,0:T(4,128)S(1)} %copy-done.28, bf16[1280,4,128]{0,2,1:T(8,128)(2,1)S(1)} %bitcast.338, bf16[160,4,8,128]{3,2,1,0:T(8,128)(2,1)S(1)} %copy-done.14), kind=kOutput, calls=%fused_computation.3 | convolution fusion | flops 1697377280 | bytes 55091200 | tf_op jit(solution)/shard_map/thd,shd->hts/dot_general | solution.py:559
  1114.9 22.5 %multiply_convert_fusion = bf16[4,1280,1280]{1,2,0:T(8,128)(2,1)} fusion(f32[4,1280,1280]{1,2,0:T(8,128)} %get-tuple-element.138, f32[4,1280,1280]{1,2,0:T(8,128)} %get-tuple-element.130, f32[4,1280]{1,0:T(4,128)S(1)} %get-tuple-element.137, f32[4,1280]{1,0:T(4,128)S(1)} %copy-done.28), kind=kLoop, calls=%fused_computation.2 | loop fusion | flops 26214400 | bytes 65576960 | tf_op jit(solution)/shard_map/convert_element_type | solution.py:563
  1155.5 14.6 %fusion.45 = bf16[4,128,1280]{2,1,0:T(8,128)(2,1)} fusion(bf16[1280,4,128]{0,2,1:T(8,128)(2,1)} %bitcast.339, f32[4,1280,1280]{1,2,0:T(8,128)} %get-tuple-element.130, f32[4,1280]{1,0:T(4,128)S(1)} %copy-done.28), kind=kOutput, calls=%fused_computation.97 | convolution fusion | flops 1691484160 | bytes 28856320 | tf_op jit(solution)/shard_map/hts,thd->shd/dot_general | solution.py:566
  1203.3 96.0 %line_reduce_7.1 = f32[352,2048]{1,0:T(8,128)S(1)} custom-call(bf16[1408,2048]{1,0:T(8,128)(2,1)} %bitcast.336), custom_call_target="tpu_custom_call" | custom-call | tf_op jit(solution)/shard_map/line_reduce_7/pallas_call | solution.py:270
  (470 shorter events, 432.6 us)
Async XLA Ops:
  7.2 190.8 %all-gather.28.cloned.1.call-start = ((), (), s32[]{:S(2)}) async-start(), calls=%async_computation.6 | async-start | bytes 2359296 | tf_op jit(solution)/shard_map/all_gather | solution.py:380
  9.5 192.3 %all-gather.30.cloned.1.call-start = ((), (), s32[]{:S(2)}) async-start(), calls=%async_computation.7 | async-start | bytes 2359296 | tf_op jit(solution)/shard_map/all_gather | solution.py:381
  10.2 196.9 %all-gather.22.cloned.1.call-start = ((), (), s32[]{:S(2)}) async-start(), calls=%async_computation.3 | async-start | bytes 4276224 | tf_op jit(solution)/shard_map/all_gather | solution.py:376
  51.8 229.4 %all-gather.24.cloned.1.call-start = ((), (), s32[]{:S(2)}) async-start(), calls=%async_computation.4 | async-start | bytes 7077888 | tf_op jit(solution)/shard_map/all_gather | solution.py:375
  73.1 303.8 %all-gather.26.cloned.1.call-start = ((), (), s32[]{:S(2)}) async-start(), calls=%async_computation.5 | async-start | bytes 9437184 | tf_op jit(solution)/shard_map/all_gather | solution.py:377
  73.7 522.6 %all-gather.32.cloned.1.call-start = ((), (), s32[]{:S(2)}) async-start(), calls=%async_computation.9 | async-start | bytes 9437184 | tf_op jit(solution)/shard_map/all_gather | solution.py:384
  78.1 539.3 %all-gather.34.cloned.1.call-start = ((), (), s32[]{:S(2)}) async-start(), calls=%async_computation.10 | async-start | bytes 4718592 | tf_op jit(solution)/shard_map/all_gather | solution.py:385
  79.6 555.3 %all-gather.36.cloned.1.call-start = ((), (), s32[]{:S(2)}) async-start(), calls=%async_computation.11 | async-start | bytes 9437184 | tf_op jit(solution)/shard_map/all_gather | solution.py:384
  80.3 575.5 %all-gather.44.cloned.1.call-start = ((), (), s32[]{:S(2)}) async-start(), calls=%async_computation.15 | async-start | bytes 9437184 | tf_op jit(solution)/shard_map/all_gather | solution.py:384
  81.1 595.6 %all-gather.38.cloned.1.call-start = ((), (), s32[]{:S(2)}) async-start(), calls=%async_computation.12 | async-start | bytes 4718592 | tf_op jit(solution)/shard_map/all_gather | solution.py:385
  81.7 612.0 %all-gather.46.cloned.1.call-start = ((), (), s32[]{:S(2)}) async-start(), calls=%async_computation.16 | async-start | bytes 4718592 | tf_op jit(solution)/shard_map/all_gather | solution.py:385
  82.4 635.4 %all-gather.40.cloned.1.call-start = ((), (), s32[]{:S(2)}) async-start(), calls=%async_computation.13 | async-start | bytes 9437184 | tf_op jit(solution)/shard_map/all_gather | solution.py:384
  83.0 655.7 %all-gather.42.cloned.1.call-start = ((), (), s32[]{:S(2)}) async-start(), calls=%async_computation.14 | async-start | bytes 4718592 | tf_op jit(solution)/shard_map/all_gather | solution.py:385
  201.8 381.7 %copy-start.30 = (bf16[2,8,8,256]{3,1,2,0:T(8,128)(2,1)}, bf16[2,8,8,256]{3,1,2,0:T(8,128)(2,1)S(1)}, u32[]{:S(2)}) copy-start(bf16[2,8,8,256]{3,1,2,0:T(8,128)(2,1)S(1)} %copy.384) | copy-start | bytes 196612
  203.7 387.1 %copy-start.32 = (bf16[2,8,8,256]{3,1,2,0:T(8,128)(2,1)}, bf16[2,8,8,256]{3,1,2,0:T(8,128)(2,1)S(1)}, u32[]{:S(2)}) copy-start(bf16[2,8,8,256]{3,1,2,0:T(8,128)(2,1)S(1)} %copy.386) | copy-start | bytes 196612
  237.5 341.8 %copy-start.22 = (bf16[2048,1,3,16]{0,3,2,1:T(8,128)(2,1)}, bf16[2048,1,3,16]{0,3,2,1:T(8,128)(2,1)S(1)}, u32[]{:S(2)}) copy-start(bf16[2048,1,3,16]{0,3,2,1:T(8,128)(2,1)S(1)} %copy.315) | copy-start | bytes 589828
  239.4 144.5 %copy-start.53 = (f32[2048]{0:T(1024)}, f32[2048]{0:T(1024)S(1)}, u32[]{:S(2)}) copy-start(f32[2048]{0:T(1024)S(1)} %get-tuple-element.78) | copy-start | bytes 24580
  275.3 107.3 %copy-start.35 = (bf16[2048,1,16]{0,2,1:T(8,128)(2,1)}, bf16[2048,1,16]{0,2,1:T(8,128)(2,1)S(1)}, u32[]{:S(2)}) copy-start(bf16[2048,1,16]{0,2,1:T(8,128)(2,1)S(1)} %copy.322) | copy-start | bytes 196612
  275.8 309.2 %copy-start.16 = (bf16[2048,16]{1,0:T(8,128)(2,1)}, bf16[2048,16]{1,0:T(8,128)(2,1)S(1)}, u32[]{:S(2)}) copy-start(bf16[2048,16]{1,0:T(8,128)(2,1)S(1)} %reshape.365) | copy-start | bytes 196612
  383.9 199.6 %copy-start.58 = (f32[320]{0:T(512)}, f32[320]{0:T(512)S(1)}, u32[]{:S(2)}) copy-start(f32[320]{0:T(512)S(1)} %get-tuple-element.128) | copy-start | bytes 3844
  777.3 273.6 %all-to-all-start.1 = ((bf16[8,128,256]{2,1,0:T(8,128)(2,1)}), bf16[8,128,256]{2,1,0:T(8,128)(2,1)}, u32[]{:S(2)}, u32[]{:S(2)}) async-start(bf16[8,128,256]{2,1,0:T(8,128)(2,1)} %maximum_bitcast_fusion), calls=%async_computation.2 | async-start | bytes 1048576 | tf_op jit(solution)/shard_map/all_to_all | solution.py:521
  787.1 267.7 %reduce-scatter.2.cloned.1.call-start = ((), (), s32[]{:S(2)}) async-start(), calls=%async_computation.8 | async-start | bytes 6553600 | tf_op jit(solution)/shard_map/reduce_scatter | solution.py:513
  948.3 98.7 %copy-start.17 = (bf16[2048,16]{1,0:T(8,128)(2,1)S(1)}, bf16[2048,16]{1,0:T(8,128)(2,1)}, u32[]{:S(2)}) copy-start(bf16[2048,16]{1,0:T(8,128)(2,1)} %copy-done.16) | copy-start | bytes 196612
  1300.9 13.8 %all-to-all-start = ((f32[8,1,7424]{2,1,0:T(1,128)}), f32[8,1,7424]{2,1,0:T(1,128)S(1)}, u32[]{:S(2)}, u32[]{:S(2)}) async-start(f32[8,1,7424]{2,1,0:T(1,128)} %all_to_all.15), calls=%async_computation.1 | async-start | bytes 475136 | tf_op jit(solution)/shard_map/all_to_all | solution.py:616
  (100 other events, 1417.7 us)
Sparse Core Ops, SparseCore 0:
  10.5 29.4 all-gather.27
  41.9 27.8 all-gather.29
  71.7 35.0 all-gather.21
  108.5 45.5 all-gather.23
  155.8 54.3 all-gather.25
  212.0 54.3 all-gather.31
  268.3 36.6 all-gather.33
  306.9 54.3 all-gather.35
  363.3 54.3 all-gather.43
  420.0 36.7 all-gather.37
  459.2 36.7 all-gather.45
  497.7 54.3 all-gather.39
  554.0 36.7 all-gather.41
  840.8 94.5 reduce-scatter.1

commit v2 on v1

v2 whole, which is shorter than its diff:
```python
import functools

import jax
import jax.numpy as jnp
from jax import lax
from jax.experimental import pallas as pl
from jax.experimental.pallas import tpu as pltpu
from jax.sharding import PartitionSpec as P

D = 2048
HEAD = 128
FF = 1024
RANK = 16
ADAPTERS = 8
EXP_DEV = 4
PROMPT = 1024
EPSILON = 1e-05
MASKED = -1e30
LANES = 128
BLOCK = 256
ROWS = 1280
TILE = 512
SMALL = 1024

MESH = pl.DeviceIdType.MESH
ANY = pl.BlockSpec(memory_space=pl.ANY)
VMEM = pl.BlockSpec(memory_space=pltpu.VMEM)


def dot_plain(left, right):
    return jnp.dot(left, right, preferred_element_type=jnp.float32)


def dot_left(left, right):
    return lax.dot_general(
        left, right, (((0,), (0,)), ((), ())), preferred_element_type=jnp.float32
    )


def dot_right(left, right):
    return lax.dot_general(
        left, right, (((1,), (1,)), ((), ())), preferred_element_type=jnp.float32
    )


def transfer_cost(elements):
    return pl.CostEstimate(flops=0, bytes_accessed=140 * elements, transcendentals=0)


def greet_line(me, parts):
    barrier = pltpu.get_barrier_semaphore()

    @pl.when(me > 0)
    def _():
        pl.semaphore_signal(barrier, inc=1, device_id={"expert": me - 1}, device_id_type=MESH)

    @pl.when(me < parts - 1)
    def _():
        pl.semaphore_signal(barrier, inc=1, device_id={"expert": me + 1}, device_id_type=MESH)

    pl.semaphore_wait(barrier, jnp.where((me > 0) & (me < parts - 1), 2, 1))


def greet_all(me, parts):
    barrier = pltpu.get_barrier_semaphore()
    for k in range(1, parts):
        pl.semaphore_signal(
            barrier, inc=1, device_id={"expert": lax.rem(me + k, parts)}, device_id_type=MESH
        )
    pl.semaphore_wait(barrier, parts - 1)


def gather_kernel(parts, count, *refs):
    srcs, dsts = refs[:count], refs[count : 2 * count]
    own_sem, send_up, recv_up, send_down, recv_down = refs[2 * count :]
    me = lax.axis_index("expert")
    greet_line(me, parts)

    def block(i, origin):
        rows = srcs[i].shape[0]
        return dsts[i].at[pl.ds(pl.multiple_of(origin * rows, rows), rows)]

    def hop(i, src, origin, to, send, recv):
        return pltpu.make_async_remote_copy(
            src_ref=src,
            dst_ref=block(i, origin),
            send_sem=send,
            recv_sem=recv,
            device_id={"expert": to},
            device_id_type=MESH,
        )

    for step in range(parts - 1):
        for up in (True, False):
            origin = me - step if up else me + step
            to = me + 1 if up else me - 1
            send, recv = (send_up, recv_up) if up else (send_down, recv_down)
            has = (origin >= 0) & (origin < parts)
            for i in range(count):
                if step > 0:

                    @pl.when(has)
                    def _(i=i, origin=origin, send=send, recv=recv, step=step):
                        hop(i, block(i, origin), origin, me, send.at[i, step], recv.at[i, step - 1]).wait_recv()

                @pl.when(has & (to >= 0) & (to < parts))
                def _(i=i, origin=origin, to=to, send=send, recv=recv, step=step):
                    src = srcs[i] if step == 0 else block(i, origin)
                    hop(i, src, origin, to, send.at[i, step], recv.at[i, step]).start()

    for i in range(count):
        own = pltpu.make_async_copy(srcs[i], block(i, me), own_sem.at[i])
        own.start()
        own.wait()
    for up in (True, False):
        send, recv = (send_up, recv_up) if up else (send_down, recv_down)
        to = me + 1 if up else me - 1
        last = me - (parts - 1) if up else me + (parts - 1)
        for i in range(count):

            @pl.when((last >= 0) & (last < parts))
            def _(i=i, last=last, send=send, recv=recv):
                hop(i, block(i, last), last, me, send.at[i, 0], recv.at[i, parts - 2]).wait_recv()

            for step in range(parts - 1):
                origin = me - step if up else me + step

                @pl.when((origin >= 0) & (origin < parts) & (to >= 0) & (to < parts))
                def _(i=i, origin=origin, send=send, recv=recv, step=step):
                    hop(i, block(i, origin), origin, me, send.at[i, step], recv.at[i, step]).wait_send()


def line_gather(arrays, cid):
    parts = lax.axis_size("expert")
    n = len(arrays)
    sem = pltpu.SemaphoreType.DMA
    return pl.pallas_call(
        functools.partial(gather_kernel, parts, n),
        out_shape=[jax.ShapeDtypeStruct((parts * a.shape[0],) + a.shape[1:], a.dtype) for a in arrays],
        in_specs=[ANY] * n,
        out_specs=[ANY] * n,
        scratch_shapes=[sem((n,))] + [sem((n, parts - 1))] * 4,
        cost_estimate=transfer_cost(parts * sum(a.size for a in arrays)),
        compiler_params=pltpu.CompilerParams(collective_id=cid, has_side_effects=True),
        name="line_gather_%d" % cid,
    )(*arrays)


def exchange_kernel(parts, count, stack, *refs):
    srcs, dsts = refs[:count], refs[count : 2 * count]
    own_sem, send, recv = refs[2 * count :]
    me = lax.axis_index("expert")
    greet_all(me, parts)

    def piece(i, owner):
        rows = srcs[i].shape[0] // parts
        return srcs[i].at[pl.ds(pl.multiple_of(owner * rows, rows), rows)]

    def place(i, origin):
        rows, cols = srcs[i].shape[0] // parts, srcs[i].shape[1]
        if stack:
            return dsts[i].at[pl.ds(pl.multiple_of(origin * rows, rows), rows)]
        return dsts[i].at[:, pl.ds(pl.multiple_of(origin * cols, cols), cols)]

    copies = []
    for k in list(range(parts - 1, 0, -1)):
        to = lax.rem(me + k, parts)
        for i in range(count):
            copy = pltpu.make_async_remote_copy(
                src_ref=piece(i, to),
                dst_ref=place(i, me),
                send_sem=send.at[i, k - 1],
                recv_sem=recv.at[i, k - 1],
                device_id={"expert": to},
                device_id_type=MESH,
            )
            copy.start()
            copies.append(copy)
    for i in range(count):
        own = pltpu.make_async_copy(piece(i, me), place(i, me), own_sem.at[i])
        own.start()
        own.wait()
    for copy in copies:
        copy.wait_send()
    for k in list(range(parts - 1, 0, -1)):
        origin = lax.rem(me + parts - k, parts)
        for i in range(count):
            pltpu.make_async_remote_copy(
                src_ref=piece(i, me),
                dst_ref=place(i, origin),
                send_sem=send.at[i, k - 1],
                recv_sem=recv.at[i, k - 1],
                device_id={"expert": origin},
                device_id_type=MESH,
            ).wait_recv()


def exchange(arrays, cid, stack=False):
    parts = lax.axis_size("expert")
    n = len(arrays)
    sem = pltpu.SemaphoreType.DMA
    return pl.pallas_call(
        functools.partial(exchange_kernel, parts, n, stack),
        out_shape=[
            jax.ShapeDtypeStruct(
                a.shape if stack else (a.shape[0] // parts, a.shape[1] * parts), a.dtype
            )
            for a in arrays
        ],
        in_specs=[ANY] * n,
        out_specs=[ANY] * n,
        scratch_shapes=[sem((n,)), sem((n, parts - 1)), sem((n, parts - 1))],
        cost_estimate=transfer_cost(sum(a.size for a in arrays)),
        compiler_params=pltpu.CompilerParams(collective_id=cid, has_side_effects=True),
        name="exchange_%d" % cid,
    )(*arrays)


def reduce_kernel(parts, src, out, slot_up, slot_down, send_up, recv_up, send_down, recv_down):
    me = lax.axis_index("expert")
    greet_line(me, parts)
    rows = out.shape[0]
    step_rows = 16

    def term(dest):
        return src.at[pl.ds(pl.multiple_of(dest * rows, rows), rows)]

    def add(into, dest):
        @pl.loop(0, rows // step_rows)
        def _(r):
            here = pl.ds(pl.multiple_of(r * step_rows, step_rows), step_rows)
            there = pl.ds(pl.multiple_of(dest * rows + r * step_rows, step_rows), step_rows)
            total = into[here, :].astype(jnp.float32) + src[there, :].astype(jnp.float32)
            into[here, :] = total.astype(jnp.bfloat16)

    def hop(ref, slot, step, to, send, recv):
        return pltpu.make_async_remote_copy(
            src_ref=ref,
            dst_ref=slot.at[step],
            send_sem=send.at[step],
            recv_sem=recv.at[step],
            device_id={"expert": to},
            device_id_type=MESH,
        )

    streams = ((True, slot_up, send_up, recv_up), (False, slot_down, send_down, recv_down))
    for step in range(parts - 1):
        for up, slot, send, recv in streams:
            line = me if up else parts - 1 - me
            dest_line = parts - 1 - step + line
            dest = dest_line if up else parts - 1 - dest_line
            to = me + 1 if up else me - 1

            @pl.when(line == 0)
            def _(dest=dest, slot=slot, step=step, to=to, send=send, recv=recv):
                hop(term(dest), slot, step, to, send, recv).start()

            if step > 0:

                @pl.when((line > 0) & (step >= line) & (line < parts - 1))
                def _(dest=dest, slot=slot, step=step, to=to, send=send, recv=recv):
                    hop(slot.at[step - 1], slot, step - 1, me, send, recv).wait_recv()
                    add(slot.at[step - 1], dest)
                    hop(slot.at[step - 1], slot, step, to, send, recv).start()

    @pl.loop(0, rows // step_rows)
    def _(r):
        here = pl.ds(pl.multiple_of(r * step_rows, step_rows), step_rows)
        there = pl.ds(pl.multiple_of(me * rows + r * step_rows, step_rows), step_rows)
        out[here, :] = src[there, :].astype(jnp.float32)

    last = parts - 2
    for up, slot, send, recv in streams:
        line = me if up else parts - 1 - me

        @pl.when(line > 0)
        def _(slot=slot, send=send, recv=recv):
            hop(slot.at[last], slot, last, me, send, recv).wait_recv()

            @pl.loop(0, rows // step_rows)
            def _(r):
                here = pl.ds(pl.multiple_of(r * step_rows, step_rows), step_rows)
                out[here, :] = out[here, :] + slot[last, here, :].astype(jnp.float32)

    for up, slot, send, recv in streams:
        line = me if up else parts - 1 - me
        for step in range(parts - 1):

            @pl.when((step >= line) & (line < parts - 1))
            def _(slot=slot, step=step, send=send, recv=recv):
                hop(slot.at[step], slot, step, me, send, recv).wait_send()


def line_reduce(terms, cid):
    parts = lax.axis_size("expert")
    rows, cols = terms.shape[0] // parts, terms.shape[1]
    sem = pltpu.SemaphoreType.DMA
    return pl.pallas_call(
        functools.partial(reduce_kernel, parts),
        out_shape=jax.ShapeDtypeStruct((rows, cols), jnp.float32),
        in_specs=[VMEM],
        out_specs=VMEM,
        scratch_shapes=[pltpu.VMEM((parts - 1, rows, cols), jnp.bfloat16)] * 2 + [sem((parts - 1,))] * 4,
        cost_estimate=transfer_cost(terms.size),
        compiler_params=pltpu.CompilerParams(
            collective_id=cid, has_side_effects=True, vmem_limit_bytes=48 * 1024 * 1024
        ),
        name="line_reduce_%d" % cid,
    )(terms)


def weights_kernel(parts, blocks, out, small, dst, own_sem, send, recv, send_up, recv_up, send_down, recv_down):
    me = lax.axis_index("expert")
    share = out.shape[0]
    wide = blocks.shape[1]
    greet_all(me, parts)

    def rows(origin):
        return pl.ds(pl.multiple_of(origin * share, share), share)

    def exchanged(k, to, origin):
        return pltpu.make_async_remote_copy(
            src_ref=blocks.at[rows(to)],
            dst_ref=dst.at[rows(origin), :wide],
            send_sem=send.at[k - 1],
            recv_sem=recv.at[k - 1],
            device_id={"expert": to},
            device_id_type=MESH,
        )

    shared = ((out, wide), (small, wide + out.shape[1]))

    def place(i, origin):
        src, at = shared[i]
        return dst.at[rows(origin), at : at + src.shape[1]]

    def hop(i, src, origin, to, send_sem, recv_sem):
        return pltpu.make_async_remote_copy(
            src_ref=src,
            dst_ref=place(i, origin),
            send_sem=send_sem,
            recv_sem=recv_sem,
            device_id={"expert": to},
            device_id_type=MESH,
        )

    streams = ((1, send_up, recv_up), (-1, send_down, recv_down))
    for step in range(parts - 1):
        for way, sends, recvs in streams:
            origin, to = me - way * step, me + way
            has = (origin >= 0) & (origin < parts)
            for i in range(2):
                if step > 0:

                    @pl.when(has)
                    def _(i=i, origin=origin, sends=sends, recvs=recvs, step=step):
                        hop(i, place(i, origin), origin, me, sends.at[i, step], recvs.at[i, step - 1]).wait_recv()

                @pl.when(has & (to >= 0) & (to < parts))
                def _(i=i, origin=origin, to=to, sends=sends, recvs=recvs, step=step):
                    src = shared[i][0] if step == 0 else place(i, origin)
                    hop(i, src, origin, to, sends.at[i, step], recvs.at[i, step]).start()

        if step == 0:
            for k in range(parts - 1, 0, -1):
                to = lax.rem(me + k, parts)
                exchanged(k, to, me).start()

    for i in range(3):
        src, target = (
            (blocks.at[rows(me)], dst.at[rows(me), :wide]) if i == 2 else (shared[i][0], place(i, me))
        )
        own = pltpu.make_async_copy(src, target, own_sem.at[i])
        own.start()
        own.wait()
    for way, sends, recvs in streams:
        to, last = me + way, me - way * (parts - 1)
        for i in range(2):

            @pl.when((last >= 0) & (last < parts))
            def _(i=i, last=last, sends=sends, recvs=recvs):
                hop(i, place(i, last), last, me, sends.at[i, 0], recvs.at[i, parts - 2]).wait_recv()

            for step in range(parts - 1):
                origin = me - way * step

                @pl.when((origin >= 0) & (origin < parts) & (to >= 0) & (to < parts))
                def _(i=i, origin=origin, sends=sends, recvs=recvs, step=step):
                    hop(i, place(i, origin), origin, me, sends.at[i, step], recvs.at[i, step]).wait_send()

    for k in range(parts - 1, 0, -1):
        exchanged(k, lax.rem(me + k, parts), me).wait_send()
        exchanged(k, me, lax.rem(me + parts - k, parts)).wait_recv()


def gather_weights(blocks, out, small, cid):
    parts = lax.axis_size("expert")
    sem = pltpu.SemaphoreType.DMA
    cols = blocks.shape[1] + out.shape[1] + small.shape[1]
    return pl.pallas_call(
        functools.partial(weights_kernel, parts),
        out_shape=jax.ShapeDtypeStruct((blocks.shape[0], cols), blocks.dtype),
        in_specs=[ANY] * 3,
        out_specs=ANY,
        scratch_shapes=[sem((3,)), sem((parts - 1,)), sem((parts - 1,))] + [sem((2, parts - 1))] * 4,
        cost_estimate=transfer_cost(blocks.shape[0] * cols),
        compiler_params=pltpu.CompilerParams(collective_id=cid, has_side_effects=True),
        name="gather_weights",
    )(blocks, out, small)


def diagonal_mask(column_ref, row_ref, block):
    here = pl.ds(block * BLOCK, BLOCK)
    seg_query = column_ref[here, :]
    seg_key = row_ref[:, here]
    shape = (BLOCK, BLOCK)
    causal = lax.broadcasted_iota(jnp.int32, shape, 1) <= lax.broadcasted_iota(jnp.int32, shape, 0)
    same = (seg_query == seg_key) & causal
    return same | ((seg_key == 0) & (seg_query != 0))


def masked_scores(query, key_ref, column_ref, row_ref, block):
    scale = HEAD ** (-0.5)
    here = pl.ds(block * BLOCK, BLOCK)
    own = dot_right(query, key_ref[here, :]) * scale
    own = jnp.where(diagonal_mask(column_ref, row_ref, block), own, MASKED)
    if block == 0:
        return own
    ahead = dot_right(query, key_ref[: block * BLOCK, :]) * scale
    return jnp.concatenate([ahead, own], axis=1)


def attention_kernel(column_ref, row_ref, query_ref, key_ref, value_ref, mixed_ref, lse_ref):
    total = query_ref.shape[0]
    for block in range(total // BLOCK):
        here = pl.ds(block * BLOCK, BLOCK)
        scores = masked_scores(query_ref[here, :], key_ref, column_ref, row_ref, block)
        top = jnp.max(scores, axis=1, keepdims=True)
        expd = jnp.exp(scores - top)
        mass = jnp.sum(expd, axis=1, keepdims=True)
        probs = (expd / mass).astype(jnp.bfloat16)
        mixed = dot_plain(probs, value_ref[: (block + 1) * BLOCK, :])
        mixed_ref[here, :] = mixed.astype(jnp.bfloat16)
        lse_ref[0, here, :] = top + jnp.log(mass)


def head_specs(total, heads):
    return [
        pl.BlockSpec((total, HEAD), lambda h, part=part: (0, part * heads + h)) for part in range(3)
    ]


def run_attention(column, row, qkv):
    total, heads = qkv.shape[0], qkv.shape[1] // (3 * HEAD)
    whole = pl.BlockSpec(memory_space=pltpu.VMEM)
    return pl.pallas_call(
        attention_kernel,
        grid=(heads,),
        in_specs=[whole, whole] + head_specs(total, heads),
        out_specs=[
            pl.BlockSpec((total, HEAD), lambda h: (0, h)),
            pl.BlockSpec((1, total, 1), lambda h: (h, 0, 0)),
        ],
        out_shape=[
            jax.ShapeDtypeStruct((total, heads * HEAD), jnp.bfloat16),
            jax.ShapeDtypeStruct((heads, total, 1), jnp.float32),
        ],
        compiler_params=pltpu.CompilerParams(
            dimension_semantics=("arbitrary",), vmem_limit_bytes=48 * 1024 * 1024
        ),
        cost_estimate=pl.CostEstimate(
            flops=3 * heads * total * total * HEAD,
            bytes_accessed=8 * total * heads * HEAD,
            transcendentals=heads * total * total // 2,
        ),
        name="attention",
    )(column, row, qkv, qkv, qkv)


def attention_back_kernel(
    column_ref, row_ref, query_ref, key_ref, value_ref, grad_ref, lse_ref, back_query_ref, back_key_ref, back_value_ref, key_acc, value_acc
):
    scale = HEAD ** (-0.5)
    total = query_ref.shape[0]
    key_acc[...] = jnp.zeros_like(key_acc)
    value_acc[...] = jnp.zeros_like(value_acc)
    for block in range(total // BLOCK):
        here = pl.ds(block * BLOCK, BLOCK)
        upto = pl.ds(0, (block + 1) * BLOCK)
        query, grad = query_ref[here, :], grad_ref[here, :]
        scores = masked_scores(query, key_ref, column_ref, row_ref, block)
        probs = jnp.exp(scores - lse_ref[0, here, :])
        prob_back = dot_right(grad, value_ref[upto, :])
        delta = jnp.sum(probs * prob_back, axis=1, keepdims=True)
        score_grad = (probs * (prob_back - delta)).astype(jnp.bfloat16)
        back_query_ref[here, :] = (dot_plain(score_grad, key_ref[upto, :]) * scale).astype(jnp.bfloat16)
        key_acc[upto, :] += dot_left(score_grad, query)
        value_acc[upto, :] += dot_left(probs.astype(jnp.bfloat16), grad)
    back_key_ref[...] = (key_acc[...] * scale).astype(jnp.bfloat16)
    back_value_ref[...] = value_acc[...].astype(jnp.bfloat16)


def run_attention_back(column, row, qkv, grad, lse):
    total, heads = qkv.shape[0], qkv.shape[1] // (3 * HEAD)
    whole = pl.BlockSpec(memory_space=pltpu.VMEM)
    head = pl.BlockSpec((total, HEAD), lambda h: (0, h))
    return pl.pallas_call(
        attention_back_kernel,
        grid=(heads,),
        in_specs=[whole, whole]
        + head_specs(total, heads)
        + [head, pl.BlockSpec((1, total, 1), lambda h: (h, 0, 0))],
        out_specs=[head] * 3,
        out_shape=[jax.ShapeDtypeStruct((total, heads * HEAD), jnp.bfloat16)] * 3,
        scratch_shapes=[pltpu.VMEM((total, HEAD), jnp.float32)] * 2,
        compiler_params=pltpu.CompilerParams(
            dimension_semantics=("arbitrary",), vmem_limit_bytes=48 * 1024 * 1024
        ),
        cost_estimate=pl.CostEstimate(
            flops=8 * heads * total * total * HEAD,
            bytes_accessed=16 * total * heads * HEAD,
            transcendentals=heads * total * total // 2,
        ),
        name="attention_back",
    )(column, row, qkv, qkv, qkv, grad, lse)


def own_lift(lift_ref, j):
    row = lax.broadcasted_iota(jnp.int32, (LANES, TILE), 0)
    own = (row >= j * RANK) & (row < (j + 1) * RANK)
    return jnp.where(own, lift_ref[...].astype(jnp.float32), 0.0).astype(jnp.bfloat16)


def gate_column(gates_ref, here, j):
    shape = (ROWS, LANES)
    mine = lax.broadcasted_iota(jnp.int32, shape, 1) == lax.axis_index("expert") * EXP_DEV + j
    return mine, jnp.sum(
        jnp.where(mine, gates_ref[here, :].astype(jnp.float32), 0.0), axis=1, keepdims=True
    )


def row_chunk(b, rows=None):
    rows = rows or ROWS
    return pl.ds(pl.multiple_of(b * rows, rows), rows)


def forward_kernel(
    rows_ref,
    gates_ref,
    down_ref,
    lift_gate_ref,
    lift_up_ref,
    in_gate_ref,
    in_up_ref,
    out_ref,
    output_ref,
    ranks_ref,
    gate_ref,
    up_ref,
    output_acc,
    stage,
    sem,
):
    j, f = pl.program_id(0), pl.program_id(1)
    total = rows_ref.shape[0]

    @pl.when((j == 0) & (f == 0))
    def _():
        @pl.loop(0, total // ROWS)
        def _(b):
            here = row_chunk(b)
            ranks_ref[here, :] = dot_right(rows_ref[here, :], down_ref[...]).astype(jnp.bfloat16)
            output_acc[here, :] = jnp.zeros((ROWS, D), jnp.float32)

    lift_gate, lift_up = own_lift(lift_gate_ref, j), own_lift(lift_up_ref, j)

    @pl.loop(0, total // ROWS)
    def _(b):
        here = row_chunk(b)
        rows = rows_ref[here, :]
        _, column = gate_column(gates_ref, here, j)
        gate = dot_plain(rows, in_gate_ref[0]) + dot_plain(ranks_ref[here, :], lift_gate)
        up = dot_plain(rows, in_up_ref[0]) + dot_plain(ranks_ref[here, :], lift_up)
        gate_ref[0, here, :] = gate.astype(jnp.bfloat16)
        up_ref[0, here, :] = up.astype(jnp.bfloat16)
        hidden = (column * (gate * jax.nn.sigmoid(gate) * up)).astype(jnp.bfloat16)
        output_acc[here, :] += dot_plain(hidden, out_ref[0])

    @pl.when((j == EXP_DEV - 1) & (f == FF // TILE - 1))
    def _():
        @pl.loop(0, total // stage.shape[0])
        def _(b):
            here = row_chunk(b, stage.shape[0])
            stage[...] = output_acc[here, :].astype(jnp.bfloat16)
            copy = pltpu.make_async_copy(stage, output_ref.at[here], sem)
            copy.start()
            copy.wait()


def weight_specs():
    tiles = FF // TILE
    return [
        pl.BlockSpec((LANES, TILE), lambda j, f: (0, f)),
        pl.BlockSpec((LANES, TILE), lambda j, f: (0, f + tiles)),
        pl.BlockSpec((1, D, TILE), lambda j, f: (j, 0, f)),
        pl.BlockSpec((1, D, TILE), lambda j, f: (j, 0, f + tiles)),
        pl.BlockSpec((1, TILE, D), lambda j, f: (j, f, 0)),
    ]


EXPERT_PARAMS = pltpu.CompilerParams(
    dimension_semantics=("arbitrary", "arbitrary"), vmem_limit_bytes=60 * 1024 * 1024
)


def experts_forward(rows, gates, down, lift, matrix_in, matrix_out):
    total = rows.shape[0]
    kept = pl.BlockSpec((1, total, TILE), lambda j, f: (j, 0, f))
    return pl.pallas_call(
        forward_kernel,
        grid=(EXP_DEV, FF // TILE),
        in_specs=[VMEM] * 3 + weight_specs(),
        out_specs=[
            ANY,
            pl.BlockSpec((total, LANES), lambda j, f: (0, 0), pipeline_mode=pl.Buffered(1)),
            kept,
            kept,
        ],
        out_shape=[
            jax.ShapeDtypeStruct((total, D), jnp.bfloat16),
            jax.ShapeDtypeStruct((total, LANES), jnp.bfloat16),
            jax.ShapeDtypeStruct((EXP_DEV, total, FF), jnp.bfloat16),
            jax.ShapeDtypeStruct((EXP_DEV, total, FF), jnp.bfloat16),
        ],
        scratch_shapes=[
            pltpu.VMEM((total, D), jnp.float32),
            pltpu.VMEM((320, D), jnp.bfloat16),
            pltpu.SemaphoreType.DMA,
        ],
        compiler_params=EXPERT_PARAMS,
        cost_estimate=pl.CostEstimate(
            flops=6 * EXP_DEV * total * D * FF,
            bytes_accessed=EXP_DEV * 6 * D * FF + 8 * total * D,
            transcendentals=EXP_DEV * total * FF,
        ),
        name="experts_forward",
    )(rows, gates, down, lift, lift, matrix_in, matrix_in, matrix_out)


def backward_kernel(
    parts,
    gates_ref,
    ranks_ref,
    down_ref,
    lift_gate_ref,
    lift_up_ref,
    in_gate_ref,
    in_up_ref,
    out_ref,
    gate_ref,
    up_ref,
    *refs,
):
    blocks, refs = refs[:parts], refs[parts:]
    slot_ref, rank_ref, lift_grad_gate_ref, lift_grad_up_ref, upstream, slot_acc, rank_acc, gate_acc, lift_acc, stage, sems = refs
    j, f = pl.program_id(0), pl.program_id(1)
    total = upstream.shape[0]

    @pl.when((j == 0) & (f == 0))
    def _():
        piece = total // parts
        copies = []
        for shift in range(parts):
            owner = lax.rem(lax.axis_index("expert") + parts - shift, parts)
            there = row_chunk(owner, piece)
            copies.append(pltpu.make_async_copy(blocks[shift], upstream.at[there], sems.at[shift]))
        for copy in copies:
            copy.start()

        @pl.loop(0, total // ROWS)
        def _(b):
            here = row_chunk(b)
            slot_acc[here, :] = jnp.zeros((ROWS, D), jnp.float32)
            rank_acc[here, :] = jnp.zeros((ROWS, LANES), jnp.float32)
            gate_acc[here, :] = jnp.zeros((ROWS, LANES), jnp.float32)

        for copy in copies:
            copy.wait()

    lift_acc[...] = jnp.zeros_like(lift_acc)
    lift_gate, lift_up = own_lift(lift_gate_ref, j), own_lift(lift_up_ref, j)

    @pl.loop(0, total // ROWS)
    def _(b):
        here = row_chunk(b)
        mine, column = gate_column(gates_ref, here, j)
        raw = dot_right(upstream[here, :], out_ref[0])
        gate = gate_ref[0, here, :].astype(jnp.float32)
        up = up_ref[0, here, :].astype(jnp.float32)
        sigma = jax.nn.sigmoid(gate)
        silu = gate * sigma
        gate_grad = jnp.sum(raw * (silu * up), axis=1, keepdims=True)
        back = raw * column
        to_gate = (back * up * (sigma + silu * (1.0 - sigma))).astype(jnp.bfloat16)
        to_up = (back * silu).astype(jnp.bfloat16)
        slot_acc[here, :] += dot_right(to_gate, in_gate_ref[0]) + dot_right(to_up, in_up_ref[0])
        rank_acc[here, :] += dot_right(to_gate, lift_gate) + dot_right(to_up, lift_up)
        gate_acc[here, :] += jnp.where(mine, gate_grad, 0.0)
        lift_acc[0] += dot_left(ranks_ref[here, :], to_gate)
        lift_acc[1] += dot_left(ranks_ref[here, :], to_up)

    own = row_chunk(j, RANK)
    lift_grad_gate_ref[0] = lift_acc[0, own, :]
    lift_grad_up_ref[0] = lift_acc[1, own, :]

    @pl.when((j == EXP_DEV - 1) & (f == FF // TILE - 1))
    def _():
        @pl.loop(0, total // stage.shape[0])
        def _(b):
            here = row_chunk(b, stage.shape[0])
            rank_low = rank_acc[here, :].astype(jnp.bfloat16)
            rank_ref[here, :] = rank_low
            slot = slot_acc[here, :] + dot_plain(rank_low, down_ref[...])
            stage[:, :D] = slot.astype(jnp.bfloat16)
            wide = gate_acc[here, :]
            high = wide.astype(jnp.bfloat16).astype(jnp.float32)
            both = high + pltpu.roll(wide - high, LANES // 2, 1)
            stage[:, D:] = both.astype(jnp.bfloat16)
            copy = pltpu.make_async_copy(stage, slot_ref.at[here], sems.at[0])
            copy.start()
            copy.wait()


def experts_backward(blocks, gates, ranks, down, lift, matrix_in, matrix_out, gate, up):
    total, parts = gates.shape[0], len(blocks)
    grad = pl.BlockSpec((1, RANK, TILE), lambda j, f: (j, 0, f))
    kept = pl.BlockSpec((1, total, TILE), lambda j, f: (j, 0, f))
    return pl.pallas_call(
        functools.partial(backward_kernel, parts),
        grid=(EXP_DEV, FF // TILE),
        in_specs=[VMEM] * 3 + weight_specs() + [kept, kept] + [ANY] * parts,
        out_specs=[
            ANY,
            pl.BlockSpec((total, LANES), lambda j, f: (0, 0), pipeline_mode=pl.Buffered(1)),
            grad,
            grad,
        ],
        out_shape=[
            jax.ShapeDtypeStruct((total, D + LANES), jnp.bfloat16),
            jax.ShapeDtypeStruct((total, LANES), jnp.bfloat16),
            jax.ShapeDtypeStruct((EXP_DEV, RANK, FF), jnp.float32),
            jax.ShapeDtypeStruct((EXP_DEV, RANK, FF), jnp.float32),
        ],
        scratch_shapes=[
            pltpu.VMEM((total, D), jnp.bfloat16),
            pltpu.VMEM((total, D), jnp.float32),
            pltpu.VMEM((total, LANES), jnp.float32),
            pltpu.VMEM((total, LANES), jnp.float32),
            pltpu.VMEM((2, LANES, TILE), jnp.float32),
            pltpu.VMEM((320, D + LANES), jnp.bfloat16),
            pltpu.SemaphoreType.DMA((parts,)),
        ],
        compiler_params=EXPERT_PARAMS,
        cost_estimate=pl.CostEstimate(
            flops=8 * EXP_DEV * total * D * FF,
            bytes_accessed=EXP_DEV * 6 * D * FF + 8 * total * D,
            transcendentals=EXP_DEV * total * FF,
        ),
        name="experts_backward",
    )(gates, ranks, down, lift, lift, matrix_in, matrix_in, matrix_out, gate, up, *blocks)


def norm_inverse(values):
    return lax.rsqrt(jnp.mean(values * values, axis=-1, keepdims=True) + EPSILON)


def norm_backward(values, inverse, gain_row, upstream):
    scaled = upstream * gain_row
    return inverse * scaled - values * inverse**3 * jnp.mean(
        scaled * values, axis=-1, keepdims=True
    )


def segments_of(lengths, places):
    upto = jnp.arange(lengths.shape[0])
    limits = PROMPT + jnp.sum(
        jnp.where(upto[:, None] <= upto[None, :], lengths[:, None], 0), axis=0
    )
    passed = jnp.sum((places[:, None] >= limits[None, :]).astype(jnp.int32), axis=1)
    return jnp.where(places < PROMPT, 0, 1 + passed)


def body(
    tokens,
    cotangent,
    norm_gains,
    qkv_weight,
    out_weight,
    router_weight,
    adapter_down,
    adapter_qkv,
    adapter_out,
    adapter_router,
    expert_input,
    expert_output,
    expert_down,
    expert_lift,
    routes,
    adapter_ids,
    cont_lengths,
):
    low = jnp.bfloat16
    piece = tokens.shape[0]
    parts = lax.axis_size("expert")
    groups = lax.axis_size("dp")
    ways = parts * groups
    me = lax.axis_index("expert")
    total = parts * piece
    experts = EXP_DEV * parts
    width = D // parts
    share = D // ways
    route_rows = ADAPTERS * RANK // ways
    adapter = adapter_ids[0]

    adapter_cols = expert_lift.shape[3]
    expert_pairs = jnp.concatenate([expert_down.transpose(0, 2, 3, 1), expert_lift]).reshape(
        2 * EXP_DEV * ADAPTERS * RANK, adapter_cols
    )
    matrix_out = lax.all_gather(expert_output, "dp", axis=1, tiled=True)

    qkv_blocks = (
        qkv_weight.reshape(share, 3, parts, width).transpose(2, 0, 1, 3).reshape(parts * share, 3 * width)
    )

    def columns(array, upto):
        return jnp.pad(array, ((0, share - array.shape[0]), (0, upto - array.shape[1])))

    own_hot = (jnp.arange(ADAPTERS, dtype=jnp.int32) == adapter).astype(low)
    small = jnp.concatenate(
        [
            adapter_down.reshape(share, ADAPTERS * 3 * RANK),
            adapter_out.reshape(ADAPTERS * RANK, share).T,
            columns(router_weight, 32),
            columns(adapter_router, 32),
            columns(norm_gains.T, 8),
            columns(jnp.broadcast_to(own_hot, (share, ADAPTERS)), 56),
            adapter_qkv.reshape(ADAPTERS * RANK, 3, share).transpose(2, 1, 0).reshape(share, 3 * LANES),
        ],
        axis=1,
    )
    dense_line = gather_weights(qkv_blocks, out_weight, small, 0)
    dense_line, matrix_out = lax.optimization_barrier((dense_line, matrix_out))
    dense_all = lax.all_gather(dense_line, "dp", axis=0, tiled=True)
    (tokens_all,) = line_gather([tokens], 1)
    expert_input, expert_pairs, dense_all, tokens_all = lax.optimization_barrier(
        (expert_input, expert_pairs, dense_all, tokens_all)
    )
    pairs_all = lax.all_gather(expert_pairs, "dp", axis=0, tiled=False)
    matrix_in = lax.all_gather(expert_input, "dp", axis=1, tiled=True)
    qkv_matrix = dense_all[:, : 3 * width]
    out_matrix = dense_all[:, 3 * width : 3 * width + D]
    small_at = 3 * width + D

    row = jnp.arange(152, dtype=jnp.int32)[:, None]
    at = jnp.arange(small_at + SMALL, dtype=jnp.int32)[None, :]
    wanted = jnp.where(
        row < 48,
        adapter * 48 + row,
        jnp.where(
            row < 64,
            384 + adapter * RANK + row - 48,
            jnp.where(
                row < 112,
                640 + LANES * ((row - 64) // RANK) + adapter * RANK + (row - 64) % RANK,
                jnp.where(row < 120, 576 + row - 112, 512 + row - 120),
            ),
        ),
    )
    picked = dot_right((at == small_at + wanted).astype(low), dense_all)
    gain_rows = picked[112:114]
    picked = picked.astype(low)
    down_query, down_mix, down_route = picked[:16], picked[16:32], picked[32:48]
    lift_mix = picked[48:64]
    router_rows = picked[120 : 120 + experts]
    lift_query = (
        picked[64:112].reshape(3, RANK, ways, share).transpose(1, 2, 0, 3).reshape(RANK, 3, parts, width)
    )
    lift_query = lax.dynamic_index_in_dim(lift_query, me, 2, keepdims=False).reshape(RANK, 3 * width)
    by_owner = dense_all[:, small_at + 512 : small_at + 512 + LANES].reshape(ways, share, LANES)
    lift_route = lax.dynamic_slice_in_dim(
        by_owner[:, :route_rows, 32 : 32 + experts].reshape(ADAPTERS * RANK, experts),
        adapter * RANK,
        RANK,
        0,
    )
    group_hot = by_owner.reshape(groups, parts, share, LANES)[:, 0, 0, 72 : 72 + ADAPTERS].astype(
        jnp.float32
    )
    pairs = lax.dynamic_index_in_dim(
        pairs_all.reshape(groups, 2, EXP_DEV, ADAPTERS, RANK, adapter_cols), adapter, 3, keepdims=False
    )
    pairs = pairs.transpose(1, 2, 3, 0, 4).reshape(2, EXP_DEV * RANK, D)
    pairs = jnp.pad(pairs, ((0, 0), (0, LANES - EXP_DEV * RANK), (0, 0)))

    def shifted(array, by):
        return lax.ppermute(array, "expert", [(i, (i + by) % parts) for i in range(parts)])

    early, tokens_all = lax.optimization_barrier((cotangent, tokens_all))
    next_cotangent = shifted(early, 1)

    inputs_all = tokens_all.astype(jnp.float32)
    normed_low = (inputs_all * norm_inverse(inputs_all) * gain_rows[0:1]).astype(low)
    rank_query = dot_right(normed_low, down_query).astype(low)
    qkv_low = (dot_plain(normed_low, qkv_matrix) + dot_plain(rank_query, lift_query)).astype(low)
    segments = segments_of(cont_lengths[0], jnp.arange(total, dtype=jnp.int32))
    segment_column, segment_row = segments[:, None], segments[None, :]
    mixed_heads, log_mass = run_attention(segment_column, segment_row, qkv_low)
    (mixed_low,) = exchange([mixed_heads], 3)

    inputs = tokens.astype(jnp.float32)
    upstream = cotangent.astype(jnp.float32)
    rank_mix = dot_right(mixed_low, down_mix).astype(low)
    middle = inputs + dot_plain(mixed_low, out_matrix) + dot_plain(rank_mix, lift_mix)
    inverse_second = norm_inverse(middle)
    second_low = (middle * inverse_second * gain_rows[1:2]).astype(low)
    rank_route = dot_right(second_low, down_route).astype(low)
    logits = dot_right(second_low, router_rows) + dot_plain(rank_route, lift_route)
    logit_exp = jnp.exp(logits - jnp.max(logits, axis=-1, keepdims=True))
    router_probs = logit_exp / jnp.sum(logit_exp, axis=-1, keepdims=True)
    expert_ids = jnp.arange(experts, dtype=jnp.int32)
    routed = jnp.any(routes[:, :, None] == expert_ids[None, None, :], axis=1)
    gates = jnp.where(routed, router_probs, 0.0).astype(low)
    gates = jnp.pad(gates, ((0, 0), (0, LANES - experts)))
    second_low, next_cotangent = lax.optimization_barrier((second_low, next_cotangent))
    second_all, gates_all = line_gather([second_low, gates], 4)

    late, second_all = lax.optimization_barrier((cotangent, second_all))
    cotangents = [cotangent, next_cotangent] + [shifted(late, s) for s in range(2, parts)]
    output_terms, ranks, gate, up = experts_forward(
        second_all, gates_all, pairs[0], pairs[1], matrix_in, matrix_out
    )
    output_sum = lax.psum_scatter(output_terms, "expert", scatter_dimension=0, tiled=True)
    slot_terms, rank_expert_grad, lift_gate_grad, lift_up_grad = experts_backward(
        cotangents, gates_all, ranks, pairs[0], pairs[1], matrix_in, matrix_out, gate, up
    )
    slot_sum = line_reduce(slot_terms, 5)
    layer_output = (middle + output_sum.astype(jnp.float32)).astype(low)

    lift_sent = jnp.concatenate([lift_gate_grad, lift_up_grad], axis=2).reshape(EXP_DEV * RANK, D)
    down_sent = dot_left(rank_expert_grad[:, : EXP_DEV * RANK], second_all)
    expert_sent = (
        jnp.concatenate([lift_sent, down_sent], axis=0)
        .astype(low)
        .reshape(2 * EXP_DEV * RANK, groups, -1)
        .transpose(1, 0, 2)
    )
    expert_got = lax.all_to_all(expert_sent, "dp", split_axis=0, concat_axis=0, tiled=True)
    by_adapter = jnp.einsum(
        "ga,gkc->akc", group_hot, expert_got.astype(jnp.float32), precision=lax.Precision.HIGHEST
    ).reshape(ADAPTERS, 2, EXP_DEV, RANK, -1)
    explift_grad = by_adapter[:, 0].transpose(1, 0, 2, 3)
    expdown_grad = by_adapter[:, 1].transpose(1, 3, 0, 2)

    prob_grad = slot_sum[:, D : D + experts] + slot_sum[:, D + 64 : D + 64 + experts]
    prob_grad = jnp.where(routed, prob_grad, 0.0)
    logit_grad = (
        router_probs * (prob_grad - jnp.sum(router_probs * prob_grad, axis=1, keepdims=True))
    ).astype(low)
    rank_route_grad = dot_right(logit_grad, lift_route).astype(low)
    second_grad = (
        slot_sum[:, :D] + dot_plain(logit_grad, router_rows) + dot_plain(rank_route_grad, down_route)
    )
    middle_grad = upstream + norm_backward(middle, inverse_second, gain_rows[1:2], second_grad)
    branch_grad = middle_grad.astype(low)
    rank_mix_grad = dot_right(branch_grad, lift_mix).astype(low)
    mixed_grad = (dot_right(branch_grad, out_matrix) + dot_plain(rank_mix_grad, down_mix)).astype(low)

    (mixed_back,) = exchange(
        [mixed_grad.reshape(piece, parts, width).transpose(1, 0, 2).reshape(total, width)], 6, stack=True
    )
    back_query, back_key, back_value = run_attention_back(
        segment_column, segment_row, qkv_low, mixed_back, log_mass
    )
    qkv_back = jnp.concatenate([back_query, back_key, back_value], axis=1)
    rank_query_grad = dot_right(qkv_back, lift_query).astype(low)
    first_terms = (dot_right(qkv_back, qkv_matrix) + dot_plain(rank_query_grad, down_query)).astype(low)
    lift_query_grad = lax.dynamic_update_slice(
        jnp.zeros((RANK, 3, parts, width), jnp.float32),
        dot_left(rank_query, qkv_back).reshape(RANK, 3, 1, width),
        (0, 0, me, 0),
    )
    downs = jnp.concatenate(
        [
            dot_left(rank_query_grad, normed_low),
            dot_left(rank_mix_grad, mixed_low),
            dot_left(rank_route_grad, second_low),
            dot_left(rank_mix, branch_grad),
        ]
    )
    owned = jnp.concatenate(
        [
            downs.reshape(4 * RANK, ways, share).transpose(1, 0, 2).reshape(ways, -1),
            lift_query_grad.reshape(RANK, ways, 3 * share).transpose(1, 0, 2).reshape(ways, -1),
            jnp.broadcast_to(dot_left(rank_route, logit_grad).reshape(1, -1), (ways, RANK * experts)),
        ],
        axis=1,
    ).astype(low)
    owned, first_terms = lax.optimization_barrier((owned, first_terms))
    first_grad = line_reduce(first_terms, 7)
    got = lax.all_to_all(owned, ("dp", "expert"), split_axis=0, concat_axis=0, tiled=True)
    got, first_grad = lax.optimization_barrier((got, first_grad))
    inverse_first = norm_inverse(inputs)
    input_grad = (
        middle_grad + norm_backward(inputs, inverse_first, gain_rows[0:1], first_grad)
    ).astype(low)
    summed = jnp.einsum(
        "ga,gek->ak",
        group_hot,
        got.astype(jnp.float32).reshape(groups, parts, -1),
        precision=lax.Precision.HIGHEST,
    )
    n_down, n_qkv = 4 * RANK * share, 3 * RANK * share
    downs = summed[:, :n_down].reshape(ADAPTERS, 4, RANK, share)
    down_grad = downs[:, :3].transpose(3, 0, 1, 2)
    proj_grad = downs[:, 3]
    qkv_grad = summed[:, n_down : n_down + n_qkv].reshape(ADAPTERS, RANK, 3 * share)
    router_grad = lax.dynamic_slice_in_dim(
        summed[:, n_down + n_qkv :].reshape(ADAPTERS * RANK, experts),
        (lax.axis_index("dp") * parts + me) * route_rows,
        route_rows,
        0,
    )
    return (
        layer_output,
        input_grad,
        down_grad,
        qkv_grad,
        proj_grad,
        router_grad,
        expdown_grad,
        explift_grad,
    )


def solution(mesh):
    placed = (
        P(("dp", "expert"), None),
        P(("dp", "expert"), None),
        P(None, ("dp", "expert")),
        P(("dp", "expert"), None),
        P(("dp", "expert"), None),
        P(("dp", "expert"), None),
        P(("dp", "expert"), None, None, None),
        P(None, None, ("dp", "expert")),
        P(None, None, ("dp", "expert")),
        P(("dp", "expert"), None),
        P("expert", "dp", None),
        P("expert", "dp", None),
        P("expert", "dp", None, None),
        P("expert", None, None, "dp"),
        P(("dp", "expert"), None),
        P("dp"),
        P("dp", None),
    )
    return jax.shard_map(
        body,
        mesh=mesh,
        in_specs=placed,
        out_specs=(
            P(("dp", "expert"), None),
            P(("dp", "expert"), None),
            P(("dp", "expert"), None, None, None),
            P(None, None, ("dp", "expert")),
            P(None, None, ("dp", "expert")),
            P(("dp", "expert"), None),
            P("expert", "dp", None, None),
            P("expert", None, None, "dp"),
        ),
        check_vma=False,
    )
```

time: 1330 us -> 953 us (0.72)
  matrix products: 464 us -> 82.5 us
  Pallas kernels: 602 us -> 728 us
  local copies, waits for them, and re-layouts: 153 us -> 40.9 us
  other arithmetic: 63 us -> 24.2 us
  waiting for transfers between devices: 6.73 us -> 27.7 us
    pallas_call x0 -> x5, Pallas kernels: none -> 281 us  [the longest x1 101 us: experts_backward(): pl.pallas_call(functools.partial(backward_kernel, parts), grid=(EXP_DEV,...]
    dot_general x25 -> x10, matrix products: 194 us -> 43.2 us  [dot_right(): lax.dot_general(left, right, (((1,), (1,)), ((), ())), preferred_element_...]
    dot_general x25 -> x9, matrix products: 179 us -> 32 us  [dot_plain(): return jnp.dot(left, right, preferred_element_type=jnp.float32)]
    pallas_call x3 -> x2, Pallas kernels: 330 us -> 206 us  [line_gather(): pl.pallas_call(functools.partial(gather_kernel, parts, n), out_shape=[jax...]
    dot_general x7 -> x1, matrix products: 76.1 us -> 0.31 us  [body(): jnp.einsum('ga,gek->ak', group_hot, got.astype(jnp.float32).reshape(group...]
    reshape x25 -> x15, local copies, waits for them, and re-layouts: 54.2 us -> 7.01 us  [the longest x3 1.18 us: body(): downs.reshape(4 * RANK, ways, share).transpose(1, 0, 2).reshape(ways, -1)]
    all_gather x13 -> x4, waiting for transfers between devices: 0.04 us -> 26.5 us  [the longest x1 26.5 us: body(): matrix_out = lax.all_gather(expert_output, 'dp', axis=1, tiled=True)]
    convert_element_type x6 -> x2, other arithmetic: 24.6 us -> 0.44 us  [the longest x1 0.29 us: body(): second_low = (middle * inverse_second * gain_rows[1:2]).astype(low)]
  transfers between devices with their start and end apart: 16 -> 10, of which waited for: 1 -> 1; matrix products, arithmetic and copies ran while one was open for 38% -> 13% of each run, Pallas kernels for 36% -> 77%
where the time goes in v2:
time: 953 us; the launch traced here: 940 us
  Pallas kernels  728 us (76%)
  matrix products  82.5 us (9%)
  local copies, waits for them, and re-layouts  40.9 us (4%)
  waiting for transfers between devices  27.7 us (3%)
  other arithmetic  24.2 us (3%)
  starting transfers between devices  20.4 us (2%)
  between operations  16 us (2%)
    pallas_call x2, Pallas kernels, line_gather(): pl.pallas_call(functools.partial(gather_kernel, parts, n), out_shape=[jax...  206 us
    pallas_call x2, Pallas kernels, line_reduce(): pl.pallas_call(functools.partial(reduce_kernel, parts), out_shape=jax.Sha...  182 us
    pallas_call x1, Pallas kernels, experts_backward(): pl.pallas_call(functools.partial(backward_kernel, parts), grid=(EXP_DEV,...  101 us
    pallas_call x1, Pallas kernels, experts_forward(): pl.pallas_call(forward_kernel, grid=(EXP_DEV, FF // TILE), in_specs=[VMEM...  88.5 us
    pallas_call x2, Pallas kernels, exchange(): pl.pallas_call(functools.partial(exchange_kernel, parts, n, stack), out_s...  59.5 us
    pallas_call x1, Pallas kernels, gather_weights(): pl.pallas_call(functools.partial(weights_kernel, parts), out_shape=jax.Sh...  58.3 us
    dot_general x10, matrix products, dot_right(): lax.dot_general(left, right, (((1,), (1,)), ((), ())), preferred_element_...  43.2 us
    dot_general x9, matrix products, dot_plain(): return jnp.dot(left, right, preferred_element_type=jnp.float32)  32 us
  transfers between devices with their start and end apart: 10, of which 1 were waited for; matrix products, arithmetic and copies ran while one was open for 13% of the time, Pallas kernels for 77%

profile of v2, /device:TPU:9, one launch (start us, length us, event | category | flops | bytes accessed | tf_op | source)
XLA Modules:
  0.0 939.7 jit_solution(3155396665350603246)
XLA Ops:
  16.7 58.3 %gather_weights.1 = bf16[256,4608]{1,0:T(8,128)(2,1)} custom-call(bf16[256,1536]{1,0:T(8,128)(2,1)} %bitcast.129, bf16[64,2048]{1,0:T(8,128)(2,1)} %out.1, bf16[64,1024]{1,0:T(8,128)(2,1)} %concatenate.31.small), custom_call_target="tpu_custom_call" | custom-call | bytes 165150720 | tf_op jit(solution)/shard_map/gather_weights/pallas_call | solution.py:400
  74.9 26.5 %all-gather.6.cloned.1.call-done.out_ref = bf16[4,1024,2048]{2,1,0:T(8,128)(2,1)} async-done(((bf16[4,128,2048]{2,1,0:T(8,128)(2,1)}), bf16[4,1024,2048]{2,1,0:T(8,128)(2,1)}) %all-gather.6.cloned.1.call-update) | async-done | bytes 16777232 | tf_op jit(solution)/shard_map/all_gather | solution.py:829
  101.5 101.0 %line_gather_1.1 = bf16[1280,2048]{1,0:T(8,128)(2,1)} custom-call(bf16[320,2048]{1,0:T(8,128)(2,1)} %refs_0_.2), custom_call_target="tpu_custom_call" | custom-call | bytes 367001600 | tf_op jit(solution)/shard_map/line_gather_1/pallas_call | solution.py:137
  204.9 13.9 %fusion.64 = (bf16[152,2048]{1,0:T(8,128)(2,1)S(1)}, f32[152,2048]{1,0:T(8,128)}) fusion(bf16[2048,4608]{1,0:T(8,128)(2,1)} %all-gather.8.cloned.1.call-done, s32[152]{0:T(256)S(1)} %fusion.51), kind=kOutput, calls=%fused_computation.146 | convolution fusion | flops 2869915648 | bytes 20742752 | tf_op jit(solution)/shard_map/dot_general | solution.py:41
  220.3 3.7 fusion
  225.0 4.8 convolution_convert_fusion.6
  229.9 11.1 %fusion.10 = f32[1280,1536]{1,0:T(8,128)S(1)} fusion(bf16[2048,4608]{1,0:T(8,128)(2,1)} %all-gather.8.cloned.1.call-done, bf16[1280,2048]{1,0:T(8,128)(2,1)S(1)} %bitcast.123, f32[2048]{0:T(1024)S(1)} %bitcast.153, f32[1280]{0:T(1024)S(1)} %add_rsqrt_fusion), kind=kOutput, calls=%fused_computation.14 | convolution fusion | flops 8063549440 | bytes 19411968 | tf_op jit(solution)/shard_map/dot_general | solution.py:31
  244.1 14.1 %attention.1 = (bf16[1280,512]{1,0:T(8,128)(2,1)S(1)}, f32[4,1280,1]{2,1,0:T(8,128)S(1)}) custom-call(s32[1280,1]{1,0:T(8,128)S(1)} %reshape_select_fusion.column_ref, s32[1,1280]{1,0:T(1,128)S(1)} %compare_select_fusion.row_ref, bf16[1280,1536]{1,0:T(8,128)(2,1)} %fusion.3.query_ref.key_ref.value_ref, bf16[1280,1536]{1,0:T(8,128)(2,1)} %fusion.3.query_ref.key_ref.value_ref, ...), custom_call_target="tpu_custom_call" | custom-call | flops 2516582400 | bytes 5242880 | tf_op jit(solution)/shard_map/attention/pallas_call | solution.py:456
  260.8 30.8 %exchange_3.1 = bf16[320,2048]{1,0:T(8,128)(2,1)} custom-call(bf16[1280,512]{1,0:T(8,128)(2,1)} %copy-done.3), custom_call_target="tpu_custom_call" | custom-call | bytes 91750400 | tf_op jit(solution)/shard_map/exchange_3/pallas_call | solution.py:202
  293.4 5.7 convert_add_fusion
  305.3 104.5 %line_gather_4.1 = (bf16[1280,2048]{1,0:T(8,128)(2,1)}, bf16[1280,128]{1,0:T(8,128)(2,1)}) custom-call(bf16[320,2048]{1,0:T(8,128)(2,1)} %copy-done.10, bf16[320,128]{1,0:T(8,128)(2,1)} %pad.34.refs_1_), custom_call_target="tpu_custom_call" | custom-call | bytes 389939200 | tf_op jit(solution)/shard_map/line_gather_4/pallas_call | solution.py:137
  416.9 88.5 %experts_forward.1 = (bf16[1280,2048]{1,0:T(8,128)(2,1)}, bf16[1280,128]{1,0:T(8,128)(2,1)}, bf16[4,1280,1024]{2,1,0:T(8,128)(2,1)}, bf16[4,1280,1024]{2,1,0:T(8,128)(2,1)}) custom-call(bf16[1280,2048]{1,0:T(8,128)(2,1)} %get-tuple-element.47.rows_ref, bf16[1280,128]{1,0:T(8,128)(2,1)} %get-tuple-element.48.gates_ref, ...), custom_call_target="tpu_custom_call" | custom-call | flops 64424509440 | bytes 71303168 | tf_op jit(solution)/shard_map/experts_forward/pallas_call | solution.py:619
  506.5 101.0 %experts_backward.1 = (bf16[1280,2176]{1,0:T(8,128)(2,1)}, bf16[1280,128]{1,0:T(8,128)(2,1)}, f32[4,16,1024]{2,1,0:T(8,128)}, f32[4,16,1024]{2,1,0:T(8,128)}) custom-call(bf16[1280,128]{1,0:T(8,128)(2,1)} %get-tuple-element.48.gates_ref, bf16[1280,128]{1,0:T(8,128)(2,1)} %get-tuple-element.53.ranks_ref, bf16[128,2048]{1,0:T(8,128)(2,1)} %get-tuple-element.119.down_ref, ...), custom_call_target="tpu_custom_call" | custom-call | flops 85899345920 | bytes 71303168 | tf_op jit(solution)/shard_map/experts_backward/pallas_call | solution.py:738
  611.9 91.4 %line_reduce_5.1 = f32[320,2176]{1,0:T(8,128)S(1)} custom-call(bf16[1280,2176]{1,0:T(8,128)(2,1)} %get-tuple-element.58.src), custom_call_target="tpu_custom_call" | custom-call | bytes 389939200 | tf_op jit(solution)/shard_map/line_reduce_5/pallas_call | solution.py:298
  708.0 8.9 all-to-all-start.1
  721.5 5.1 subtract_add_fusion
  728.0 5.4 fusion.4
  735.5 28.7 %exchange_6.1.grad_ref = bf16[1280,512]{1,0:T(8,128)(2,1)} custom-call(bf16[1280,512]{1,0:T(8,128)(2,1)} %bitcast.127), custom_call_target="tpu_custom_call" | custom-call | bytes 91750400 | tf_op jit(solution)/shard_map/exchange_6/pallas_call | solution.py:202
  765.5 19.1 %attention_back.1 = (bf16[1280,512]{1,0:T(8,128)(2,1)S(1)}, bf16[1280,512]{1,0:T(8,128)(2,1)S(1)}, bf16[1280,512]{1,0:T(8,128)(2,1)S(1)}) custom-call(s32[1280,1]{1,0:T(8,128)S(1)} %copy-done.1, s32[1,1280]{1,0:T(1,128)S(1)} %copy-done.5, bf16[1280,1536]{1,0:T(8,128)(2,1)} %fusion.3.query_ref.key_ref.value_ref, ...), custom_call_target="tpu_custom_call" | custom-call | flops 6710886400 | bytes 10485760 | tf_op jit(solution)/shard_map/attention_back/pallas_call | solution.py:507
  784.9 13.7 %fusion.8 = f32[1280,2048]{1,0:T(8,128)} fusion(bf16[1280,1536]{1,0:T(8,128)(2,1)S(1)} %constant_dynamic-update-slice_fusion, bf16[2048,4608]{1,0:T(8,128)(2,1)} %all-gather.8.cloned.1.call-done), kind=kOutput, calls=%fused_computation.12 | convolution fusion | flops 8053063680 | bytes 20709376 | tf_op jit(solution)/shard_map/dot_general | solution.py:41
  805.6 7.8 add_convert_fusion.src
  815.7 6.7 all-to-all-start
  826.9 90.6 %line_reduce_7.1 = f32[320,2048]{1,0:T(8,128)S(1)} custom-call(bf16[1280,2048]{1,0:T(8,128)(2,1)} %add_convert_fusion.src), custom_call_target="tpu_custom_call" | custom-call | bytes 367001600 | tf_op jit(solution)/shard_map/line_reduce_7/pallas_call | solution.py:298
  928.8 3.9 fusion.20
  (247 shorter events, 78.5 us)
Async XLA Ops:
  7.2 94.2 %all-gather.6.cloned.1.call-start = ((), (), s32[]{:S(2)}) async-start(), calls=%async_computation.3 | async-start | bytes 18874368 | tf_op jit(solution)/shard_map/all_gather | solution.py:829
  7.9 195.5 %all-gather.8.cloned.1.call-start = ((), (), s32[]{:S(2)}) async-start(), calls=%async_computation.4 | async-start | bytes 21233664 | tf_op jit(solution)/shard_map/all_gather | solution.py:853
  101.4 101.1 %copy-start.24 = (bf16[4,8,16,256]{3,2,1,0:T(8,128)(2,1)S(1)}, bf16[4,8,16,256]{3,2,1,0:T(8,128)(2,1)}, u32[]{:S(2)}) copy-start(bf16[4,8,16,256]{3,2,1,0:T(8,128)(2,1)} %param.30) | copy-start | bytes 786436
  101.4 101.1 %copy-start.25 = (bf16[4,256,8,16]{1,3,2,0:T(8,128)(2,1)S(1)}, bf16[4,256,8,16]{1,3,2,0:T(8,128)(2,1)}, u32[]{:S(2)}) copy-start(bf16[4,256,8,16]{1,3,2,0:T(8,128)(2,1)} %param.29) | copy-start | bytes 786436
  101.4 312.7 %all-gather.12.cloned.1.call-start = ((), (), s32[]{:S(2)}) async-start(), calls=%async_computation.7 | async-start | bytes 4718592 | tf_op jit(solution)/shard_map/all_gather | solution.py:858
  203.4 213.5 %all-gather.10.cloned.1.call-start = ((), (), s32[]{:S(2)}) async-start(), calls=%async_computation.5 | async-start | bytes 37748736 | tf_op jit(solution)/shard_map/all_gather | solution.py:859
  204.0 517.5 %reduce-scatter.2.cloned.1.call-start = ((), (), s32[]{:S(2)}) async-start(), calls=%async_computation.6 | async-start | bytes 6553600 | tf_op jit(solution)/shard_map/reduce_scatter | solution.py:942
  204.2 99.9 %copy-start.19 = (pred[320,16]{1,0:T(8,128)(4,1)}, pred[320,16]{1,0:T(8,128)(4,1)S(1)}, u32[]{:S(2)}) copy-start(pred[320,16]{1,0:T(8,128)(4,1)S(1)} %copy.122) | copy-start | bytes 15364
  204.5 39.6 %copy-start.4 = (s32[1,1280]{1,0:T(1,128)}, s32[1,1280]{1,0:T(1,128)S(1)}, u32[]{:S(2)}) copy-start(s32[1,1280]{1,0:T(1,128)S(1)} %compare_select_fusion.row_ref) | copy-start | bytes 15364
  204.6 100.7 %collective-permute-start = (bf16[320,2048]{1,0:T(8,128)(2,1)}, bf16[320,2048]{1,0:T(8,128)(2,1)}, u32[]{:S(2)}, u32[]{:S(2)}) collective-permute-start(bf16[320,2048]{1,0:T(8,128)(2,1)} %refs_0_.3), channel_id=1, source_target_pairs={{0,1},{1,2},{2,3},{3,0},{4,5},{5,6},{6,7},{7,4},{8,9},{9,10},{10,1... | collective-permute-start | bytes 3932168 | tf_op jit(solution)/shard_map/ppermute | solution.py:906
  218.8 84.4 %copy-start.16 = (bf16[152,2048]{1,0:T(8,128)(2,1)}, bf16[152,2048]{1,0:T(8,128)(2,1)S(1)}, u32[]{:S(2)}) copy-start(bf16[152,2048]{1,0:T(8,128)(2,1)S(1)} %get-tuple-element.124) | copy-start | bytes 1867780
  225.0 75.4 %copy-start.34 = (f32[1,2048]{1,0:T(1,128)}, f32[1,2048]{1,0:T(1,128)S(1)}, u32[]{:S(2)}) copy-start(f32[1,2048]{1,0:T(1,128)S(1)} %get-tuple-element.114) | copy-start | bytes 24580
  302.8 112.8 %copy-start.28 = (bf16[320,16]{0,1:T(8,128)(2,1)}, bf16[320,16]{0,1:T(8,128)(2,1)S(1)}, u32[]{:S(2)}) copy-start(bf16[320,16]{0,1:T(8,128)(2,1)S(1)} %convolution_convert_fusion.8) | copy-start | bytes 30724
  303.9 113.0 %copy-start.36 = (f32[320]{0:T(512)}, f32[320]{0:T(512)S(1)}, u32[]{:S(2)}) copy-start(f32[320]{0:T(512)S(1)} %get-tuple-element.128) | copy-start | bytes 3844
  304.5 112.4 %copy-start.39 = (f32[320]{0:T(512)}, f32[320]{0:T(512)S(1)}, u32[]{:S(2)}) copy-start(f32[320]{0:T(512)S(1)} %fusion.28) | copy-start | bytes 3844
  409.9 95.6 %collective-permute-start.2 = (bf16[320,2048]{1,0:T(8,128)(2,1)}, bf16[320,2048]{1,0:T(8,128)(2,1)S(1)}, u32[]{:S(2)}, u32[]{:S(2)}) collective-permute-start(bf16[320,2048]{1,0:T(8,128)(2,1)} %refs_0_.3), channel_id=1, source_target_pairs={{0,3},{1,0},{2,1},{3,2},{4,7},{5,4},{6,5},{7,6},{8,11},{9,8},{10,9... | collective-permute-start | bytes 3932168 | tf_op jit(solution)/shard_map/ppermute | solution.py:906
  413.4 92.0 %collective-permute-start.1 = (bf16[320,2048]{1,0:T(8,128)(2,1)}, bf16[320,2048]{1,0:T(8,128)(2,1)}, u32[]{:S(2)}, u32[]{:S(2)}) collective-permute-start(bf16[320,2048]{1,0:T(8,128)(2,1)} %refs_0_.3), channel_id=1, source_target_pairs={{0,2},{1,3},{2,0},{3,1},{4,6},{5,7},{6,4},{7,5},{8,10},{9,11},{10,... | collective-permute-start | bytes 3932168 | tf_op jit(solution)/shard_map/ppermute | solution.py:906
  611.9 91.4 %copy-start.15 = (f32[320,16]{1,0:T(8,128)S(1)}, f32[320,16]{1,0:T(8,128)}, u32[]{:S(2)}) copy-start(f32[320,16]{1,0:T(8,128)} %copy-done.14) | copy-start | bytes 61444
  611.9 91.4 %copy-start.20 = (pred[320,16]{1,0:T(8,128)(4,1)S(1)}, pred[320,16]{1,0:T(8,128)(4,1)}, u32[]{:S(2)}) copy-start(pred[320,16]{1,0:T(8,128)(4,1)} %copy-done.19) | copy-start | bytes 15364
  611.9 91.4 %copy-start.37 = (f32[320]{0:T(512)S(1)}, f32[320]{0:T(512)}, u32[]{:S(2)}) copy-start(f32[320]{0:T(512)} %copy-done.36) | copy-start | bytes 3844
  611.9 91.4 %copy-start.40 = (f32[320]{0:T(512)S(1)}, f32[320]{0:T(512)}, u32[]{:S(2)}) copy-start(f32[320]{0:T(512)} %copy-done.39) | copy-start | bytes 3844
  611.9 92.0 %copy-start.29 = (bf16[320,16]{0,1:T(8,128)(2,1)S(1)}, bf16[320,16]{0,1:T(8,128)(2,1)}, u32[]{:S(2)}) copy-start(bf16[320,16]{0,1:T(8,128)(2,1)} %copy-done.28) | copy-start | bytes 30724
  708.0 107.7 %all-to-all-start.1 = ((bf16[8,128,256]{2,1,0:T(8,128)(2,1)}), bf16[8,128,256]{2,1,0:T(8,128)(2,1)}, u32[]{:S(2)}, u32[]{:S(2)}) async-start(bf16[8,128,256]{2,1,0:T(8,128)(2,1)} %maximum_bitcast_fusion), calls=%async_computation.2 | async-start | bytes 1048576 | tf_op jit(solution)/shard_map/all_to_all | solution.py:957
  815.7 101.8 %all-to-all-start = ((bf16[32,2,3712]{2,1,0:T(2,128)(2,1)}), bf16[32,2,3712]{2,1,0:T(2,128)(2,1)S(1)}, u32[]{:S(2)}, u32[]{:S(2)}) async-start(bf16[32,2,3712]{2,1,0:T(2,128)(2,1)} %reshape.346), calls=%async_computation.1 | async-start | bytes 950272 | tf_op jit(solution)/shard_map/all_to_all | solution.py:1010
  (39 other events, 311.2 us)
Sparse Core Ops, SparseCore 0:
  9.9 91.4 all-gather.5
  103.3 98.7 all-gather.7
  204.5 36.7 all-gather.11
  243.0 160.7 all-gather.9
  505.6 96.9 reduce-scatter.1

commit v3 on v2

--- a/solution.py
+++ b/solution.py
@@ -70,76 +70,86 @@
     pl.semaphore_wait(barrier, parts - 1)
 
 
-def gather_kernel(parts, count, *refs):
+def gather_kernel(parts, pieces, count, *refs):
     srcs, dsts = refs[:count], refs[count : 2 * count]
     own_sem, send_up, recv_up, send_down, recv_down = refs[2 * count :]
     me = lax.axis_index("expert")
     greet_line(me, parts)
 
-    def block(i, origin):
-        rows = srcs[i].shape[0]
-        return dsts[i].at[pl.ds(pl.multiple_of(origin * rows, rows), rows)]
-
-    def hop(i, src, origin, to, send, recv):
+    def block(i, origin, piece):
+        rows = srcs[i].shape[0] // pieces
+        at = origin * srcs[i].shape[0] + piece * rows
+        return dsts[i].at[pl.ds(pl.multiple_of(at, rows), rows)]
+
+    def hop(i, src, origin, piece, to, send, recv, step, got):
+        n = i * pieces + piece
         return pltpu.make_async_remote_copy(
             src_ref=src,
-            dst_ref=block(i, origin),
-            send_sem=send,
-            recv_sem=recv,
+            dst_ref=block(i, origin, piece),
+            send_sem=send.at[n, step],
+            recv_sem=recv.at[n, got],
             device_id={"expert": to},
             device_id_type=MESH,
         )
 
+    streams = ((1, send_up, recv_up), (-1, send_down, recv_down))
     for step in range(parts - 1):
-        for up in (True, False):
-            origin = me - step if up else me + step
-            to = me + 1 if up else me - 1
-            send, recv = (send_up, recv_up) if up else (send_down, recv_down)
-            has = (origin >= 0) & (origin < parts)
+        for piece in range(pieces):
             for i in range(count):
-                if step > 0:
-
-                    @pl.when(has)
-                    def _(i=i, origin=origin, send=send, recv=recv, step=step):
-                        hop(i, block(i, origin), origin, me, send.at[i, step], recv.at[i, step - 1]).wait_recv()
-
-                @pl.when(has & (to >= 0) & (to < parts))
-                def _(i=i, origin=origin, to=to, send=send, recv=recv, step=step):
-                    src = srcs[i] if step == 0 else block(i, origin)
-                    hop(i, src, origin, to, send.at[i, step], recv.at[i, step]).start()
-
+                for way, send, recv in streams:
+                    origin, to = me - way * step, me + way
+                    has = (origin >= 0) & (origin < parts)
+                    if step > 0:
+
+                        @pl.when(has)
+                        def _(i=i, origin=origin, piece=piece, send=send, recv=recv, step=step):
+                            here = block(i, origin, piece)
+                            hop(i, here, origin, piece, me, send, recv, step, step - 1).wait_recv()
+
+                    @pl.when(has & (to >= 0) & (to < parts))
+                    def _(i=i, origin=origin, piece=piece, to=to, send=send, recv=recv, step=step):
+                        rows = srcs[i].shape[0] // pieces
+                        src = srcs[i].at[piece * rows : (piece + 1) * rows] if step == 0 else block(i, origin, piece)
+                        hop(i, src, origin, piece, to, send, recv, step, step).start()
+
+        if step == 0:
+            for i in range(count):
+                rows = srcs[i].shape[0]
+                there = dsts[i].at[pl.ds(pl.multiple_of(me * rows, rows), rows)]
+                pltpu.make_async_copy(srcs[i], there, own_sem.at[i]).start()
     for i in range(count):
-        own = pltpu.make_async_copy(srcs[i], block(i, me), own_sem.at[i])
-        own.start()
-        own.wait()
-    for up in (True, False):
-        send, recv = (send_up, recv_up) if up else (send_down, recv_down)
-        to = me + 1 if up else me - 1
-        last = me - (parts - 1) if up else me + (parts - 1)
+        rows = srcs[i].shape[0]
+        there = dsts[i].at[pl.ds(pl.multiple_of(me * rows, rows), rows)]
+        pltpu.make_async_copy(srcs[i], there, own_sem.at[i]).wait()
+    for way, send, recv in streams:
+        to, last = me + way, me - way * (parts - 1)
         for i in range(count):
-
-            @pl.when((last >= 0) & (last < parts))
-            def _(i=i, last=last, send=send, recv=recv):
-                hop(i, block(i, last), last, me, send.at[i, 0], recv.at[i, parts - 2]).wait_recv()
-
-            for step in range(parts - 1):
-                origin = me - step if up else me + step
-
-                @pl.when((origin >= 0) & (origin < parts) & (to >= 0) & (to < parts))
-                def _(i=i, origin=origin, send=send, recv=recv, step=step):
-                    hop(i, block(i, origin), origin, me, send.at[i, step], recv.at[i, step]).wait_send()
-
-
-def line_gather(arrays, cid):
+            for piece in range(pieces):
+
+                @pl.when((last >= 0) & (last < parts))
+                def _(i=i, piece=piece, last=last, send=send, recv=recv):
+                    here = block(i, last, piece)
+                    hop(i, here, last, piece, me, send, recv, 0, parts - 2).wait_recv()
+
+                for step in range(parts - 1):
+                    origin = me - way * step
+
+                    @pl.when((origin >= 0) & (origin < parts) & (to >= 0) & (to < parts))
+                    def _(i=i, piece=piece, origin=origin, send=send, recv=recv, step=step):
+                        here = block(i, origin, piece)
+                        hop(i, here, origin, piece, me, send, recv, step, step).wait_send()
+
+
+def line_gather(arrays, cid, pieces=1):
     parts = lax.axis_size("expert")
     n = len(arrays)
     sem = pltpu.SemaphoreType.DMA
     return pl.pallas_call(
-        functools.partial(gather_kernel, parts, n),
+        functools.partial(gather_kernel, parts, pieces, n),
         out_shape=[jax.ShapeDtypeStruct((parts * a.shape[0],) + a.shape[1:], a.dtype) for a in arrays],
         in_specs=[ANY] * n,
         out_specs=[ANY] * n,
-        scratch_shapes=[sem((n,))] + [sem((n, parts - 1))] * 4,
+        scratch_shapes=[sem((n,))] + [sem((n * pieces, parts - 1))] * 4,
         cost_estimate=transfer_cost(parts * sum(a.size for a in arrays)),
         compiler_params=pltpu.CompilerParams(collective_id=cid, has_side_effects=True),
         name="line_gather_%d" % cid,
@@ -216,52 +226,56 @@
     )(*arrays)
 
 
-def reduce_kernel(parts, src, out, slot_up, slot_down, send_up, recv_up, send_down, recv_down):
+def reduce_kernel(parts, pieces, src, out, slot_up, slot_down, send_up, recv_up, send_down, recv_down):
     me = lax.axis_index("expert")
     greet_line(me, parts)
     rows = out.shape[0]
+    part = rows // pieces
     step_rows = 16
 
-    def term(dest):
-        return src.at[pl.ds(pl.multiple_of(dest * rows, rows), rows)]
-
-    def add(into, dest):
-        @pl.loop(0, rows // step_rows)
-        def _(r):
-            here = pl.ds(pl.multiple_of(r * step_rows, step_rows), step_rows)
-            there = pl.ds(pl.multiple_of(dest * rows + r * step_rows, step_rows), step_rows)
-            total = into[here, :].astype(jnp.float32) + src[there, :].astype(jnp.float32)
-            into[here, :] = total.astype(jnp.bfloat16)
-
-    def hop(ref, slot, step, to, send, recv):
+    def hop(ref, slot, step, piece, to, send, recv):
         return pltpu.make_async_remote_copy(
             src_ref=ref,
-            dst_ref=slot.at[step],
-            send_sem=send.at[step],
-            recv_sem=recv.at[step],
+            dst_ref=slot.at[step, piece * part : (piece + 1) * part],
+            send_sem=send.at[step, piece],
+            recv_sem=recv.at[step, piece],
             device_id={"expert": to},
             device_id_type=MESH,
         )
 
+    def landed(slot, step, piece, send, recv):
+        return hop(slot.at[step, piece * part : (piece + 1) * part], slot, step, piece, me, send, recv)
+
     streams = ((True, slot_up, send_up, recv_up), (False, slot_down, send_down, recv_down))
     for step in range(parts - 1):
-        for up, slot, send, recv in streams:
-            line = me if up else parts - 1 - me
-            dest_line = parts - 1 - step + line
-            dest = dest_line if up else parts - 1 - dest_line
-            to = me + 1 if up else me - 1
-
-            @pl.when(line == 0)
-            def _(dest=dest, slot=slot, step=step, to=to, send=send, recv=recv):
-                hop(term(dest), slot, step, to, send, recv).start()
-
-            if step > 0:
-
-                @pl.when((line > 0) & (step >= line) & (line < parts - 1))
-                def _(dest=dest, slot=slot, step=step, to=to, send=send, recv=recv):
-                    hop(slot.at[step - 1], slot, step - 1, me, send, recv).wait_recv()
-                    add(slot.at[step - 1], dest)
-                    hop(slot.at[step - 1], slot, step, to, send, recv).start()
+        for piece in range(pieces):
+            for up, slot, send, recv in streams:
+                line = me if up else parts - 1 - me
+                dest_line = parts - 1 - step + line
+                dest = dest_line if up else parts - 1 - dest_line
+                to = me + 1 if up else me - 1
+
+                @pl.when(line == 0)
+                def _(dest=dest, slot=slot, step=step, piece=piece, to=to, send=send, recv=recv):
+                    there = pl.ds(pl.multiple_of(dest * rows + piece * part, part), part)
+                    hop(src.at[there], slot, step, piece, to, send, recv).start()
+
+                if step > 0:
+
+                    @pl.when((line > 0) & (step >= line) & (line < parts - 1))
+                    def _(dest=dest, slot=slot, step=step, piece=piece, to=to, send=send, recv=recv):
+                        landed(slot, step - 1, piece, send, recv).wait_recv()
+
+                        @pl.loop(0, part // step_rows)
+                        def _(r):
+                            at = piece * part + r * step_rows
+                            here = pl.ds(pl.multiple_of(at, step_rows), step_rows)
+                            there = pl.ds(pl.multiple_of(dest * rows + at, step_rows), step_rows)
+                            both = slot[step - 1, here, :].astype(jnp.float32) + src[there, :].astype(jnp.float32)
+                            slot[step - 1, here, :] = both.astype(jnp.bfloat16)
+
+                        sent = slot.at[step - 1, piece * part : (piece + 1) * part]
+                        hop(sent, slot, step, piece, to, send, recv).start()
 
     @pl.loop(0, rows // step_rows)
     def _(r):
@@ -270,37 +284,40 @@
         out[here, :] = src[there, :].astype(jnp.float32)
 
     last = parts - 2
-    for up, slot, send, recv in streams:
-        line = me if up else parts - 1 - me
-
-        @pl.when(line > 0)
-        def _(slot=slot, send=send, recv=recv):
-            hop(slot.at[last], slot, last, me, send, recv).wait_recv()
-
-            @pl.loop(0, rows // step_rows)
-            def _(r):
-                here = pl.ds(pl.multiple_of(r * step_rows, step_rows), step_rows)
-                out[here, :] = out[here, :] + slot[last, here, :].astype(jnp.float32)
+    for piece in range(pieces):
+        for up, slot, send, recv in streams:
+            line = me if up else parts - 1 - me
+
+            @pl.when(line > 0)
+            def _(slot=slot, piece=piece, send=send, recv=recv):
+                landed(slot, last, piece, send, recv).wait_recv()
+
+                @pl.loop(0, part // step_rows)
+                def _(r):
+                    here = pl.ds(pl.multiple_of(piece * part + r * step_rows, step_rows), step_rows)
+                    out[here, :] = out[here, :] + slot[last, here, :].astype(jnp.float32)
 
     for up, slot, send, recv in streams:
         line = me if up else parts - 1 - me
         for step in range(parts - 1):
-
-            @pl.when((step >= line) & (line < parts - 1))
-            def _(slot=slot, step=step, send=send, recv=recv):
-                hop(slot.at[step], slot, step, me, send, recv).wait_send()
-
-
-def line_reduce(terms, cid):
+            for piece in range(pieces):
+
+                @pl.when((step >= line) & (line < parts - 1))
+                def _(slot=slot, step=step, piece=piece, send=send, recv=recv):
+                    landed(slot, step, piece, send, recv).wait_send()
+
+
+def line_reduce(terms, cid, pieces=1):
     parts = lax.axis_size("expert")
     rows, cols = terms.shape[0] // parts, terms.shape[1]
     sem = pltpu.SemaphoreType.DMA
     return pl.pallas_call(
-        functools.partial(reduce_kernel, parts),
+        functools.partial(reduce_kernel, parts, pieces),
         out_shape=jax.ShapeDtypeStruct((rows, cols), jnp.float32),
         in_specs=[VMEM],
         out_specs=VMEM,
-        scratch_shapes=[pltpu.VMEM((parts - 1, rows, cols), jnp.bfloat16)] * 2 + [sem((parts - 1,))] * 4,
+        scratch_shapes=[pltpu.VMEM((parts - 1, rows, cols), jnp.bfloat16)] * 2
+        + [sem((parts - 1, pieces))] * 4,
         cost_estimate=transfer_cost(terms.size),
         compiler_params=pltpu.CompilerParams(
             collective_id=cid, has_side_effects=True, vmem_limit_bytes=48 * 1024 * 1024
@@ -309,7 +326,7 @@
     )(terms)
 
 
-def weights_kernel(parts, blocks, out, small, dst, own_sem, send, recv, send_up, recv_up, send_down, recv_down):
+def weights_kernel(parts, blocks, out, small, dst, dst_out, own_sem, send, recv, send_up, recv_up, send_down, recv_down):
     me = lax.axis_index("expert")
     share = out.shape[0]
     wide = blocks.shape[1]
@@ -328,11 +345,11 @@
             device_id_type=MESH,
         )
 
-    shared = ((out, wide), (small, wide + out.shape[1]))
+    shared = ((out, dst_out, 0), (small, dst, wide))
 
     def place(i, origin):
-        src, at = shared[i]
-        return dst.at[rows(origin), at : at + src.shape[1]]
+        src, into, at = shared[i]
+        return into.at[rows(origin), at : at + src.shape[1]]
 
     def hop(i, src, origin, to, send_sem, recv_sem):
         return pltpu.make_async_remote_copy(
@@ -365,14 +382,21 @@
             for k in range(parts - 1, 0, -1):
                 to = lax.rem(me + k, parts)
                 exchanged(k, to, me).start()
-
-    for i in range(3):
-        src, target = (
-            (blocks.at[rows(me)], dst.at[rows(me), :wide]) if i == 2 else (shared[i][0], place(i, me))
-        )
-        own = pltpu.make_async_copy(src, target, own_sem.at[i])
-        own.start()
-        own.wait()
+            owns = [
+                pltpu.make_async_copy(src, target, own_sem.at[i])
+                for i, (src, target) in enumerate(
+                    (
+                        (blocks.at[rows(me)], dst.at[rows(me), :wide]),
+                        (out, place(0, me)),
+                        (small, place(1, me)),
+                    )
+                )
+            ]
+            for copy in owns:
+                copy.start()
+
+    for copy in owns:
+        copy.wait()
     for way, sends, recvs in streams:
         to, last = me + way, me - way * (parts - 1)
         for i in range(2):
@@ -396,14 +420,17 @@
 def gather_weights(blocks, out, small, cid):
     parts = lax.axis_size("expert")
     sem = pltpu.SemaphoreType.DMA
-    cols = blocks.shape[1] + out.shape[1] + small.shape[1]
+    rows, cols = blocks.shape[0], blocks.shape[1] + small.shape[1]
     return pl.pallas_call(
         functools.partial(weights_kernel, parts),
-        out_shape=jax.ShapeDtypeStruct((blocks.shape[0], cols), blocks.dtype),
+        out_shape=[
+            jax.ShapeDtypeStruct((rows, cols), blocks.dtype),
+            jax.ShapeDtypeStruct((rows, out.shape[1]), blocks.dtype),
+        ],
         in_specs=[ANY] * 3,
-        out_specs=ANY,
+        out_specs=[ANY] * 2,
         scratch_shapes=[sem((3,)), sem((parts - 1,)), sem((parts - 1,))] + [sem((2, parts - 1))] * 4,
-        cost_estimate=transfer_cost(blocks.shape[0] * cols),
+        cost_estimate=transfer_cost(rows * (cols + out.shape[1])),
         compiler_params=pltpu.CompilerParams(collective_id=cid, has_side_effects=True),
         name="gather_weights",
     )(blocks, out, small)
@@ -553,14 +580,9 @@
     in_gate_ref,
     in_up_ref,
     out_ref,
-    output_ref,
-    ranks_ref,
-    gate_ref,
-    up_ref,
-    output_acc,
-    stage,
-    sem,
+    *refs,
 ):
+    output_ref, ranks_ref, gate_ref, up_ref, output_acc, stage, sems = refs
     j, f = pl.program_id(0), pl.program_id(1)
     total = rows_ref.shape[0]
 
@@ -579,8 +601,8 @@
         here = row_chunk(b)
         rows = rows_ref[here, :]
         _, column = gate_column(gates_ref, here, j)
-        gate = dot_plain(rows, in_gate_ref[0]) + dot_plain(ranks_ref[here, :], lift_gate)
-        up = dot_plain(rows, in_up_ref[0]) + dot_plain(ranks_ref[here, :], lift_up)
+        gate = dot_plain(rows, in_gate_ref[0].reshape(D, TILE)) + dot_plain(ranks_ref[here, :], lift_gate)
+        up = dot_plain(rows, in_up_ref[0].reshape(D, TILE)) + dot_plain(ranks_ref[here, :], lift_up)
         gate_ref[0, here, :] = gate.astype(jnp.bfloat16)
         up_ref[0, here, :] = up.astype(jnp.bfloat16)
         hidden = (column * (gate * jax.nn.sigmoid(gate) * up)).astype(jnp.bfloat16)
@@ -588,22 +610,34 @@
 
     @pl.when((j == EXP_DEV - 1) & (f == FF // TILE - 1))
     def _():
-        @pl.loop(0, total // stage.shape[0])
+        def copy(b):
+            slot = lax.rem(b, 2)
+            here = row_chunk(b, stage.shape[1])
+            return pltpu.make_async_copy(stage.at[slot], output_ref.at[here], sems.at[slot])
+
+        steps = total // stage.shape[1]
+
+        @pl.loop(0, steps)
         def _(b):
-            here = row_chunk(b, stage.shape[0])
-            stage[...] = output_acc[here, :].astype(jnp.bfloat16)
-            copy = pltpu.make_async_copy(stage, output_ref.at[here], sem)
-            copy.start()
-            copy.wait()
-
-
-def weight_specs():
+            @pl.when(b >= 2)
+            def _():
+                copy(b - 2).wait()
+
+            here = row_chunk(b, stage.shape[1])
+            stage[lax.rem(b, 2)] = output_acc[here, :].astype(jnp.bfloat16)
+            copy(b).start()
+
+        for b in range(steps - 2, steps):
+            copy(b).wait()
+
+
+def weight_specs(ring, share):
     tiles = FF // TILE
     return [
         pl.BlockSpec((LANES, TILE), lambda j, f: (0, f)),
         pl.BlockSpec((LANES, TILE), lambda j, f: (0, f + tiles)),
-        pl.BlockSpec((1, D, TILE), lambda j, f: (j, 0, f)),
-        pl.BlockSpec((1, D, TILE), lambda j, f: (j, 0, f + tiles)),
+        pl.BlockSpec((1, ring, share, TILE), lambda j, f: (j, 0, 0, f)),
+        pl.BlockSpec((1, ring, share, TILE), lambda j, f: (j, 0, 0, f + tiles)),
         pl.BlockSpec((1, TILE, D), lambda j, f: (j, f, 0)),
     ]
 
@@ -619,7 +653,7 @@
     return pl.pallas_call(
         forward_kernel,
         grid=(EXP_DEV, FF // TILE),
-        in_specs=[VMEM] * 3 + weight_specs(),
+        in_specs=[VMEM] * 3 + weight_specs(*matrix_in.shape[1:2], D // matrix_in.shape[1]),
         out_specs=[
             ANY,
             pl.BlockSpec((total, LANES), lambda j, f: (0, 0), pipeline_mode=pl.Buffered(1)),
@@ -634,8 +668,8 @@
         ],
         scratch_shapes=[
             pltpu.VMEM((total, D), jnp.float32),
-            pltpu.VMEM((320, D), jnp.bfloat16),
-            pltpu.SemaphoreType.DMA,
+            pltpu.VMEM((2, 160, D), jnp.bfloat16),
+            pltpu.SemaphoreType.DMA((2,)),
         ],
         compiler_params=EXPERT_PARAMS,
         cost_estimate=pl.CostEstimate(
@@ -703,7 +737,9 @@
         back = raw * column
         to_gate = (back * up * (sigma + silu * (1.0 - sigma))).astype(jnp.bfloat16)
         to_up = (back * silu).astype(jnp.bfloat16)
-        slot_acc[here, :] += dot_right(to_gate, in_gate_ref[0]) + dot_right(to_up, in_up_ref[0])
+        slot_acc[here, :] += dot_right(to_gate, in_gate_ref[0].reshape(D, TILE)) + dot_right(
+            to_up, in_up_ref[0].reshape(D, TILE)
+        )
         rank_acc[here, :] += dot_right(to_gate, lift_gate) + dot_right(to_up, lift_up)
         gate_acc[here, :] += jnp.where(mine, gate_grad, 0.0)
         lift_acc[0] += dot_left(ranks_ref[here, :], to_gate)
@@ -715,20 +751,32 @@
 
     @pl.when((j == EXP_DEV - 1) & (f == FF // TILE - 1))
     def _():
-        @pl.loop(0, total // stage.shape[0])
+        def copy(b):
+            slot = lax.rem(b, 2)
+            here = row_chunk(b, stage.shape[1])
+            return pltpu.make_async_copy(stage.at[slot], slot_ref.at[here], sems.at[slot])
+
+        steps = total // stage.shape[1]
+
+        @pl.loop(0, steps)
         def _(b):
-            here = row_chunk(b, stage.shape[0])
+            @pl.when(b >= 2)
+            def _():
+                copy(b - 2).wait()
+
+            here = row_chunk(b, stage.shape[1])
             rank_low = rank_acc[here, :].astype(jnp.bfloat16)
             rank_ref[here, :] = rank_low
             slot = slot_acc[here, :] + dot_plain(rank_low, down_ref[...])
-            stage[:, :D] = slot.astype(jnp.bfloat16)
             wide = gate_acc[here, :]
             high = wide.astype(jnp.bfloat16).astype(jnp.float32)
             both = high + pltpu.roll(wide - high, LANES // 2, 1)
-            stage[:, D:] = both.astype(jnp.bfloat16)
-            copy = pltpu.make_async_copy(stage, slot_ref.at[here], sems.at[0])
-            copy.start()
-            copy.wait()
+            stage[lax.rem(b, 2), :, :D] = slot.astype(jnp.bfloat16)
+            stage[lax.rem(b, 2), :, D:] = both.astype(jnp.bfloat16)
+            copy(b).start()
+
+        for b in range(steps - 2, steps):
+            copy(b).wait()
 
 
 def experts_backward(blocks, gates, ranks, down, lift, matrix_in, matrix_out, gate, up):
@@ -738,7 +786,7 @@
     return pl.pallas_call(
         functools.partial(backward_kernel, parts),
         grid=(EXP_DEV, FF // TILE),
-        in_specs=[VMEM] * 3 + weight_specs() + [kept, kept] + [ANY] * parts,
+        in_specs=[VMEM] * 3 + weight_specs(*matrix_in.shape[1:2], D // matrix_in.shape[1]) + [kept, kept] + [ANY] * parts,
         out_specs=[
             ANY,
             pl.BlockSpec((total, LANES), lambda j, f: (0, 0), pipeline_mode=pl.Buffered(1)),
@@ -757,7 +805,7 @@
             pltpu.VMEM((total, LANES), jnp.float32),
             pltpu.VMEM((total, LANES), jnp.float32),
             pltpu.VMEM((2, LANES, TILE), jnp.float32),
-            pltpu.VMEM((320, D + LANES), jnp.bfloat16),
+            pltpu.VMEM((2, 160, D + LANES), jnp.bfloat16),
             pltpu.SemaphoreType.DMA((parts,)),
         ],
         compiler_params=EXPERT_PARAMS,
@@ -768,6 +816,57 @@
         ),
         name="experts_backward",
     )(gates, ranks, down, lift, lift, matrix_in, matrix_in, matrix_out, gate, up, *blocks)
+
+
+def pick_kernel(sel_ref, rows_ref, out_ref):
+    @pl.when(pl.program_id(0) == 0)
+    def _():
+        out_ref[...] = jnp.zeros_like(out_ref)
+
+    out_ref[...] += dot_right(sel_ref[...], rows_ref[...])
+
+
+def pick_rows(chosen, dense, at):
+    rows, cols = chosen.shape
+    wide = 2 * LANES
+    return pl.pallas_call(
+        pick_kernel,
+        grid=(cols // wide,),
+        in_specs=[
+            pl.BlockSpec((rows, wide), lambda i: (0, i)),
+            pl.BlockSpec((dense.shape[0], wide), lambda i: (0, at // wide + i)),
+        ],
+        out_specs=pl.BlockSpec((rows, dense.shape[0]), lambda i: (0, 0)),
+        out_shape=jax.ShapeDtypeStruct((rows, dense.shape[0]), jnp.float32),
+        name="pick_rows",
+    )(chosen, dense)
+
+
+def first_kernel(query_ref, key_ref, value_ref, rank_ref, down_ref, *refs):
+    weights, out_ref = refs[:3], refs[3]
+    total = dot_right(query_ref[...], weights[0][...]) + dot_right(key_ref[...], weights[1][...])
+    total = total + dot_right(value_ref[...], weights[2][...]) + dot_plain(rank_ref[...], down_ref[...])
+    out_ref[...] = total.astype(jnp.bfloat16)
+
+
+def first_products(backs, ranks, down, dense):
+    total, width = backs[0].shape
+    tile = 512
+    weights = [
+        pl.BlockSpec((tile, width), lambda i, part=part: (i, part)) for part in range(3)
+    ]
+    return pl.pallas_call(
+        first_kernel,
+        grid=(D // tile,),
+        in_specs=[VMEM] * 4 + [pl.BlockSpec((RANK, tile), lambda i: (0, i))] + weights,
+        out_specs=pl.BlockSpec((total, tile), lambda i: (0, i)),
+        out_shape=jax.ShapeDtypeStruct((total, D), jnp.bfloat16),
+        compiler_params=pltpu.CompilerParams(vmem_limit_bytes=48 * 1024 * 1024),
+        cost_estimate=pl.CostEstimate(
+            flops=6 * total * width * D, bytes_accessed=6 * width * D + 2 * total * D, transcendentals=0
+        ),
+        name="first_products",
+    )(*backs, ranks, down, dense, dense, dense)
 
 
 def norm_inverse(values):
@@ -823,9 +922,15 @@
     adapter = adapter_ids[0]
 
     adapter_cols = expert_lift.shape[3]
-    expert_pairs = jnp.concatenate([expert_down.transpose(0, 2, 3, 1), expert_lift]).reshape(
-        2 * EXP_DEV * ADAPTERS * RANK, adapter_cols
-    )
+    pairs_own = jnp.stack([expert_down.transpose(0, 2, 3, 1), expert_lift], axis=1)
+    abreast = D // (ADAPTERS * adapter_cols)
+    pair_rows = 2 * RANK // abreast
+    pairs_own = (
+        pairs_own.reshape(EXP_DEV, 2 // abreast, abreast, ADAPTERS, RANK, adapter_cols)
+        .transpose(0, 1, 4, 2, 3, 5)
+        .reshape(EXP_DEV, pair_rows, D)
+    )
+    expert_rows = jnp.concatenate([expert_input, pairs_own], axis=1)
     matrix_out = lax.all_gather(expert_output, "dp", axis=1, tiled=True)
 
     qkv_blocks = (
@@ -848,21 +953,19 @@
         ],
         axis=1,
     )
-    dense_line = gather_weights(qkv_blocks, out_weight, small, 0)
-    dense_line, matrix_out = lax.optimization_barrier((dense_line, matrix_out))
+    dense_line, out_line = gather_weights(qkv_blocks, out_weight, small, 0)
+    dense_line, out_line, expert_rows, matrix_out = lax.optimization_barrier(
+        (dense_line, out_line, expert_rows, matrix_out)
+    )
     dense_all = lax.all_gather(dense_line, "dp", axis=0, tiled=True)
-    (tokens_all,) = line_gather([tokens], 1)
-    expert_input, expert_pairs, dense_all, tokens_all = lax.optimization_barrier(
-        (expert_input, expert_pairs, dense_all, tokens_all)
-    )
-    pairs_all = lax.all_gather(expert_pairs, "dp", axis=0, tiled=False)
-    matrix_in = lax.all_gather(expert_input, "dp", axis=1, tiled=True)
+    (tokens_all,) = line_gather([tokens], 1, 2)
+    out_matrix = lax.all_gather(out_line, "dp", axis=0, tiled=True)
+    matrix_in = lax.all_gather(expert_rows, "dp", axis=1, tiled=True).reshape(EXP_DEV, groups, -1, D)
     qkv_matrix = dense_all[:, : 3 * width]
-    out_matrix = dense_all[:, 3 * width : 3 * width + D]
-    small_at = 3 * width + D
-
-    row = jnp.arange(152, dtype=jnp.int32)[:, None]
-    at = jnp.arange(small_at + SMALL, dtype=jnp.int32)[None, :]
+    small_at = 3 * width
+
+    row = jnp.arange(160, dtype=jnp.int32)[:, None]
+    at = jnp.arange(SMALL, dtype=jnp.int32)[None, :]
     wanted = jnp.where(
         row < 48,
         adapter * 48 + row,
@@ -876,7 +979,7 @@
             ),
         ),
     )
-    picked = dot_right((at == small_at + wanted).astype(low), dense_all)
+    picked = pick_rows((at == wanted).astype(low), dense_all, small_at)
     gain_rows = picked[112:114]
     picked = picked.astype(low)
     down_query, down_mix, down_route = picked[:16], picked[16:32], picked[32:48]
@@ -896,17 +999,12 @@
     group_hot = by_owner.reshape(groups, parts, share, LANES)[:, 0, 0, 72 : 72 + ADAPTERS].astype(
         jnp.float32
     )
-    pairs = lax.dynamic_index_in_dim(
-        pairs_all.reshape(groups, 2, EXP_DEV, ADAPTERS, RANK, adapter_cols), adapter, 3, keepdims=False
-    )
-    pairs = pairs.transpose(1, 2, 3, 0, 4).reshape(2, EXP_DEV * RANK, D)
-    pairs = jnp.pad(pairs, ((0, 0), (0, LANES - EXP_DEV * RANK), (0, 0)))
-
     def shifted(array, by):
         return lax.ppermute(array, "expert", [(i, (i + by) % parts) for i in range(parts)])
 
     early, tokens_all = lax.optimization_barrier((cotangent, tokens_all))
-    next_cotangent = shifted(early, 1)
+    early_shifts, late_shifts = [1], list(range(2, parts))
+    moved = {s: shifted(early, s) for s in early_shifts}
 
     inputs_all = tokens_all.astype(jnp.float32)
     normed_low = (inputs_all * norm_inverse(inputs_all) * gain_rows[0:1]).astype(low)
@@ -931,11 +1029,29 @@
     routed = jnp.any(routes[:, :, None] == expert_ids[None, None, :], axis=1)
     gates = jnp.where(routed, router_probs, 0.0).astype(low)
     gates = jnp.pad(gates, ((0, 0), (0, LANES - experts)))
-    second_low, next_cotangent = lax.optimization_barrier((second_low, next_cotangent))
-    second_all, gates_all = line_gather([second_low, gates], 4)
+    held = lax.optimization_barrier([second_low] + [moved[s] for s in early_shifts])
+    second_low = held[0]
+    moved.update(zip(early_shifts, held[1:]))
+    second_all, gates_all = line_gather([second_low, gates], 4, 2)
 
     late, second_all = lax.optimization_barrier((cotangent, second_all))
-    cotangents = [cotangent, next_cotangent] + [shifted(late, s) for s in range(2, parts)]
+    moved.update({s: shifted(late, s) for s in late_shifts})
+    cotangents = [cotangent] + [moved[s] for s in range(1, parts)]
+    pairs = jnp.stack(
+        [
+            lax.dynamic_slice_in_dim(
+                matrix_in[:, :, matrix_in.shape[2] - pair_rows :],
+                (beside * ADAPTERS + adapter) * adapter_cols,
+                adapter_cols,
+                3,
+            ).reshape(EXP_DEV, groups, 2 // abreast, RANK, adapter_cols)
+            for beside in range(abreast)
+        ],
+        axis=3,
+    )
+    pairs = pairs.reshape(EXP_DEV, groups, 2, RANK, adapter_cols).transpose(2, 0, 3, 1, 4)
+    pairs = pairs.reshape(2, EXP_DEV * RANK, D)
+    pairs = jnp.pad(pairs, ((0, 0), (0, LANES - EXP_DEV * RANK), (0, 0)))
     output_terms, ranks, gate, up = experts_forward(
         second_all, gates_all, pairs[0], pairs[1], matrix_in, matrix_out
     )
@@ -943,8 +1059,7 @@
     slot_terms, rank_expert_grad, lift_gate_grad, lift_up_grad = experts_backward(
         cotangents, gates_all, ranks, pairs[0], pairs[1], matrix_in, matrix_out, gate, up
     )
-    slot_sum = line_reduce(slot_terms, 5)
-    layer_output = (middle + output_sum.astype(jnp.float32)).astype(low)
+    slot_sum = line_reduce(slot_terms, 5, 2)
 
     lift_sent = jnp.concatenate([lift_gate_grad, lift_up_grad], axis=2).reshape(EXP_DEV * RANK, D)
     down_sent = dot_left(rank_expert_grad[:, : EXP_DEV * RANK], second_all)
@@ -983,7 +1098,7 @@
     )
     qkv_back = jnp.concatenate([back_query, back_key, back_value], axis=1)
     rank_query_grad = dot_right(qkv_back, lift_query).astype(low)
-    first_terms = (dot_right(qkv_back, qkv_matrix) + dot_plain(rank_query_grad, down_query)).astype(low)
+    first_terms = first_products([back_query, back_key, back_value], rank_query_grad, down_query, dense_all)
     lift_query_grad = lax.dynamic_update_slice(
         jnp.zeros((RANK, 3, parts, width), jnp.float32),
         dot_left(rank_query, qkv_back).reshape(RANK, 3, 1, width),
@@ -1005,10 +1120,8 @@
         ],
         axis=1,
     ).astype(low)
-    owned, first_terms = lax.optimization_barrier((owned, first_terms))
-    first_grad = line_reduce(first_terms, 7)
+    first_grad = lax.psum_scatter(first_terms, "expert", scatter_dimension=0, tiled=True).astype(jnp.float32)
     got = lax.all_to_all(owned, ("dp", "expert"), split_axis=0, concat_axis=0, tiled=True)
-    got, first_grad = lax.optimization_barrier((got, first_grad))
     inverse_first = norm_inverse(inputs)
     input_grad = (
         middle_grad + norm_backward(inputs, inverse_first, gain_rows[0:1], first_grad)
@@ -1030,6 +1143,7 @@
         route_rows,
         0,
     )
+    layer_output = (middle + output_sum.astype(jnp.float32)).astype(low)
     return (
         layer_output,
         input_grad,

time: 953 us -> 901 us (0.945)
  Pallas kernels: 728 us -> 612 us
  waiting for transfers between devices: 27.7 us -> 93.2 us
  matrix products: 82.5 us -> 63 us
  local copies, waits for them, and re-layouts: 40.9 us -> 57.5 us
  other arithmetic: 24.2 us -> 36.7 us
    pallas_call x5 -> x6, Pallas kernels: 446 us -> 331 us  [the longest x2 177 us: line_gather(): pl.pallas_call(functools.partial(gather_kernel, parts, pieces, n), out_sh...]
    dot_general x10 -> x8, matrix products: 43.2 us -> 16.9 us  [dot_right(): lax.dot_general(left, right, (((1,), (1,)), ((), ())), preferred_element_...]
    all_to_all x1, waiting for transfers between devices: 0.01 us -> 21.7 us  [body(): lax.all_to_all(owned, ('dp', 'expert'), split_axis=0, concat_axis=0, tile...]
    all_gather x2, waiting for transfers between devices: 0.01 us -> 20.9 us  [the longest x1 20.9 us: body(): lax.all_gather(expert_rows, 'dp', axis=1, tiled=True)]
    all_gather x1, waiting for transfers between devices: 26.5 us -> 38.4 us  [body(): matrix_out = lax.all_gather(expert_output, 'dp', axis=1, tiled=True)]
    reduce_scatter x0 -> x1, waiting for transfers between devices: none -> 10.3 us  [body(): lax.psum_scatter(first_terms, 'expert', scatter_dimension=0, tiled=True)]
    dot_general x9 -> x8, matrix products: 32 us -> 30.1 us  [dot_plain(): return jnp.dot(left, right, preferred_element_type=jnp.float32)]
  transfers between devices with their start and end apart: 10 -> 11, of which waited for: 1 -> 4; matrix products, arithmetic and copies ran while one was open for 13% -> 15% of each run, Pallas kernels for 77% -> 62%
where the time goes in v3:
time: 901 us; the launch traced here: 894 us
  Pallas kernels  612 us (68%)
  waiting for transfers between devices  93.2 us (10%)
  matrix products  63 us (7%)
  local copies, waits for them, and re-layouts  57.5 us (6%)
  other arithmetic  36.7 us (4%)
  between operations  16.3 us (2%)
  starting transfers between devices  15.6 us (2%)
    pallas_call x2, Pallas kernels, line_gather(): pl.pallas_call(functools.partial(gather_kernel, parts, pieces, n), out_sh...  177 us
    pallas_call x1, Pallas kernels, experts_backward(): pl.pallas_call(functools.partial(backward_kernel, parts), grid=(EXP_DEV,...  101 us
    pallas_call x1, Pallas kernels, line_reduce(): pl.pallas_call(functools.partial(reduce_kernel, parts, pieces), out_shape...  95 us
    pallas_call x1, Pallas kernels, experts_forward(): pl.pallas_call(forward_kernel, grid=(EXP_DEV, FF // TILE), in_specs=[VMEM...  86.6 us
    pallas_call x2, Pallas kernels, exchange(): pl.pallas_call(functools.partial(exchange_kernel, parts, n, stack), out_s...  59.8 us
    pallas_call x1, Pallas kernels, gather_weights(): pl.pallas_call(functools.partial(weights_kernel, parts), out_shape=[jax.S...  40.7 us
    all_gather x1, waiting for transfers between devices, body(): matrix_out = lax.all_gather(expert_output, 'dp', axis=1, tiled=True)  38.4 us
    dot_general x8, matrix products, dot_plain(): return jnp.dot(left, right, preferred_element_type=jnp.float32)  30.1 us
  transfers between devices with their start and end apart: 11, of which 4 were waited for; matrix products, arithmetic and copies ran while one was open for 15% of the time, Pallas kernels for 62%

profile of v3, /device:TPU:9, one launch (start us, length us, event | category | flops | bytes accessed | tf_op | source)
XLA Modules:
  0.0 894.1 jit_solution(5898731184772329941)
XLA Ops:
  17.2 40.7 %gather_weights.1 = (bf16[256,2560]{1,0:T(8,128)(2,1)}, bf16[256,2048]{1,0:T(8,128)(2,1)}) custom-call(bf16[256,1536]{1,0:T(8,128)(2,1)} %bitcast.126, bf16[64,2048]{1,0:T(8,128)(2,1)} %out.1, bf16[64,1024]{1,0:T(8,128)(2,1)} %concatenate.41.small), custom_call_target="tpu_custom_call" | custom-call | bytes 165150720 | tf_op jit(solution)/shard_map/gather_weights/pallas_call | solution.py:424
  57.9 5.2 pad_maximum_fusion
  63.1 38.4 %all-gather.5.cloned.1.call-done.out_ref = bf16[4,1024,2048]{2,1,0:T(8,128)(2,1)} async-done(((bf16[4,128,2048]{2,1,0:T(8,128)(2,1)}), bf16[4,1024,2048]{2,1,0:T(8,128)(2,1)}) %all-gather.5.cloned.1.call-update) | async-done | bytes 16777232 | tf_op jit(solution)/shard_map/all_gather | solution.py:934
  102.8 85.9 %line_gather_1.1 = bf16[1280,2048]{1,0:T(8,128)(2,1)} custom-call(bf16[320,2048]{1,0:T(8,128)(2,1)} %refs_0_.2), custom_call_target="tpu_custom_call" | custom-call | bytes 367001600 | tf_op jit(solution)/shard_map/line_gather_1/pallas_call | solution.py:147
  197.0 5.7 pick_rows.1
  210.6 12.3 %fusion.4 = f32[1280,1536]{1,0:T(8,128)S(1)} fusion(bf16[2048,2560]{1,0:T(8,128)(2,1)} %all-gather.7.cloned.1.call-done.rows_ref.refs_0_.refs_1_.refs_2_, bf16[1280,2048]{1,0:T(8,128)(2,1)} %line_gather_1.1, f32[2048]{0:T(1024)S(1)} %bitcast.154, f32[1280]{0:T(1024)S(1)} %add_rsqrt_fusion), kind=kOutput, calls=%fused_computation.7 | convolution fusion | flops 8063549440 | bytes 19411968 | tf_op jit(solution)/shard_map/dot_general | solution.py:31
  226.1 14.1 %attention.1 = (bf16[1280,512]{1,0:T(8,128)(2,1)S(1)}, f32[4,1280,1]{2,1,0:T(8,128)S(1)}) custom-call(s32[1280,1]{1,0:T(8,128)S(1)} %reshape_select_fusion.column_ref, s32[1,1280]{1,0:T(1,128)S(1)} %compare_select_fusion.row_ref, bf16[1280,1536]{1,0:T(8,128)(2,1)} %fusion.3.query_ref.key_ref.value_ref, bf16[1280,1536]{1,0:T(8,128)(2,1)} %fusion.3.query_ref.key_ref.value_ref, ...), custom_call_target="tpu_custom_call" | custom-call | flops 2516582400 | bytes 5242880 | tf_op jit(solution)/shard_map/attention/pallas_call | solution.py:483
  242.7 30.8 %exchange_3.1 = bf16[320,2048]{1,0:T(8,128)(2,1)} custom-call(bf16[1280,512]{1,0:T(8,128)(2,1)} %copy-done.1), custom_call_target="tpu_custom_call" | custom-call | bytes 91750400 | tf_op jit(solution)/shard_map/exchange_3/pallas_call | solution.py:212
  273.6 7.2 convert_add_fusion
  289.6 91.0 %line_gather_4.1 = (bf16[1280,2048]{1,0:T(8,128)(2,1)}, bf16[1280,128]{1,0:T(8,128)(2,1)}) custom-call(bf16[320,2048]{1,0:T(8,128)(2,1)} %copy-done.7, bf16[320,128]{1,0:T(8,128)(2,1)} %pad.34.refs_1_), custom_call_target="tpu_custom_call" | custom-call | bytes 389939200 | tf_op jit(solution)/shard_map/line_gather_4/pallas_call | solution.py:147
  383.0 20.9 %all-gather.11.cloned.1.call-done = bf16[4,2304,2048]{2,1,0:T(8,128)(2,1)} async-done(((bf16[4,288,2048]{2,1,0:T(8,128)(2,1)}), bf16[4,2304,2048]{2,1,0:T(8,128)(2,1)}) %all-gather.11.cloned.1.call-update) | async-done | bytes 37748752 | tf_op jit(solution)/shard_map/all_gather | solution.py:963
  408.1 86.6 %experts_forward.1 = (bf16[1280,2048]{1,0:T(8,128)(2,1)}, bf16[1280,128]{1,0:T(8,128)(2,1)}, bf16[4,1280,1024]{2,1,0:T(8,128)(2,1)}, bf16[4,1280,1024]{2,1,0:T(8,128)(2,1)}) custom-call(bf16[1280,2048]{1,0:T(8,128)(2,1)} %get-tuple-element.44.rows_ref, bf16[1280,128]{1,0:T(8,128)(2,1)} %get-tuple-element.45.gates_ref, ...), custom_call_target="tpu_custom_call" | custom-call | flops 64424509440 | bytes 71303168 | tf_op jit(solution)/shard_map/experts_forward/pallas_call | solution.py:653
  495.7 100.8 %experts_backward.1 = (bf16[1280,2176]{1,0:T(8,128)(2,1)}, bf16[1280,128]{1,0:T(8,128)(2,1)}, f32[4,16,1024]{2,1,0:T(8,128)}, f32[4,16,1024]{2,1,0:T(8,128)}) custom-call(bf16[1280,128]{1,0:T(8,128)(2,1)} %get-tuple-element.45.gates_ref, bf16[1280,128]{1,0:T(8,128)(2,1)} %get-tuple-element.49.ranks_ref, bf16[128,2048]{1,0:T(8,128)(2,1)} %get-tuple-element.103.down_ref, ...), custom_call_target="tpu_custom_call" | custom-call | flops 85899345920 | bytes 71303168 | tf_op jit(solution)/shard_map/experts_backward/pallas_call | solution.py:786
  596.5 95.0 %line_reduce_5.1 = f32[320,2176]{1,0:T(8,128)S(1)} custom-call(bf16[1280,2176]{1,0:T(8,128)(2,1)} %get-tuple-element.54.src), custom_call_target="tpu_custom_call" | custom-call | bytes 389939200 | tf_op jit(solution)/shard_map/line_reduce_5/pallas_call | solution.py:314
  697.8 5.2 subtract_add_fusion
  704.3 5.3 fusion.47
  712.2 29.0 %exchange_6.1.grad_ref = bf16[1280,512]{1,0:T(8,128)(2,1)} custom-call(bf16[1280,512]{1,0:T(8,128)(2,1)} %bitcast.124), custom_call_target="tpu_custom_call" | custom-call | bytes 91750400 | tf_op jit(solution)/shard_map/exchange_6/pallas_call | solution.py:212
  742.6 19.1 %attention_back.1 = (bf16[1280,512]{1,0:T(8,128)(2,1)S(1)}, bf16[1280,512]{1,0:T(8,128)(2,1)S(1)}, bf16[1280,512]{1,0:T(8,128)(2,1)S(1)}) custom-call(s32[1280,1]{1,0:T(8,128)S(1)} %reshape_select_fusion.column_ref, s32[1,1280]{1,0:T(1,128)S(1)} %copy-done.3, bf16[1280,1536]{1,0:T(8,128)(2,1)} %fusion.3.query_ref.key_ref.value_ref, ...), custom_call_target="tpu_custom_call" | custom-call | flops 6710886400 | bytes 10485760 | tf_op jit(solution)/shard_map/attention_back/pallas_call | solution.py:534
  764.4 12.9 %first_products.1 = bf16[1280,2048]{1,0:T(8,128)(2,1)} custom-call(bf16[1280,512]{1,0:T(8,128)(2,1)S(1)} %get-tuple-element.56.query_ref, bf16[1280,512]{1,0:T(8,128)(2,1)S(1)} %get-tuple-element.57.key_ref, bf16[1280,512]{1,0:T(8,128)(2,1)S(1)} %get-tuple-element.58.value_ref, bf16[1280,16]{1,0:T(8,128)(2,1)S(1)} %convolution_convert_fusion.rank_ref, ...), custom_call_target="tpu_custom_call" | custom-call | flops 8053063680 | bytes 11534336 | tf_op jit(solution)/shard_map/first_products/pallas_call | solution.py:858
  784.9 5.2 all-to-all-start.1
  824.7 6.7 all-to-all-start
  834.8 21.7 %all-to-all-done = bf16[32,2,3712]{2,1,0:T(2,128)(2,1)} async-done(((bf16[32,2,3712]{2,1,0:T(2,128)(2,1)}), bf16[32,2,3712]{2,1,0:T(2,128)(2,1)}, u32[]{:S(2)}, u32[]{:S(2)}) %all-to-all-start) | async-done | bytes 475168 | tf_op jit(solution)/shard_map/all_to_all | solution.py:1124
  859.9 4.8 convert_reduce_fusion
  872.0 10.3 %reduce-scatter.5.cloned.1.call-done = bf16[320,2048]{1,0:T(8,128)(2,1)} async-done(((bf16[1280,2048]{1,0:T(8,128)(2,1)}), bf16[320,2048]{1,0:T(8,128)(2,1)}) %reduce-scatter.5.cloned.1.call-update) | async-done | bytes 1310736 | tf_op jit(solution)/shard_map/reduce_scatter | solution.py:1123
  (243 shorter events, 122.9 us)
Async XLA Ops:
  7.2 94.2 %all-gather.5.cloned.1.call-start = ((), (), s32[]{:S(2)}) async-start(), calls=%async_computation.4 | async-start | bytes 18874368 | tf_op jit(solution)/shard_map/all_gather | solution.py:934
  7.9 187.1 %all-gather.7.cloned.1.call-start = ((), (), s32[]{:S(2)}) async-start(), calls=%async_computation.5 | async-start | bytes 11796480 | tf_op jit(solution)/shard_map/all_gather | solution.py:960
  101.4 172.2 %all-gather.9.cloned.1.call-start = ((), (), s32[]{:S(2)}) async-start(), calls=%async_computation.6 | async-start | bytes 9437184 | tf_op jit(solution)/shard_map/all_gather | solution.py:962
  102.2 301.7 %all-gather.11.cloned.1.call-start = ((), (), s32[]{:S(2)}) async-start(), calls=%async_computation.7 | async-start | bytes 42467328 | tf_op jit(solution)/shard_map/all_gather | solution.py:963
  102.8 87.2 %copy-start.43 = (s32[320,8]{0,1:T(8,128)S(1)}, s32[320,8]{0,1:T(8,128)}, u32[]{:S(2)}) copy-start(s32[320,8]{0,1:T(8,128)} %param.31) | copy-start | bytes 30724
  102.8 87.4 %copy-start.47 = (s32[1,8]{1,0:T(1,128)S(1)}, s32[1,8]{1,0:T(1,128)}, u32[]{:S(2)}) copy-start(s32[1,8]{1,0:T(1,128)} %param.33) | copy-start | bytes 100
  102.8 595.0 %reduce-scatter.3.cloned.1.call-start = ((), (), s32[]{:S(2)}) async-start(), calls=%async_computation.8 | async-start | bytes 6553600 | tf_op jit(solution)/shard_map/reduce_scatter | solution.py:1058
  188.8 96.2 %collective-permute-start = (bf16[320,2048]{1,0:T(8,128)(2,1)}, bf16[320,2048]{1,0:T(8,128)(2,1)}, u32[]{:S(2)}, u32[]{:S(2)}) collective-permute-start(bf16[320,2048]{1,0:T(8,128)(2,1)} %refs_0_.3), channel_id=1, source_target_pairs={{0,1},{1,2},{2,3},{3,0},{4,5},{5,6},{6,7},{7,4},{8,9},{9,10},{10,1... | collective-permute-start | bytes 3932168 | tf_op jit(solution)/shard_map/ppermute | solution.py:1003
  190.2 98.6 %copy-start.18 = (pred[320,16]{1,0:T(8,128)(4,1)}, pred[320,16]{1,0:T(8,128)(4,1)S(1)}, u32[]{:S(2)}) copy-start(pred[320,16]{1,0:T(8,128)(4,1)S(1)} %copy.102) | copy-start | bytes 15364
  190.4 35.6 %copy-start.2 = (s32[1,1280]{1,0:T(1,128)}, s32[1,1280]{1,0:T(1,128)S(1)}, u32[]{:S(2)}) copy-start(s32[1,1280]{1,0:T(1,128)S(1)} %compare_select_fusion.row_ref) | copy-start | bytes 15364
  197.0 89.4 %copy-start.38 = (bf16[32,4,16]{2,1,0:T(4,128)(2,1)}, bf16[32,4,16]{2,1,0:T(4,128)(2,1)S(1)}, u32[]{:S(2)}) copy-start(bf16[32,4,16]{2,1,0:T(4,128)(2,1)S(1)} %slice.121) | copy-start | bytes 12292
  206.5 77.7 %copy-start.33 = (f32[1,2048]{1,0:T(1,128)}, f32[1,2048]{1,0:T(1,128)S(1)}, u32[]{:S(2)}) copy-start(f32[1,2048]{1,0:T(1,128)S(1)} %get-tuple-element.98) | copy-start | bytes 24580
  288.5 115.3 %copy-start.36 = (f32[320]{0:T(512)}, f32[320]{0:T(512)S(1)}, u32[]{:S(2)}) copy-start(f32[320]{0:T(512)S(1)} %get-tuple-element.110) | copy-start | bytes 3844
  288.5 117.8 %copy-start.13 = (f32[320,16]{1,0:T(8,128)}, f32[320,16]{1,0:T(8,128)S(1)}, u32[]{:S(2)}) copy-start(f32[320,16]{1,0:T(8,128)S(1)} %get-tuple-element.111) | copy-start | bytes 61444
  288.8 115.1 %copy-start.39 = (f32[320]{0:T(512)}, f32[320]{0:T(512)S(1)}, u32[]{:S(2)}) copy-start(f32[320]{0:T(512)S(1)} %fusion.19) | copy-start | bytes 3844
  380.7 115.0 %collective-permute-start.2 = (bf16[320,2048]{1,0:T(8,128)(2,1)}, bf16[320,2048]{1,0:T(8,128)(2,1)}, u32[]{:S(2)}, u32[]{:S(2)}) collective-permute-start(bf16[320,2048]{1,0:T(8,128)(2,1)} %refs_0_.3), channel_id=1, source_target_pairs={{0,3},{1,0},{2,1},{3,2},{4,7},{5,4},{6,5},{7,6},{8,11},{9,8},{10,9... | collective-permute-start | bytes 3932168 | tf_op jit(solution)/shard_map/ppermute | solution.py:1003
  382.9 112.7 %collective-permute-start.1 = (bf16[320,2048]{1,0:T(8,128)(2,1)}, bf16[320,2048]{1,0:T(8,128)(2,1)}, u32[]{:S(2)}, u32[]{:S(2)}) collective-permute-start(bf16[320,2048]{1,0:T(8,128)(2,1)} %refs_0_.3), channel_id=1, source_target_pairs={{0,2},{1,3},{2,0},{3,1},{4,6},{5,7},{6,4},{7,5},{8,10},{9,11},{10,... | collective-permute-start | bytes 3932168 | tf_op jit(solution)/shard_map/ppermute | solution.py:1003
  494.8 387.6 %reduce-scatter.5.cloned.1.call-start = ((), (), s32[]{:S(2)}) async-start(), calls=%async_computation.9 | async-start | bytes 6553600 | tf_op jit(solution)/shard_map/reduce_scatter | solution.py:1123
  596.5 95.0 %copy-start.14 = (f32[320,16]{1,0:T(8,128)S(1)}, f32[320,16]{1,0:T(8,128)}, u32[]{:S(2)}) copy-start(f32[320,16]{1,0:T(8,128)} %copy-done.13) | copy-start | bytes 61444
  596.5 95.0 %copy-start.19 = (pred[320,16]{1,0:T(8,128)(4,1)S(1)}, pred[320,16]{1,0:T(8,128)(4,1)}, u32[]{:S(2)}) copy-start(pred[320,16]{1,0:T(8,128)(4,1)} %copy-done.18) | copy-start | bytes 15364
  596.5 95.0 %copy-start.37 = (f32[320]{0:T(512)S(1)}, f32[320]{0:T(512)}, u32[]{:S(2)}) copy-start(f32[320]{0:T(512)} %copy-done.36) | copy-start | bytes 3844
  596.5 95.0 %copy-start.40 = (f32[320]{0:T(512)S(1)}, f32[320]{0:T(512)}, u32[]{:S(2)}) copy-start(f32[320]{0:T(512)} %copy-done.39) | copy-start | bytes 3844
  784.9 39.8 %all-to-all-start.1 = ((bf16[8,128,256]{2,1,0:T(8,128)(2,1)}), bf16[8,128,256]{2,1,0:T(8,128)(2,1)S(1)}, u32[]{:S(2)}, u32[]{:S(2)}) async-start(bf16[8,128,256]{2,1,0:T(8,128)(2,1)} %maximum_bitcast_fusion.1), calls=%async_computation.3 | async-start | bytes 1048576 | tf_op jit(solution)/shard_map/all_to_all | solution.py:1072
  824.7 31.8 %all-to-all-start = ((bf16[32,2,3712]{2,1,0:T(2,128)(2,1)}), bf16[32,2,3712]{2,1,0:T(2,128)(2,1)}, u32[]{:S(2)}, u32[]{:S(2)}) async-start(bf16[32,2,3712]{2,1,0:T(2,128)(2,1)} %reshape.394), calls=%async_computation.2 | async-start | bytes 950272 | tf_op jit(solution)/shard_map/all_to_all | solution.py:1124
  (35 other events, 220.0 us)
Sparse Core Ops, SparseCore 0:
  9.9 91.4 all-gather.4
  103.3 63.2 all-gather.6
  168.5 54.3 all-gather.8
  224.7 179.1 all-gather.10
  494.9 93.3 reduce-scatter.2
  777.5 104.8 reduce-scatter.4

commit v4 on v3

--- a/solution.py
+++ b/solution.py
@@ -326,7 +326,7 @@
     )(terms)
 
 
-def weights_kernel(parts, blocks, out, small, dst, dst_out, own_sem, send, recv, send_up, recv_up, send_down, recv_down):
+def weights_kernel(parts, blocks, out, small, chosen, dst, dst_out, dst_chosen, own_sem, send, recv, send_up, recv_up, send_down, recv_down):
     me = lax.axis_index("expert")
     share = out.shape[0]
     wide = blocks.shape[1]
@@ -345,7 +345,7 @@
             device_id_type=MESH,
         )
 
-    shared = ((out, dst_out, 0), (small, dst, wide))
+    shared = ((out, dst_out, 0), (small, dst, wide), (chosen, dst_chosen, 0))
 
     def place(i, origin):
         src, into, at = shared[i]
@@ -366,7 +366,7 @@
         for way, sends, recvs in streams:
             origin, to = me - way * step, me + way
             has = (origin >= 0) & (origin < parts)
-            for i in range(2):
+            for i in range(3):
                 if step > 0:
 
                     @pl.when(has)
@@ -389,6 +389,7 @@
                         (blocks.at[rows(me)], dst.at[rows(me), :wide]),
                         (out, place(0, me)),
                         (small, place(1, me)),
+                        (chosen, place(2, me)),
                     )
                 )
             ]
@@ -399,7 +400,7 @@
         copy.wait()
     for way, sends, recvs in streams:
         to, last = me + way, me - way * (parts - 1)
-        for i in range(2):
+        for i in range(3):
 
             @pl.when((last >= 0) & (last < parts))
             def _(i=i, last=last, sends=sends, recvs=recvs):
@@ -417,7 +418,7 @@
         exchanged(k, me, lax.rem(me + parts - k, parts)).wait_recv()
 
 
-def gather_weights(blocks, out, small, cid):
+def gather_weights(blocks, out, small, chosen, cid):
     parts = lax.axis_size("expert")
     sem = pltpu.SemaphoreType.DMA
     rows, cols = blocks.shape[0], blocks.shape[1] + small.shape[1]
@@ -426,14 +427,15 @@
         out_shape=[
             jax.ShapeDtypeStruct((rows, cols), blocks.dtype),
             jax.ShapeDtypeStruct((rows, out.shape[1]), blocks.dtype),
-        ],
-        in_specs=[ANY] * 3,
-        out_specs=[ANY] * 2,
-        scratch_shapes=[sem((3,)), sem((parts - 1,)), sem((parts - 1,))] + [sem((2, parts - 1))] * 4,
+            jax.ShapeDtypeStruct((rows, chosen.shape[1]), blocks.dtype),
+        ],
+        in_specs=[ANY] * 4,
+        out_specs=[ANY] * 3,
+        scratch_shapes=[sem((4,)), sem((parts - 1,)), sem((parts - 1,))] + [sem((3, parts - 1))] * 4,
         cost_estimate=transfer_cost(rows * (cols + out.shape[1])),
         compiler_params=pltpu.CompilerParams(collective_id=cid, has_side_effects=True),
         name="gather_weights",
-    )(blocks, out, small)
+    )(blocks, out, small, chosen)
 
 
 def diagonal_mask(column_ref, row_ref, block):
@@ -601,8 +603,8 @@
         here = row_chunk(b)
         rows = rows_ref[here, :]
         _, column = gate_column(gates_ref, here, j)
-        gate = dot_plain(rows, in_gate_ref[0].reshape(D, TILE)) + dot_plain(ranks_ref[here, :], lift_gate)
-        up = dot_plain(rows, in_up_ref[0].reshape(D, TILE)) + dot_plain(ranks_ref[here, :], lift_up)
+        gate = dot_plain(rows, in_gate_ref[0]) + dot_plain(ranks_ref[here, :], lift_gate)
+        up = dot_plain(rows, in_up_ref[0]) + dot_plain(ranks_ref[here, :], lift_up)
         gate_ref[0, here, :] = gate.astype(jnp.bfloat16)
         up_ref[0, here, :] = up.astype(jnp.bfloat16)
         hidden = (column * (gate * jax.nn.sigmoid(gate) * up)).astype(jnp.bfloat16)
@@ -631,13 +633,13 @@
             copy(b).wait()
 
 
-def weight_specs(ring, share):
+def weight_specs():
     tiles = FF // TILE
     return [
         pl.BlockSpec((LANES, TILE), lambda j, f: (0, f)),
         pl.BlockSpec((LANES, TILE), lambda j, f: (0, f + tiles)),
-        pl.BlockSpec((1, ring, share, TILE), lambda j, f: (j, 0, 0, f)),
-        pl.BlockSpec((1, ring, share, TILE), lambda j, f: (j, 0, 0, f + tiles)),
+        pl.BlockSpec((1, D, TILE), lambda j, f: (j, 0, f)),
+        pl.BlockSpec((1, D, TILE), lambda j, f: (j, 0, f + tiles)),
         pl.BlockSpec((1, TILE, D), lambda j, f: (j, f, 0)),
     ]
 
@@ -653,7 +655,7 @@
     return pl.pallas_call(
         forward_kernel,
         grid=(EXP_DEV, FF // TILE),
-        in_specs=[VMEM] * 3 + weight_specs(*matrix_in.shape[1:2], D // matrix_in.shape[1]),
+        in_specs=[VMEM] * 3 + weight_specs(),
         out_specs=[
             ANY,
             pl.BlockSpec((total, LANES), lambda j, f: (0, 0), pipeline_mode=pl.Buffered(1)),
@@ -673,7 +675,7 @@
         ],
         compiler_params=EXPERT_PARAMS,
         cost_estimate=pl.CostEstimate(
-            flops=6 * EXP_DEV * total * D * FF,
+            flops=10 * EXP_DEV * total * D * FF,
             bytes_accessed=EXP_DEV * 6 * D * FF + 8 * total * D,
             transcendentals=EXP_DEV * total * FF,
         ),
@@ -737,8 +739,8 @@
         back = raw * column
         to_gate = (back * up * (sigma + silu * (1.0 - sigma))).astype(jnp.bfloat16)
         to_up = (back * silu).astype(jnp.bfloat16)
-        slot_acc[here, :] += dot_right(to_gate, in_gate_ref[0].reshape(D, TILE)) + dot_right(
-            to_up, in_up_ref[0].reshape(D, TILE)
+        slot_acc[here, :] += dot_right(to_gate, in_gate_ref[0]) + dot_right(
+            to_up, in_up_ref[0]
         )
         rank_acc[here, :] += dot_right(to_gate, lift_gate) + dot_right(to_up, lift_up)
         gate_acc[here, :] += jnp.where(mine, gate_grad, 0.0)
@@ -786,7 +788,7 @@
     return pl.pallas_call(
         functools.partial(backward_kernel, parts),
         grid=(EXP_DEV, FF // TILE),
-        in_specs=[VMEM] * 3 + weight_specs(*matrix_in.shape[1:2], D // matrix_in.shape[1]) + [kept, kept] + [ANY] * parts,
+        in_specs=[VMEM] * 3 + weight_specs() + [kept, kept] + [ANY] * parts,
         out_specs=[
             ANY,
             pl.BlockSpec((total, LANES), lambda j, f: (0, 0), pipeline_mode=pl.Buffered(1)),
@@ -810,7 +812,7 @@
         ],
         compiler_params=EXPERT_PARAMS,
         cost_estimate=pl.CostEstimate(
-            flops=8 * EXP_DEV * total * D * FF,
+            flops=12 * EXP_DEV * total * D * FF,
             bytes_accessed=EXP_DEV * 6 * D * FF + 8 * total * D,
             transcendentals=EXP_DEV * total * FF,
         ),
@@ -818,26 +820,29 @@
     )(gates, ranks, down, lift, lift, matrix_in, matrix_in, matrix_out, gate, up, *blocks)
 
 
-def pick_kernel(sel_ref, rows_ref, out_ref):
-    @pl.when(pl.program_id(0) == 0)
-    def _():
-        out_ref[...] = jnp.zeros_like(out_ref)
-
-    out_ref[...] += dot_right(sel_ref[...], rows_ref[...])
-
-
-def pick_rows(chosen, dense, at):
-    rows, cols = chosen.shape
-    wide = 2 * LANES
+def pick_kernel(experts, chosen_ref, small_ref, picked_ref, router_ref, gain_ref):
+    row = lax.broadcasted_iota(jnp.int32, (LANES, LANES), 0)
+    same = row == lax.broadcasted_iota(jnp.int32, (LANES, LANES), 1)
+    every = same.astype(jnp.float32).astype(jnp.bfloat16)
+    router = (same & (row < experts)).astype(jnp.float32).astype(jnp.bfloat16)
+    gain_row = lax.broadcasted_iota(jnp.int32, (8, LANES), 0) + 64
+    gain = gain_row == lax.broadcasted_iota(jnp.int32, (8, LANES), 1)
+    picked_ref[...] = dot_right(every, chosen_ref[...]).astype(jnp.bfloat16)
+    router_ref[...] = dot_right(router, small_ref[...]).astype(jnp.bfloat16)
+    gain_ref[...] = dot_right(gain.astype(jnp.float32).astype(jnp.bfloat16), small_ref[...])
+
+
+def pick_rows(chosen, dense, at, experts):
     return pl.pallas_call(
-        pick_kernel,
-        grid=(cols // wide,),
-        in_specs=[
-            pl.BlockSpec((rows, wide), lambda i: (0, i)),
-            pl.BlockSpec((dense.shape[0], wide), lambda i: (0, at // wide + i)),
-        ],
-        out_specs=pl.BlockSpec((rows, dense.shape[0]), lambda i: (0, 0)),
-        out_shape=jax.ShapeDtypeStruct((rows, dense.shape[0]), jnp.float32),
+        functools.partial(pick_kernel, experts),
+        grid=(1,),
+        in_specs=[VMEM, pl.BlockSpec((D, LANES), lambda i: (0, at // LANES))],
+        out_specs=[all_of(LANES, D), all_of(LANES, D), all_of(8, D)],
+        out_shape=[
+            jax.ShapeDtypeStruct((LANES, D), jnp.bfloat16),
+            jax.ShapeDtypeStruct((LANES, D), jnp.bfloat16),
+            jax.ShapeDtypeStruct((8, D), jnp.float32),
+        ],
         name="pick_rows",
     )(chosen, dense)
 
@@ -867,6 +872,236 @@
         ),
         name="first_products",
     )(*backs, ranks, down, dense, dense, dense)
+
+
+def sublayer_params():
+    return pltpu.CompilerParams(
+        dimension_semantics=("arbitrary",), vmem_limit_bytes=56 * 1024 * 1024
+    )
+
+
+def all_of(*shape):
+    return pl.BlockSpec(shape, lambda i: (0,) * len(shape))
+
+
+def qkv_kernel(tokens_ref, gain_ref, down_ref, lift_ref, weight_ref, normed_ref, rank_ref, qkv_ref):
+    @pl.when(pl.program_id(0) == 0)
+    def _():
+        rows = tokens_ref.shape[0] // 4
+
+        @pl.loop(0, 4)
+        def _(b):
+            here = row_chunk(b, rows)
+            values = tokens_ref[here, :].astype(jnp.float32)
+            normed = (values * norm_inverse(values) * gain_ref[...]).astype(jnp.bfloat16)
+            normed_ref[here, :] = normed
+            rank_ref[here, :] = dot_right(normed, down_ref[...]).astype(jnp.bfloat16)
+
+    total = dot_plain(normed_ref[...], weight_ref[...]) + dot_plain(rank_ref[...], lift_ref[...])
+    qkv_ref[...] = total.astype(jnp.bfloat16)
+
+
+def project_qkv(tokens, gain, down, lift, dense):
+    total, width = tokens.shape[0], lift.shape[1] // 3
+    return pl.pallas_call(
+        qkv_kernel,
+        grid=(3,),
+        in_specs=[
+            VMEM,
+            VMEM,
+            VMEM,
+            pl.BlockSpec((RANK, width), lambda i: (0, i)),
+            pl.BlockSpec((D, width), lambda i: (0, i)),
+        ],
+        out_specs=[
+            all_of(total, D),
+            all_of(total, RANK),
+            pl.BlockSpec((total, width), lambda i: (0, i)),
+        ],
+        out_shape=[
+            jax.ShapeDtypeStruct((total, D), jnp.bfloat16),
+            jax.ShapeDtypeStruct((total, RANK), jnp.bfloat16),
+            jax.ShapeDtypeStruct((total, 3 * width), jnp.bfloat16),
+        ],
+        compiler_params=sublayer_params(),
+        cost_estimate=pl.CostEstimate(
+            flops=6 * total * D * width, bytes_accessed=6 * D * width + 8 * total * D, transcendentals=0
+        ),
+        name="project_qkv",
+    )(tokens, gain, down, lift, dense)
+
+
+def middle_kernel(
+    experts,
+    mixed_ref,
+    tokens_ref,
+    down_mix_ref,
+    lift_mix_ref,
+    gain_ref,
+    down_route_ref,
+    router_ref,
+    lift_route_ref,
+    routed_ref,
+    out_ref,
+    middle_ref,
+    rank_mix_ref,
+    inverse_ref,
+    second_ref,
+    rank_route_ref,
+    probs_ref,
+    gates_ref,
+):
+    i = pl.program_id(0)
+    tile = out_ref.shape[1]
+
+    @pl.when(i == 0)
+    def _():
+        rank_mix_ref[...] = dot_right(mixed_ref[...], down_mix_ref[...]).astype(jnp.bfloat16)
+
+    here = pl.ds(pl.multiple_of(i * tile, tile), tile)
+    branch = dot_plain(mixed_ref[...], out_ref[...]) + dot_plain(rank_mix_ref[...], lift_mix_ref[...])
+    middle_ref[:, here] = tokens_ref[...].astype(jnp.float32) + branch
+
+    @pl.when(i == D // tile - 1)
+    def _():
+        middle = middle_ref[...]
+        inverse = norm_inverse(middle)
+        inverse_ref[...] = inverse
+        second = (middle * inverse * gain_ref[...]).astype(jnp.bfloat16)
+        second_ref[...] = second
+        rank_route = dot_right(second, down_route_ref[...]).astype(jnp.bfloat16)
+        rank_route_ref[...] = rank_route
+        logits = dot_right(second, router_ref[...]) + dot_plain(rank_route, lift_route_ref[...])
+        lane = lax.broadcasted_iota(jnp.int32, logits.shape, 1)
+        logits = jnp.where(lane < experts, logits, MASKED)
+        exped = jnp.exp(logits - jnp.max(logits, axis=1, keepdims=True))
+        probs = exped / jnp.sum(exped, axis=1, keepdims=True)
+        probs_ref[...] = probs
+        gates_ref[...] = (probs * routed_ref[...]).astype(jnp.bfloat16)
+
+
+def finish_attention(experts, mixed, tokens, down_mix, lift_mix, gain, down_route, router, lift_route, routed, out_matrix):
+    piece, tile = tokens.shape[0], 512
+    column = lambda i: (0, i)
+    return pl.pallas_call(
+        functools.partial(middle_kernel, experts),
+        grid=(D // tile,),
+        in_specs=[
+            VMEM,
+            pl.BlockSpec((piece, tile), column),
+            VMEM,
+            pl.BlockSpec((RANK, tile), column),
+            VMEM,
+            VMEM,
+            VMEM,
+            VMEM,
+            VMEM,
+            pl.BlockSpec((D, tile), column),
+        ],
+        out_specs=[
+            all_of(piece, D),
+            all_of(piece, RANK),
+            all_of(piece, 1),
+            all_of(piece, D),
+            all_of(piece, RANK),
+            all_of(piece, LANES),
+            all_of(piece, LANES),
+        ],
+        out_shape=[
+            jax.ShapeDtypeStruct((piece, D), jnp.float32),
+            jax.ShapeDtypeStruct((piece, RANK), jnp.bfloat16),
+            jax.ShapeDtypeStruct((piece, 1), jnp.float32),
+            jax.ShapeDtypeStruct((piece, D), jnp.bfloat16),
+            jax.ShapeDtypeStruct((piece, RANK), jnp.bfloat16),
+            jax.ShapeDtypeStruct((piece, LANES), jnp.float32),
+            jax.ShapeDtypeStruct((piece, LANES), jnp.bfloat16),
+        ],
+        compiler_params=sublayer_params(),
+        cost_estimate=pl.CostEstimate(
+            flops=2 * piece * D * D, bytes_accessed=2 * D * D + 12 * piece * D, transcendentals=piece * LANES
+        ),
+        name="finish_attention",
+    )(mixed, tokens, down_mix, lift_mix, gain, down_route, router, lift_route, routed, out_matrix)
+
+
+def middle_back_kernel(
+    slot_ref,
+    probs_ref,
+    routed_ref,
+    middle_ref,
+    inverse_ref,
+    cotangent_ref,
+    gain_ref,
+    router_ref,
+    lift_route_ref,
+    down_route_ref,
+    lift_mix_ref,
+    down_mix_ref,
+    out_ref,
+    mixed_ref,
+    grad_ref,
+    branch_ref,
+    logit_ref,
+    rank_route_ref,
+    rank_mix_ref,
+):
+    @pl.when(pl.program_id(0) == 0)
+    def _():
+        parts = slot_ref[:, D:]
+        prob_grad = (parts + pltpu.roll(parts, LANES // 2, 1)) * routed_ref[...]
+        probs = probs_ref[...]
+        logit_grad = probs * (prob_grad - jnp.sum(probs * prob_grad, axis=1, keepdims=True))
+        logit_grad = logit_grad.astype(jnp.bfloat16)
+        logit_ref[...] = logit_grad
+        rank_route_grad = dot_right(logit_grad, lift_route_ref[...]).astype(jnp.bfloat16)
+        rank_route_ref[...] = rank_route_grad
+        upstream = slot_ref[:, :D] + dot_plain(logit_grad, router_ref[...])
+        upstream = upstream + dot_plain(rank_route_grad, down_route_ref[...])
+        middle_grad = cotangent_ref[...].astype(jnp.float32) + norm_backward(
+            middle_ref[...], inverse_ref[...], gain_ref[...], upstream
+        )
+        grad_ref[...] = middle_grad
+        branch_ref[...] = middle_grad.astype(jnp.bfloat16)
+        rank_mix_ref[...] = dot_right(branch_ref[...], lift_mix_ref[...]).astype(jnp.bfloat16)
+
+    mixed = dot_right(branch_ref[...], out_ref[...]) + dot_plain(rank_mix_ref[...], down_mix_ref[...])
+    mixed_ref[...] = mixed.astype(jnp.bfloat16)
+
+
+def middle_backward(
+    width, slot, probs, routed, middle, inverse, cotangent, gain, router, lift_route, down_route, lift_mix, down_mix, out_matrix
+):
+    piece = middle.shape[0]
+    return pl.pallas_call(
+        middle_back_kernel,
+        grid=(D // width,),
+        in_specs=[VMEM] * 11
+        + [
+            pl.BlockSpec((RANK, width), lambda i: (0, i)),
+            pl.BlockSpec((width, D), lambda i: (i, 0)),
+        ],
+        out_specs=[
+            pl.BlockSpec((piece, width), lambda i: (i, 0)),
+            all_of(piece, D),
+            all_of(piece, D),
+            all_of(piece, LANES),
+            all_of(piece, RANK),
+            all_of(piece, RANK),
+        ],
+        out_shape=[
+            jax.ShapeDtypeStruct((piece * D // width, width), jnp.bfloat16),
+            jax.ShapeDtypeStruct((piece, D), jnp.float32),
+            jax.ShapeDtypeStruct((piece, D), jnp.bfloat16),
+            jax.ShapeDtypeStruct((piece, LANES), jnp.bfloat16),
+            jax.ShapeDtypeStruct((piece, RANK), jnp.bfloat16),
+            jax.ShapeDtypeStruct((piece, RANK), jnp.bfloat16),
+        ],
+        compiler_params=sublayer_params(),
+        cost_estimate=pl.CostEstimate(
+            flops=2 * piece * D * D, bytes_accessed=2 * D * D + 24 * piece * D, transcendentals=0
+        ),
+        name="middle_backward",
+    )(slot, probs, routed, middle, inverse, cotangent, gain, router, lift_route, down_route, lift_mix, down_mix, out_matrix)
 
 
 def norm_inverse(values):
@@ -921,84 +1156,86 @@
     route_rows = ADAPTERS * RANK // ways
     adapter = adapter_ids[0]
 
+    matrix_out = lax.all_gather(expert_output, "dp", axis=1, tiled=True)
+
+    group_ids = lax.all_gather(adapter_ids, "dp", axis=0, tiled=True)
+    hot = group_ids[:, None] == jnp.arange(ADAPTERS, dtype=jnp.int32)
+    group_hot = hot.astype(jnp.float32)
     adapter_cols = expert_lift.shape[3]
-    pairs_own = jnp.stack([expert_down.transpose(0, 2, 3, 1), expert_lift], axis=1)
-    abreast = D // (ADAPTERS * adapter_cols)
-    pair_rows = 2 * RANK // abreast
-    pairs_own = (
-        pairs_own.reshape(EXP_DEV, 2 // abreast, abreast, ADAPTERS, RANK, adapter_cols)
-        .transpose(0, 1, 4, 2, 3, 5)
-        .reshape(EXP_DEV, pair_rows, D)
-    )
-    expert_rows = jnp.concatenate([expert_input, pairs_own], axis=1)
-    matrix_out = lax.all_gather(expert_output, "dp", axis=1, tiled=True)
-
-    qkv_blocks = (
-        qkv_weight.reshape(share, 3, parts, width).transpose(2, 0, 1, 3).reshape(parts * share, 3 * width)
-    )
+    pairs = jnp.stack([expert_down.transpose(0, 2, 3, 1), expert_lift])
+    pairs = pairs.transpose(2, 0, 1, 3, 4).reshape(ADAPTERS, 2 * EXP_DEV * RANK * adapter_cols)
+    pairs = dot_plain(hot.astype(low), pairs).astype(low)
+    pairs = lax.all_to_all(
+        pairs.reshape(groups, 2 * EXP_DEV * RANK, adapter_cols), "dp", split_axis=0, concat_axis=0, tiled=True
+    )
+    pairs = pairs.reshape(groups, 2, EXP_DEV * RANK, adapter_cols).transpose(1, 2, 0, 3)
+    pairs = pairs.reshape(2, EXP_DEV * RANK, D)
+    pairs = jnp.pad(pairs, ((0, 0), (0, LANES - EXP_DEV * RANK), (0, 0)))
 
     def columns(array, upto):
         return jnp.pad(array, ((0, share - array.shape[0]), (0, upto - array.shape[1])))
 
-    own_hot = (jnp.arange(ADAPTERS, dtype=jnp.int32) == adapter).astype(low)
-    small = jnp.concatenate(
+    adapters = jnp.concatenate(
         [
             adapter_down.reshape(share, ADAPTERS * 3 * RANK),
             adapter_out.reshape(ADAPTERS * RANK, share).T,
-            columns(router_weight, 32),
-            columns(adapter_router, 32),
-            columns(norm_gains.T, 8),
-            columns(jnp.broadcast_to(own_hot, (share, ADAPTERS)), 56),
             adapter_qkv.reshape(ADAPTERS * RANK, 3, share).transpose(2, 1, 0).reshape(share, 3 * LANES),
         ],
         axis=1,
     )
-    dense_line, out_line = gather_weights(qkv_blocks, out_weight, small, 0)
-    dense_line, out_line, expert_rows, matrix_out = lax.optimization_barrier(
-        (dense_line, out_line, expert_rows, matrix_out)
+    row = jnp.arange(LANES, dtype=jnp.int32)[None, :]
+    ids = group_ids[:, None]
+    wanted = jnp.where(
+        row < 48,
+        ids * 48 + row,
+        jnp.where(
+            row < 64,
+            384 + ids * RANK + row - 48,
+            jnp.where(row < 112, 512 + LANES * ((row - 64) // RANK) + ids * RANK + (row - 64) % RANK, -1),
+        ),
+    ).reshape(1, groups * LANES)
+    chosen = jnp.arange(adapters.shape[1], dtype=jnp.int32)[:, None] == wanted
+    chosen = dot_plain(adapters, chosen.astype(low)).astype(low)
+
+    qkv_blocks = (
+        qkv_weight.reshape(share, 3, parts, width).transpose(2, 0, 1, 3).reshape(parts * share, 3 * width)
+    )
+    small = jnp.concatenate(
+        [columns(router_weight, 32), columns(adapter_router, 32), columns(norm_gains.T, 64)], axis=1
+    )
+    dense_line, out_line, chosen_line = gather_weights(qkv_blocks, out_weight, small, chosen, 0)
+    chosen_all = lax.all_to_all(
+        chosen_line.reshape(parts * share, groups, LANES).transpose(1, 0, 2),
+        "dp",
+        split_axis=0,
+        concat_axis=0,
+        tiled=True,
+    ).reshape(D, LANES)
+    dense_line, out_line, expert_input, matrix_out, chosen_all, pairs = lax.optimization_barrier(
+        (dense_line, out_line, expert_input, matrix_out, chosen_all, pairs)
     )
     dense_all = lax.all_gather(dense_line, "dp", axis=0, tiled=True)
     (tokens_all,) = line_gather([tokens], 1, 2)
     out_matrix = lax.all_gather(out_line, "dp", axis=0, tiled=True)
-    matrix_in = lax.all_gather(expert_rows, "dp", axis=1, tiled=True).reshape(EXP_DEV, groups, -1, D)
-    qkv_matrix = dense_all[:, : 3 * width]
+    matrix_in = lax.all_gather(expert_input, "dp", axis=1, tiled=True)
     small_at = 3 * width
 
-    row = jnp.arange(160, dtype=jnp.int32)[:, None]
-    at = jnp.arange(SMALL, dtype=jnp.int32)[None, :]
-    wanted = jnp.where(
-        row < 48,
-        adapter * 48 + row,
-        jnp.where(
-            row < 64,
-            384 + adapter * RANK + row - 48,
-            jnp.where(
-                row < 112,
-                640 + LANES * ((row - 64) // RANK) + adapter * RANK + (row - 64) % RANK,
-                jnp.where(row < 120, 576 + row - 112, 512 + row - 120),
-            ),
-        ),
-    )
-    picked = pick_rows((at == wanted).astype(low), dense_all, small_at)
-    gain_rows = picked[112:114]
-    picked = picked.astype(low)
+    picked, router_rows, gain_rows = pick_rows(chosen_all, dense_all, small_at, experts)
     down_query, down_mix, down_route = picked[:16], picked[16:32], picked[32:48]
     lift_mix = picked[48:64]
-    router_rows = picked[120 : 120 + experts]
     lift_query = (
         picked[64:112].reshape(3, RANK, ways, share).transpose(1, 2, 0, 3).reshape(RANK, 3, parts, width)
     )
     lift_query = lax.dynamic_index_in_dim(lift_query, me, 2, keepdims=False).reshape(RANK, 3 * width)
-    by_owner = dense_all[:, small_at + 512 : small_at + 512 + LANES].reshape(ways, share, LANES)
+    by_owner = dense_all[:, small_at : small_at + LANES].reshape(ways, share, LANES)
     lift_route = lax.dynamic_slice_in_dim(
         by_owner[:, :route_rows, 32 : 32 + experts].reshape(ADAPTERS * RANK, experts),
         adapter * RANK,
         RANK,
         0,
     )
-    group_hot = by_owner.reshape(groups, parts, share, LANES)[:, 0, 0, 72 : 72 + ADAPTERS].astype(
-        jnp.float32
-    )
+    lift_route = jnp.pad(lift_route, ((0, 0), (0, LANES - experts)))
+    routed = jnp.any(routes[:, :, None] == jnp.arange(LANES, dtype=jnp.int32), axis=1).astype(jnp.float32)
     def shifted(array, by):
         return lax.ppermute(array, "expert", [(i, (i + by) % parts) for i in range(parts)])
 
@@ -1006,29 +1243,27 @@
     early_shifts, late_shifts = [1], list(range(2, parts))
     moved = {s: shifted(early, s) for s in early_shifts}
 
-    inputs_all = tokens_all.astype(jnp.float32)
-    normed_low = (inputs_all * norm_inverse(inputs_all) * gain_rows[0:1]).astype(low)
-    rank_query = dot_right(normed_low, down_query).astype(low)
-    qkv_low = (dot_plain(normed_low, qkv_matrix) + dot_plain(rank_query, lift_query)).astype(low)
+    normed_low, rank_query, qkv_low = project_qkv(
+        tokens_all, gain_rows[0:1], down_query, lift_query, dense_all
+    )
     segments = segments_of(cont_lengths[0], jnp.arange(total, dtype=jnp.int32))
     segment_column, segment_row = segments[:, None], segments[None, :]
     mixed_heads, log_mass = run_attention(segment_column, segment_row, qkv_low)
     (mixed_low,) = exchange([mixed_heads], 3)
 
-    inputs = tokens.astype(jnp.float32)
-    upstream = cotangent.astype(jnp.float32)
-    rank_mix = dot_right(mixed_low, down_mix).astype(low)
-    middle = inputs + dot_plain(mixed_low, out_matrix) + dot_plain(rank_mix, lift_mix)
-    inverse_second = norm_inverse(middle)
-    second_low = (middle * inverse_second * gain_rows[1:2]).astype(low)
-    rank_route = dot_right(second_low, down_route).astype(low)
-    logits = dot_right(second_low, router_rows) + dot_plain(rank_route, lift_route)
-    logit_exp = jnp.exp(logits - jnp.max(logits, axis=-1, keepdims=True))
-    router_probs = logit_exp / jnp.sum(logit_exp, axis=-1, keepdims=True)
-    expert_ids = jnp.arange(experts, dtype=jnp.int32)
-    routed = jnp.any(routes[:, :, None] == expert_ids[None, None, :], axis=1)
-    gates = jnp.where(routed, router_probs, 0.0).astype(low)
-    gates = jnp.pad(gates, ((0, 0), (0, LANES - experts)))
+    middle, rank_mix, inverse_second, second_low, rank_route, router_probs, gates = finish_attention(
+        experts,
+        mixed_low,
+        tokens,
+        down_mix,
+        lift_mix,
+        gain_rows[1:2],
+        down_route,
+        router_rows,
+        lift_route,
+        routed,
+        out_matrix,
+    )
     held = lax.optimization_barrier([second_low] + [moved[s] for s in early_shifts])
     second_low = held[0]
     moved.update(zip(early_shifts, held[1:]))
@@ -1037,21 +1272,6 @@
     late, second_all = lax.optimization_barrier((cotangent, second_all))
     moved.update({s: shifted(late, s) for s in late_shifts})
     cotangents = [cotangent] + [moved[s] for s in range(1, parts)]
-    pairs = jnp.stack(
-        [
-            lax.dynamic_slice_in_dim(
-                matrix_in[:, :, matrix_in.shape[2] - pair_rows :],
-                (beside * ADAPTERS + adapter) * adapter_cols,
-                adapter_cols,
-                3,
-            ).reshape(EXP_DEV, groups, 2 // abreast, RANK, adapter_cols)
-            for beside in range(abreast)
-        ],
-        axis=3,
-    )
-    pairs = pairs.reshape(EXP_DEV, groups, 2, RANK, adapter_cols).transpose(2, 0, 3, 1, 4)
-    pairs = pairs.reshape(2, EXP_DEV * RANK, D)
-    pairs = jnp.pad(pairs, ((0, 0), (0, LANES - EXP_DEV * RANK), (0, 0)))
     output_terms, ranks, gate, up = experts_forward(
         second_all, gates_all, pairs[0], pairs[1], matrix_in, matrix_out
     )
@@ -1060,6 +1280,7 @@
         cotangents, gates_all, ranks, pairs[0], pairs[1], matrix_in, matrix_out, gate, up
     )
     slot_sum = line_reduce(slot_terms, 5, 2)
+    slot_sum, output_sum = lax.optimization_barrier((slot_sum, output_sum))
 
     lift_sent = jnp.concatenate([lift_gate_grad, lift_up_grad], axis=2).reshape(EXP_DEV * RANK, D)
     down_sent = dot_left(rank_expert_grad[:, : EXP_DEV * RANK], second_all)
@@ -1076,23 +1297,24 @@
     explift_grad = by_adapter[:, 0].transpose(1, 0, 2, 3)
     expdown_grad = by_adapter[:, 1].transpose(1, 3, 0, 2)
 
-    prob_grad = slot_sum[:, D : D + experts] + slot_sum[:, D + 64 : D + 64 + experts]
-    prob_grad = jnp.where(routed, prob_grad, 0.0)
-    logit_grad = (
-        router_probs * (prob_grad - jnp.sum(router_probs * prob_grad, axis=1, keepdims=True))
-    ).astype(low)
-    rank_route_grad = dot_right(logit_grad, lift_route).astype(low)
-    second_grad = (
-        slot_sum[:, :D] + dot_plain(logit_grad, router_rows) + dot_plain(rank_route_grad, down_route)
-    )
-    middle_grad = upstream + norm_backward(middle, inverse_second, gain_rows[1:2], second_grad)
-    branch_grad = middle_grad.astype(low)
-    rank_mix_grad = dot_right(branch_grad, lift_mix).astype(low)
-    mixed_grad = (dot_right(branch_grad, out_matrix) + dot_plain(rank_mix_grad, down_mix)).astype(low)
-
-    (mixed_back,) = exchange(
-        [mixed_grad.reshape(piece, parts, width).transpose(1, 0, 2).reshape(total, width)], 6, stack=True
-    )
+    mixed_grad, middle_grad, branch_grad, logit_grad, rank_route_grad, rank_mix_grad = middle_backward(
+        width,
+        slot_sum,
+        router_probs,
+        routed,
+        middle,
+        inverse_second,
+        cotangent,
+        gain_rows[1:2],
+        router_rows,
+        lift_route,
+        down_route,
+        lift_mix,
+        down_mix,
+        out_matrix,
+    )
+
+    (mixed_back,) = exchange([mixed_grad], 6, stack=True)
     back_query, back_key, back_value = run_attention_back(
         segment_column, segment_row, qkv_low, mixed_back, log_mass
     )
@@ -1116,12 +1338,14 @@
         [
             downs.reshape(4 * RANK, ways, share).transpose(1, 0, 2).reshape(ways, -1),
             lift_query_grad.reshape(RANK, ways, 3 * share).transpose(1, 0, 2).reshape(ways, -1),
-            jnp.broadcast_to(dot_left(rank_route, logit_grad).reshape(1, -1), (ways, RANK * experts)),
+            jnp.broadcast_to(dot_left(rank_route, logit_grad)[:, :experts].reshape(1, -1), (ways, RANK * experts)),
         ],
         axis=1,
     ).astype(low)
+    first_terms, output_sum = lax.optimization_barrier((first_terms, output_sum))
     first_grad = lax.psum_scatter(first_terms, "expert", scatter_dimension=0, tiled=True).astype(jnp.float32)
     got = lax.all_to_all(owned, ("dp", "expert"), split_axis=0, concat_axis=0, tiled=True)
+    inputs = tokens.astype(jnp.float32)
     inverse_first = norm_inverse(inputs)
     input_grad = (
         middle_grad + norm_backward(inputs, inverse_first, gain_rows[0:1], first_grad)

time: 901 us -> 868 us (0.963)
  matrix products: 63 us -> 17.8 us
  Pallas kernels: 612 us -> 650 us
  local copies, waits for them, and re-layouts: 57.5 us -> 36.3 us
  other arithmetic: 36.7 us -> 16.9 us
  starting transfers between devices: 15.6 us -> 27.5 us
    pallas_call x1 -> x4, Pallas kernels: 5.75 us -> 45.3 us  [the longest x1 17.7 us: project_qkv(): pl.pallas_call(qkv_kernel, grid=(3,), in_specs=[VMEM, VMEM, VMEM, pl.Bloc...]
    dot_general x8 -> x2, matrix products: 30.1 us -> 1.81 us  [dot_plain(): return jnp.dot(left, right, preferred_element_type=jnp.float32)]
    reduce_scatter x1, waiting for transfers between devices: 10.3 us -> 37.6 us  [body(): lax.psum_scatter(first_terms, 'expert', scatter_dimension=0, tiled=True)]
    all_gather x1, waiting for transfers between devices: 20.9 us -> 0.01 us  [body(): matrix_in = lax.all_gather(expert_input, 'dp', axis=1, tiled=True)]
    all_gather x1, waiting for transfers between devices: 38.4 us -> 19.5 us  [body(): matrix_out = lax.all_gather(expert_output, 'dp', axis=1, tiled=True)]
    dot_general x8 -> x1, matrix products: 16.9 us -> 1.15 us  [dot_right(): lax.dot_general(left, right, (((1,), (1,)), ((), ())), preferred_element_...]
    all_to_all x0 -> x2, waiting for transfers between devices: none -> 11.3 us  [the longest x1 11.3 us: body(): lax.all_to_all(chosen_line.reshape(parts * share, groups, LANES).transpos...]
    all_to_all x0 -> x2, starting transfers between devices: none -> 11.2 us  [the longest x1 5.71 us: body(): lax.all_to_all(pairs.reshape(groups, 2 * EXP_DEV * RANK, adapter_cols), '...]
  transfers between devices with their start and end apart: 11 -> 13, of which waited for: 4 -> 4; matrix products, arithmetic and copies ran while one was open for 15% -> 6% of each run, Pallas kernels for 62% -> 67%
where the time goes in v4:
time: 868 us; the launch traced here: 863 us
  Pallas kernels  650 us (75%)
  waiting for transfers between devices  91.9 us (11%)
  local copies, waits for them, and re-layouts  36.3 us (4%)
  starting transfers between devices  27.5 us (3%)
  matrix products  17.8 us (2%)
  other arithmetic  16.9 us (2%)
  between operations  16.1 us (2%)
    pallas_call x2, Pallas kernels, line_gather(): pl.pallas_call(functools.partial(gather_kernel, parts, pieces, n), out_sh...  177 us
    pallas_call x1, Pallas kernels, experts_backward(): pl.pallas_call(functools.partial(backward_kernel, parts), grid=(EXP_DEV,...  99.5 us
    pallas_call x1, Pallas kernels, line_reduce(): pl.pallas_call(functools.partial(reduce_kernel, parts, pieces), out_shape...  92.7 us
    pallas_call x1, Pallas kernels, experts_forward(): pl.pallas_call(forward_kernel, grid=(EXP_DEV, FF // TILE), in_specs=[VMEM...  87.1 us
    pallas_call x2, Pallas kernels, exchange(): pl.pallas_call(functools.partial(exchange_kernel, parts, n, stack), out_s...  58.7 us
    pallas_call x1, Pallas kernels, gather_weights(): pl.pallas_call(functools.partial(weights_kernel, parts), out_shape=[jax.S...  43.5 us
    reduce_scatter x1, waiting for transfers between devices, body(): lax.psum_scatter(first_terms, 'expert', scatter_dimension=0, tiled=True)  37.6 us
    all_to_all x1, waiting for transfers between devices, body(): lax.all_to_all(owned, ('dp', 'expert'), split_axis=0, concat_axis=0, tile...  21.5 us
  transfers between devices with their start and end apart: 13, of which 4 were waited for; matrix products, arithmetic and copies ran while one was open for 6% of the time, Pallas kernels for 67%

profile of v4, /device:TPU:9, one launch (start us, length us, event | category | flops | bytes accessed | tf_op | source)
XLA Modules:
  0.0 862.7 jit_solution(12786808656111207857)
XLA Ops:
  10.6 6.5 all-reduce.5
  19.7 5.7 all-to-all-start.1
  30.2 43.5 %gather_weights.1 = (bf16[256,1664]{1,0:T(8,128)(2,1)}, bf16[256,2048]{1,0:T(8,128)(2,1)}, bf16[256,1024]{1,0:T(8,128)(2,1)}) custom-call(bf16[256,1536]{1,0:T(8,128)(2,1)} %bitcast.104, bf16[64,2048]{1,0:T(8,128)(2,1)} %out.1, bf16[64,128]{1,0:T(8,128)(2,1)} %fusion.24.small, bf16[64,1024]{1,0:T(8,128)(2,1)} %fusion.9.chosen), custom_call_target="tpu_custom_call" | custom-call | bytes 133038080 | tf_op jit(solution)/shard_map/gather_weights/pallas_call | solution.py:425
  75.7 5.5 all-to-all-start
  81.8 11.3 %all-to-all-done = bf16[8,256,128]{2,1,0:T(8,128)(2,1)S(1)} async-done(((bf16[8,256,128]{2,1,0:T(8,128)(2,1)}), bf16[8,256,128]{2,1,0:T(8,128)(2,1)S(1)}, u32[]{:S(2)}, u32[]{:S(2)}) %all-to-all-start) | async-done | bytes 524320 | tf_op jit(solution)/shard_map/all_to_all | solution.py:1207
  93.1 19.5 %all-gather.5.cloned.1.call-done.out_ref = bf16[4,1024,2048]{2,1,0:T(8,128)(2,1)} async-done(((bf16[4,128,2048]{2,1,0:T(8,128)(2,1)}), bf16[4,1024,2048]{2,1,0:T(8,128)(2,1)}) %all-gather.5.cloned.1.call-update) | async-done | bytes 16777232 | tf_op jit(solution)/shard_map/all_gather | solution.py:1159
  114.0 85.9 %line_gather_1.1.tokens_ref = bf16[1280,2048]{1,0:T(8,128)(2,1)} custom-call(bf16[320,2048]{1,0:T(8,128)(2,1)} %tokens_ref.1), custom_call_target="tpu_custom_call" | custom-call | bytes 367001600 | tf_op jit(solution)/shard_map/line_gather_1/pallas_call | solution.py:147
  213.2 17.7 %project_qkv.1 = (bf16[1280,2048]{1,0:T(8,128)(2,1)}, bf16[1280,16]{1,0:T(8,128)(2,1)}, bf16[1280,1536]{1,0:T(8,128)(2,1)}) custom-call(bf16[1280,2048]{1,0:T(8,128)(2,1)} %line_gather_1.1.tokens_ref, f32[1,2048]{1,0:T(1,128)} %get-tuple-element.125.gain_ref, bf16[16,2048]{1,0:T(8,128)(2,1)} %get-tuple-element.123.down_ref, bf16[16,1536]{1,0:T(8,128)(2,1)} %bitcast.128, ...), custom_call_target="tpu_custom_call" | custom-call | flops 8053063680 | bytes 27262976 | tf_op jit(solution)/shard_map/project_qkv/pallas_call | solution.py:906
  231.0 14.3 %attention.1 = (bf16[1280,512]{1,0:T(8,128)(2,1)S(1)}, f32[4,1280,1]{2,1,0:T(8,128)S(1)}) custom-call(s32[1280,1]{1,0:T(8,128)S(1)} %reshape_select_fusion.column_ref, s32[1,1280]{1,0:T(1,128)S(1)} %compare_select_fusion.row_ref, bf16[1280,1536]{1,0:T(8,128)(2,1)} %get-tuple-element.69.query_ref.key_ref.value_ref, ...), custom_call_target="tpu_custom_call" | custom-call | flops 2516582400 | bytes 5242880 | tf_op jit(solution)/shard_map/attention/pallas_call | solution.py:485
  247.8 30.8 %exchange_3.1.mixed_ref = bf16[320,2048]{1,0:T(8,128)(2,1)} custom-call(bf16[1280,512]{1,0:T(8,128)(2,1)} %copy-done.2), custom_call_target="tpu_custom_call" | custom-call | bytes 91750400 | tf_op jit(solution)/shard_map/exchange_3/pallas_call | solution.py:212
  279.3 12.4 %finish_attention.1 = (f32[320,2048]{1,0:T(8,128)}, bf16[320,16]{1,0:T(8,128)(2,1)}, f32[320,1]{1,0:T(8,128)}, bf16[320,2048]{1,0:T(8,128)(2,1)}, bf16[320,16]{1...) custom-call(bf16[320,2048]{1,0:T(8,128)(2,1)} %exchange_3.1.mixed_ref, bf16[320,2048]{1,0:T(8,128)(2,1)} %tokens_ref.1, ...), custom_call_target="tpu_custom_call" | custom-call | flops 2684354560 | bytes 16252928 | tf_op jit(solution)/shard_map/finish_attention/pallas_call | solution.py:986
  291.7 90.9 %line_gather_4.1 = (bf16[1280,2048]{1,0:T(8,128)(2,1)}, bf16[1280,128]{1,0:T(8,128)(2,1)}) custom-call(bf16[320,2048]{1,0:T(8,128)(2,1)} %get-tuple-element.76.refs_0_, bf16[320,128]{1,0:T(8,128)(2,1)} %get-tuple-element.77.refs_1_), custom_call_target="tpu_custom_call" | custom-call | bytes 389939200 | tf_op jit(solution)/shard_map/line_gather_4/pallas_call | solution.py:147
  385.3 87.1 %experts_forward.1 = (bf16[1280,2048]{1,0:T(8,128)(2,1)}, bf16[1280,128]{1,0:T(8,128)(2,1)}, bf16[4,1280,1024]{2,1,0:T(8,128)(2,1)}, bf16[4,1280,1024]{2,1,0:T(8,128)(2,1)}) custom-call(bf16[1280,2048]{1,0:T(8,128)(2,1)} %get-tuple-element.80.rows_ref, bf16[1280,128]{1,0:T(8,128)(2,1)} %get-tuple-element.78.gates_ref, ...), custom_call_target="tpu_custom_call" | custom-call | flops 107374182400 | bytes 71303168 | tf_op jit(solution)/shard_map/experts_forward/pallas_call | solution.py:655
  473.7 99.5 %experts_backward.1 = (bf16[1280,2176]{1,0:T(8,128)(2,1)}, bf16[1280,128]{1,0:T(8,128)(2,1)}, f32[4,16,1024]{2,1,0:T(8,128)}, f32[4,16,1024]{2,1,0:T(8,128)}) custom-call(bf16[1280,128]{1,0:T(8,128)(2,1)} %get-tuple-element.78.gates_ref, bf16[1280,128]{1,0:T(8,128)(2,1)} %get-tuple-element.84.ranks_ref, bf16[128,2048]{1,0:T(8,128)(2,1)} %get-tuple-element.119.down_ref, ...), custom_call_target="tpu_custom_call" | custom-call | flops 128849018880 | bytes 71303168 | tf_op jit(solution)/shard_map/experts_backward/pallas_call | solution.py:788
  573.2 92.7 %line_reduce_5.1.slot_ref = f32[320,2176]{1,0:T(8,128)S(1)} custom-call(bf16[1280,2176]{1,0:T(8,128)(2,1)} %get-tuple-element.89.src), custom_call_target="tpu_custom_call" | custom-call | bytes 389939200 | tf_op jit(solution)/shard_map/line_reduce_5/pallas_call | solution.py:314
  667.6 12.5 %middle_backward.1 = (bf16[1280,512]{1,0:T(8,128)(2,1)}, f32[320,2048]{1,0:T(8,128)}, bf16[320,2048]{1,0:T(8,128)(2,1)}, bf16[320,128]{1,0:T(8,128)(2,1)}, bf16[...) custom-call(f32[320,2176]{1,0:T(8,128)} %copy-done, f32[320,128]{1,0:T(8,128)} %get-tuple-element.92.probs_ref, ...), custom_call_target="tpu_custom_call" | custom-call | flops 2684354560 | bytes 24117248 | tf_op jit(solution)/shard_map/middle_backward/pallas_call | solution.py:1075
  680.1 27.9 %exchange_6.1.grad_ref = bf16[1280,512]{1,0:T(8,128)(2,1)} custom-call(bf16[1280,512]{1,0:T(8,128)(2,1)} %get-tuple-element.94.refs_0_), custom_call_target="tpu_custom_call" | custom-call | bytes 91750400 | tf_op jit(solution)/shard_map/exchange_6/pallas_call | solution.py:212
  709.3 19.0 %attention_back.1 = (bf16[1280,512]{1,0:T(8,128)(2,1)S(1)}, bf16[1280,512]{1,0:T(8,128)(2,1)S(1)}, bf16[1280,512]{1,0:T(8,128)(2,1)S(1)}) custom-call(s32[1280,1]{1,0:T(8,128)S(1)} %reshape_select_fusion.column_ref, s32[1,1280]{1,0:T(1,128)S(1)} %compare_select_fusion.row_ref, bf16[1280,1536]{1,0:T(8,128)(2,1)} %get-tuple-element.69.query_ref.key_ref.value_ref, ...), custom_call_target="tpu_custom_call" | custom-call | flops 6710886400 | bytes 10485760 | tf_op jit(solution)/shard_map/attention_back/pallas_call | solution.py:536
  731.1 12.9 %first_products.1 = bf16[1280,2048]{1,0:T(8,128)(2,1)} custom-call(bf16[1280,512]{1,0:T(8,128)(2,1)S(1)} %get-tuple-element.96.query_ref, bf16[1280,512]{1,0:T(8,128)(2,1)S(1)} %get-tuple-element.97.key_ref, bf16[1280,512]{1,0:T(8,128)(2,1)S(1)} %get-tuple-element.98.value_ref, bf16[1280,16]{1,0:T(8,128)(2,1)S(1)} %convolution_convert_fusion.1.rank_ref, ...), custom_call_target="tpu_custom_call" | custom-call | flops 8053063680 | bytes 11534336 | tf_op jit(solution)/shard_map/first_products/pallas_call | solution.py:863
  749.7 5.5 all-to-all-start.3
  773.3 6.3 all-to-all-start.2
  783.5 21.5 %all-to-all-done.2 = bf16[32,2,3712]{2,1,0:T(2,128)(2,1)S(1)} async-done(((bf16[32,2,3712]{2,1,0:T(2,128)(2,1)}), bf16[32,2,3712]{2,1,0:T(2,128)(2,1)S(1)}, u32[]{:S(2)}, u32[]{:S(2)}) %all-to-all-start.2) | async-done | bytes 475168 | tf_op jit(solution)/shard_map/all_to_all | solution.py:1347
  812.1 37.6 %reduce-scatter.5.cloned.1.call-done = bf16[320,2048]{1,0:T(8,128)(2,1)} async-done(((bf16[1280,2048]{1,0:T(8,128)(2,1)}), bf16[320,2048]{1,0:T(8,128)(2,1)}) %reduce-scatter.5.cloned.1.call-update) | async-done | bytes 1310736 | tf_op jit(solution)/shard_map/reduce_scatter | solution.py:1346
  851.8 3.6 fusion.5
  (202 shorter events, 76.5 us)
Async XLA Ops:
  7.2 105.5 %all-gather.5.cloned.1.call-start = ((), (), s32[]{:S(2)}) async-start(), calls=%async_computation.6 | async-start | bytes 18874368 | tf_op jit(solution)/shard_map/all_gather | solution.py:1159
  17.0 11.7 %copy-start.26 = (s32[8]{0:T(128)}, s32[8]{0:T(128)S(1)}, u32[]{:S(2)}) copy-start(s32[8]{0:T(128)S(1)} %all-reduce.5) | copy-start | bytes 100
  19.7 55.9 %all-to-all-start.1 = ((bf16[8,128,256]{2,1,0:T(8,128)(2,1)}), bf16[8,128,256]{2,1,0:T(8,128)(2,1)S(1)}, u32[]{:S(2)}, u32[]{:S(2)}) async-start(bf16[8,128,256]{2,1,0:T(8,128)(2,1)} %copy.100), calls=%async_computation.1 | async-start | bytes 1048576 | tf_op jit(solution)/shard_map/all_to_all | solution.py:1168
  75.7 17.5 %all-to-all-start = ((bf16[8,256,128]{2,1,0:T(8,128)(2,1)}), bf16[8,256,128]{2,1,0:T(8,128)(2,1)S(1)}, u32[]{:S(2)}, u32[]{:S(2)}) async-start(bf16[8,256,128]{2,1,0:T(8,128)(2,1)} %bitcast_bitcast_fusion), calls=%async_computation | async-start | bytes 1048576 | tf_op jit(solution)/shard_map/all_to_all | solution.py:1207
  81.2 124.2 %all-gather.7.cloned.1.call-start = ((), (), s32[]{:S(2)}) async-start(), calls=%async_computation.7 | async-start | bytes 7667712 | tf_op jit(solution)/shard_map/all_gather | solution.py:1217
  93.1 20.8 %copy-start.11 = (bf16[8,256,128]{2,1,0:T(8,128)(2,1)}, bf16[8,256,128]{2,1,0:T(8,128)(2,1)S(1)}, u32[]{:S(2)}) copy-start(bf16[8,256,128]{2,1,0:T(8,128)(2,1)S(1)} %all-to-all-done) | copy-start | bytes 1572868
  112.6 166.6 %all-gather.9.cloned.1.call-start = ((), (), s32[]{:S(2)}) async-start(), calls=%async_computation.8 | async-start | bytes 9437184 | tf_op jit(solution)/shard_map/all_gather | solution.py:1219
  113.4 272.0 %all-gather.11.cloned.1.call-start = ((), (), s32[]{:S(2)}) async-start(), calls=%async_computation.9 | async-start | bytes 37748736 | tf_op jit(solution)/shard_map/all_gather | solution.py:1220
  114.0 86.0 %copy-start.12 = (bf16[320,2048]{1,0:T(8,128)(2,1)S(1)}, bf16[320,2048]{1,0:T(8,128)(2,1)}, u32[]{:S(2)}) copy-start(bf16[320,2048]{1,0:T(8,128)(2,1)} %cotangent_ref.1) | copy-start | bytes 3932164
  114.0 87.5 %copy-start.25 = (s32[320,8]{0,1:T(8,128)S(1)}, s32[320,8]{0,1:T(8,128)}, u32[]{:S(2)}) copy-start(s32[320,8]{0,1:T(8,128)} %param.31) | copy-start | bytes 30724
  114.0 90.0 %copy-start.35 = (s32[1,8]{1,0:T(1,128)S(1)}, s32[1,8]{1,0:T(1,128)}, u32[]{:S(2)}) copy-start(s32[1,8]{1,0:T(1,128)} %param.33) | copy-start | bytes 100
  114.0 553.6 %reduce-scatter.3.cloned.1.call-start = ((), (), s32[]{:S(2)}) async-start(), calls=%async_computation.10 | async-start | bytes 6553600 | tf_op jit(solution)/shard_map/reduce_scatter | solution.py:1278
  200.0 91.7 %collective-permute-start = (bf16[320,2048]{1,0:T(8,128)(2,1)S(1)}, bf16[320,2048]{1,0:T(8,128)(2,1)}, u32[]{:S(2)}, u32[]{:S(2)}) collective-permute-start(bf16[320,2048]{1,0:T(8,128)(2,1)S(1)} %copy-done.12), channel_id=1, source_target_pairs={{0,1},{1,2},{2,3},{3,0},{4,5},{5,6},{6,7},{7,4},{8,9},{9,10},{10,1... | collective-permute-start | bytes 3932168 | tf_op jit(solution)/shard_map/ppermute | solution.py:1240
  247.8 30.8 %slice-start = ((bf16[2048,1664]{1,0:T(8,128)(2,1)}), bf16[2048,128]{1,0:T(8,128)(2,1)S(1)}, s32[]{:S(2)}) async-start(bf16[2048,1664]{1,0:T(8,128)(2,1)} %all-gather.7.cloned.1.call-done.small_ref.weight_ref.refs_0_.refs_1_.refs_2_), calls=%async_computation.12 | async-start | bytes 1048576 | tf_op jit(solution)/shard_map/slice | solution.py:1230
  382.6 90.1 %collective-permute-start.1 = (bf16[320,2048]{1,0:T(8,128)(2,1)S(1)}, bf16[320,2048]{1,0:T(8,128)(2,1)S(1)}, u32[]{:S(2)}, u32[]{:S(2)}) collective-permute-start(bf16[320,2048]{1,0:T(8,128)(2,1)S(1)} %copy-done.12), channel_id=1, source_target_pairs={{0,2},{1,3},{2,0},{3,1},{4,6},{5,7},{6,4},{7,5},{8,10},{9,11},{10,... | collective-permute-start | bytes 3932168 | tf_op jit(solution)/shard_map/ppermute | solution.py:1240
  384.9 87.8 %collective-permute-start.2 = (bf16[320,2048]{1,0:T(8,128)(2,1)S(1)}, bf16[320,2048]{1,0:T(8,128)(2,1)}, u32[]{:S(2)}, u32[]{:S(2)}) collective-permute-start(bf16[320,2048]{1,0:T(8,128)(2,1)S(1)} %copy-done.12), channel_id=1, source_target_pairs={{0,3},{1,0},{2,1},{3,2},{4,7},{5,4},{6,5},{7,6},{8,11},{9,8},{10,9... | collective-permute-start | bytes 3932168 | tf_op jit(solution)/shard_map/ppermute | solution.py:1240
  472.4 377.2 %reduce-scatter.5.cloned.1.call-start = ((), (), s32[]{:S(2)}) async-start(), calls=%async_computation.11 | async-start | bytes 6553600 | tf_op jit(solution)/shard_map/reduce_scatter | solution.py:1346
  748.8 10.7 %copy-start.9 = (bf16[320,2048]{1,0:T(8,128)(2,1)S(1)}, bf16[320,2048]{1,0:T(8,128)(2,1)}, u32[]{:S(2)}) copy-start(bf16[320,2048]{1,0:T(8,128)(2,1)} %get-tuple-element.76.refs_0_) | copy-start | bytes 3932164
  748.8 11.8 %copy-start.21 = (bf16[320,16]{1,0:T(8,128)(2,1)S(1)}, bf16[320,16]{1,0:T(8,128)(2,1)}, u32[]{:S(2)}) copy-start(bf16[320,16]{1,0:T(8,128)(2,1)} %get-tuple-element.106) | copy-start | bytes 30724
  749.7 23.6 %all-to-all-start.3 = ((bf16[8,128,256]{2,1,0:T(8,128)(2,1)}), bf16[8,128,256]{2,1,0:T(8,128)(2,1)S(1)}, u32[]{:S(2)}, u32[]{:S(2)}) async-start(bf16[8,128,256]{2,1,0:T(8,128)(2,1)} %maximum_bitcast_fusion.1), calls=%async_computation.5 | async-start | bytes 1048576 | tf_op jit(solution)/shard_map/all_to_all | solution.py:1293
  770.2 9.4 %copy-start.27 = (s32[8]{0:T(128)S(1)}, s32[8]{0:T(128)}, u32[]{:S(2)}) copy-start(s32[8]{0:T(128)} %copy-done.26) | copy-start | bytes 100
  773.3 31.7 %all-to-all-start.2 = ((bf16[32,2,3712]{2,1,0:T(2,128)(2,1)}), bf16[32,2,3712]{2,1,0:T(2,128)(2,1)S(1)}, u32[]{:S(2)}, u32[]{:S(2)}) async-start(bf16[32,2,3712]{2,1,0:T(2,128)(2,1)} %reshape.428), calls=%async_computation.4 | async-start | bytes 950272 | tf_op jit(solution)/shard_map/all_to_all | solution.py:1347
  808.1 41.6 %copy-start.5 = (bf16[320,2048]{1,0:T(8,128)(2,1)S(1)}, bf16[320,2048]{1,0:T(8,128)(2,1)}, u32[]{:S(2)}) copy-start(bf16[320,2048]{1,0:T(8,128)(2,1)} %tokens_ref.1) | copy-start | bytes 3932164
  808.1 41.6 %copy-start.22 = (f32[1,2048]{1,0:T(1,128)S(1)}, f32[1,2048]{1,0:T(1,128)}, u32[]{:S(2)}) copy-start(f32[1,2048]{1,0:T(1,128)} %get-tuple-element.125.gain_ref) | copy-start | bytes 24580
  (26 other events, 71.9 us)
Sparse Core Ops, SparseCore 0:
  9.9 102.6 all-gather.4
  114.5 47.7 all-gather.6
  164.2 54.3 all-gather.8
  220.4 160.8 all-gather.10
  472.6 96.4 reduce-scatter.2
  744.2 105.4 reduce-scatter.4

commit v5 on v4

--- a/solution.py
+++ b/solution.py
@@ -20,6 +20,7 @@
 BLOCK = 256
 ROWS = 1280
 TILE = 512
+HALF = EXP_DEV // 2
 SMALL = 1024
 
 MESH = pl.DeviceIdType.MESH
@@ -326,10 +327,10 @@
     )(terms)
 
 
-def weights_kernel(parts, blocks, out, small, chosen, dst, dst_out, dst_chosen, own_sem, send, recv, send_up, recv_up, send_down, recv_down):
+def weights_kernel(parts, blocks, out, small, chosen, dst, dst_chosen, own_sem, send, recv, send_up, recv_up, send_down, recv_down):
     me = lax.axis_index("expert")
     share = out.shape[0]
-    wide = blocks.shape[1]
+    left, wide = out.shape[1], blocks.shape[1]
     greet_all(me, parts)
 
     def rows(origin):
@@ -338,14 +339,14 @@
     def exchanged(k, to, origin):
         return pltpu.make_async_remote_copy(
             src_ref=blocks.at[rows(to)],
-            dst_ref=dst.at[rows(origin), :wide],
+            dst_ref=dst.at[rows(origin), left : left + wide],
             send_sem=send.at[k - 1],
             recv_sem=recv.at[k - 1],
             device_id={"expert": to},
             device_id_type=MESH,
         )
 
-    shared = ((out, dst_out, 0), (small, dst, wide), (chosen, dst_chosen, 0))
+    shared = ((out, dst, 0), (small, dst, left + wide), (chosen, dst_chosen, 0))
 
     def place(i, origin):
         src, into, at = shared[i]
@@ -386,7 +387,7 @@
                 pltpu.make_async_copy(src, target, own_sem.at[i])
                 for i, (src, target) in enumerate(
                     (
-                        (blocks.at[rows(me)], dst.at[rows(me), :wide]),
+                        (blocks.at[rows(me)], dst.at[rows(me), left : left + wide]),
                         (out, place(0, me)),
                         (small, place(1, me)),
                         (chosen, place(2, me)),
@@ -421,18 +422,17 @@
 def gather_weights(blocks, out, small, chosen, cid):
     parts = lax.axis_size("expert")
     sem = pltpu.SemaphoreType.DMA
-    rows, cols = blocks.shape[0], blocks.shape[1] + small.shape[1]
+    rows, cols = blocks.shape[0], out.shape[1] + blocks.shape[1] + small.shape[1]
     return pl.pallas_call(
         functools.partial(weights_kernel, parts),
         out_shape=[
             jax.ShapeDtypeStruct((rows, cols), blocks.dtype),
-            jax.ShapeDtypeStruct((rows, out.shape[1]), blocks.dtype),
             jax.ShapeDtypeStruct((rows, chosen.shape[1]), blocks.dtype),
         ],
         in_specs=[ANY] * 4,
-        out_specs=[ANY] * 3,
+        out_specs=[ANY] * 2,
         scratch_shapes=[sem((4,)), sem((parts - 1,)), sem((parts - 1,))] + [sem((3, parts - 1))] * 4,
-        cost_estimate=transfer_cost(rows * (cols + out.shape[1])),
+        cost_estimate=transfer_cost(rows * (cols + chosen.shape[1])),
         compiler_params=pltpu.CompilerParams(collective_id=cid, has_side_effects=True),
         name="gather_weights",
     )(blocks, out, small, chosen)
@@ -459,8 +459,37 @@
     return jnp.concatenate([ahead, own], axis=1)
 
 
-def attention_kernel(column_ref, row_ref, query_ref, key_ref, value_ref, mixed_ref, lse_ref):
+def row_block(owner, rows):
+    return pl.ds(pl.multiple_of(owner * rows, rows), rows)
+
+
+def attention_kernel(
+    parts, column_ref, row_ref, query_ref, key_ref, value_ref, mixed_ref, lse_ref, heads_out, own_sem, send, recv
+):
+    head, heads = pl.program_id(0), pl.num_programs(0)
+    me = lax.axis_index("expert")
     total = query_ref.shape[0]
+    piece = total // parts
+
+    @pl.when(head == 0)
+    def _():
+        greet_all(me, parts)
+
+    def moved(h, k, origin, to):
+        lanes = pl.ds(pl.multiple_of((origin * heads + h) * HEAD, HEAD), HEAD)
+        return pltpu.make_async_remote_copy(
+            src_ref=heads_out.at[h, row_block(to, piece)],
+            dst_ref=mixed_ref.at[:, lanes],
+            send_sem=send.at[h, k - 1],
+            recv_sem=recv.at[h, k - 1],
+            device_id={"expert": to},
+            device_id_type=MESH,
+        )
+
+    def kept(h):
+        lanes = pl.ds(pl.multiple_of((me * heads + h) * HEAD, HEAD), HEAD)
+        return pltpu.make_async_copy(heads_out.at[h, row_block(me, piece)], mixed_ref.at[:, lanes], own_sem.at[h])
+
     for block in range(total // BLOCK):
         here = pl.ds(block * BLOCK, BLOCK)
         scores = masked_scores(query_ref[here, :], key_ref, column_ref, row_ref, block)
@@ -469,8 +498,21 @@
         mass = jnp.sum(expd, axis=1, keepdims=True)
         probs = (expd / mass).astype(jnp.bfloat16)
         mixed = dot_plain(probs, value_ref[: (block + 1) * BLOCK, :])
-        mixed_ref[here, :] = mixed.astype(jnp.bfloat16)
+        heads_out[head, here, :] = mixed.astype(jnp.bfloat16)
         lse_ref[0, here, :] = top + jnp.log(mass)
+
+    kept(head).start()
+    for k in range(parts - 1, 0, -1):
+        moved(head, k, me, lax.rem(me + k, parts)).start()
+
+    @pl.when(head == heads - 1)
+    def _():
+        @pl.loop(0, heads)
+        def _(h):
+            kept(h).wait()
+            for k in range(parts - 1, 0, -1):
+                moved(h, k, me, lax.rem(me + k, parts)).wait_send()
+                moved(h, k, lax.rem(me + parts - k, parts), me).wait_recv()
 
 
 def head_specs(total, heads):
@@ -479,44 +521,100 @@
     ]
 
 
-def run_attention(column, row, qkv):
+def run_attention(column, row, qkv, cid):
     total, heads = qkv.shape[0], qkv.shape[1] // (3 * HEAD)
+    parts = lax.axis_size("expert")
     whole = pl.BlockSpec(memory_space=pltpu.VMEM)
+    sem = pltpu.SemaphoreType.DMA
     return pl.pallas_call(
-        attention_kernel,
+        functools.partial(attention_kernel, parts),
         grid=(heads,),
         in_specs=[whole, whole] + head_specs(total, heads),
-        out_specs=[
-            pl.BlockSpec((total, HEAD), lambda h: (0, h)),
-            pl.BlockSpec((1, total, 1), lambda h: (h, 0, 0)),
-        ],
+        out_specs=[ANY, pl.BlockSpec((1, total, 1), lambda h: (h, 0, 0))],
         out_shape=[
-            jax.ShapeDtypeStruct((total, heads * HEAD), jnp.bfloat16),
+            jax.ShapeDtypeStruct((total // parts, D), jnp.bfloat16),
             jax.ShapeDtypeStruct((heads, total, 1), jnp.float32),
         ],
+        scratch_shapes=[
+            pltpu.VMEM((heads, total, HEAD), jnp.bfloat16),
+            sem((heads,)),
+            sem((heads, parts - 1)),
+            sem((heads, parts - 1)),
+        ],
         compiler_params=pltpu.CompilerParams(
-            dimension_semantics=("arbitrary",), vmem_limit_bytes=48 * 1024 * 1024
+            dimension_semantics=("arbitrary",),
+            vmem_limit_bytes=48 * 1024 * 1024,
+            collective_id=cid,
+            has_side_effects=True,
         ),
         cost_estimate=pl.CostEstimate(
-            flops=3 * heads * total * total * HEAD,
-            bytes_accessed=8 * total * heads * HEAD,
-            transcendentals=heads * total * total // 2,
+            flops=0, bytes_accessed=200 * total * heads * HEAD, transcendentals=heads * total * total // 2
         ),
         name="attention",
     )(column, row, qkv, qkv, qkv)
 
 
 def attention_back_kernel(
-    column_ref, row_ref, query_ref, key_ref, value_ref, grad_ref, lse_ref, back_query_ref, back_key_ref, back_value_ref, key_acc, value_acc
+    parts,
+    column_ref,
+    row_ref,
+    query_ref,
+    key_ref,
+    value_ref,
+    lse_ref,
+    sent_ref,
+    back_query_ref,
+    back_key_ref,
+    back_value_ref,
+    key_acc,
+    value_acc,
+    grads,
+    own_sem,
+    send,
+    recv,
 ):
+    head, heads = pl.program_id(0), pl.num_programs(0)
+    me = lax.axis_index("expert")
     scale = HEAD ** (-0.5)
     total = query_ref.shape[0]
+    piece = total // parts
+
+    def moved(h, k, origin, to):
+        lanes = pl.ds(pl.multiple_of(h * HEAD, HEAD), HEAD)
+        return pltpu.make_async_remote_copy(
+            src_ref=sent_ref.at[row_block(to, piece), lanes],
+            dst_ref=grads.at[h, row_block(origin, piece)],
+            send_sem=send.at[h, k - 1],
+            recv_sem=recv.at[h, k - 1],
+            device_id={"expert": to},
+            device_id_type=MESH,
+        )
+
+    def kept(h):
+        lanes = pl.ds(pl.multiple_of(h * HEAD, HEAD), HEAD)
+        return pltpu.make_async_copy(
+            sent_ref.at[row_block(me, piece), lanes], grads.at[h, row_block(me, piece)], own_sem.at[h]
+        )
+
+    @pl.when(head == 0)
+    def _():
+        greet_all(me, parts)
+
+        @pl.loop(0, heads)
+        def _(h):
+            for k in range(parts - 1, 0, -1):
+                moved(h, k, me, lax.rem(me + k, parts)).start()
+            kept(h).start()
+
+    kept(head).wait()
+    for k in range(parts - 1, 0, -1):
+        moved(head, k, lax.rem(me + parts - k, parts), me).wait_recv()
     key_acc[...] = jnp.zeros_like(key_acc)
     value_acc[...] = jnp.zeros_like(value_acc)
     for block in range(total // BLOCK):
         here = pl.ds(block * BLOCK, BLOCK)
         upto = pl.ds(0, (block + 1) * BLOCK)
-        query, grad = query_ref[here, :], grad_ref[here, :]
+        query, grad = query_ref[here, :], grads[head, here, :]
         scores = masked_scores(query, key_ref, column_ref, row_ref, block)
         probs = jnp.exp(scores - lse_ref[0, here, :])
         prob_back = dot_right(grad, value_ref[upto, :])
@@ -528,30 +626,46 @@
     back_key_ref[...] = (key_acc[...] * scale).astype(jnp.bfloat16)
     back_value_ref[...] = value_acc[...].astype(jnp.bfloat16)
 
-
-def run_attention_back(column, row, qkv, grad, lse):
+    @pl.when(head == heads - 1)
+    def _():
+        @pl.loop(0, heads)
+        def _(h):
+            for k in range(parts - 1, 0, -1):
+                moved(h, k, me, lax.rem(me + k, parts)).wait_send()
+
+
+def run_attention_back(column, row, qkv, sent, lse, cid):
     total, heads = qkv.shape[0], qkv.shape[1] // (3 * HEAD)
+    parts = lax.axis_size("expert")
     whole = pl.BlockSpec(memory_space=pltpu.VMEM)
     head = pl.BlockSpec((total, HEAD), lambda h: (0, h))
+    sem = pltpu.SemaphoreType.DMA
     return pl.pallas_call(
-        attention_back_kernel,
+        functools.partial(attention_back_kernel, parts),
         grid=(heads,),
         in_specs=[whole, whole]
         + head_specs(total, heads)
-        + [head, pl.BlockSpec((1, total, 1), lambda h: (h, 0, 0))],
+        + [pl.BlockSpec((1, total, 1), lambda h: (h, 0, 0)), ANY],
         out_specs=[head] * 3,
         out_shape=[jax.ShapeDtypeStruct((total, heads * HEAD), jnp.bfloat16)] * 3,
-        scratch_shapes=[pltpu.VMEM((total, HEAD), jnp.float32)] * 2,
+        scratch_shapes=[pltpu.VMEM((total, HEAD), jnp.float32)] * 2
+        + [
+            pltpu.VMEM((heads, total, HEAD), jnp.bfloat16),
+            sem((heads,)),
+            sem((heads, parts - 1)),
+            sem((heads, parts - 1)),
+        ],
         compiler_params=pltpu.CompilerParams(
-            dimension_semantics=("arbitrary",), vmem_limit_bytes=48 * 1024 * 1024
+            dimension_semantics=("arbitrary",),
+            vmem_limit_bytes=48 * 1024 * 1024,
+            collective_id=cid,
+            has_side_effects=True,
         ),
         cost_estimate=pl.CostEstimate(
-            flops=8 * heads * total * total * HEAD,
-            bytes_accessed=16 * total * heads * HEAD,
-            transcendentals=heads * total * total // 2,
+            flops=0, bytes_accessed=200 * total * heads * HEAD, transcendentals=heads * total * total // 2
         ),
         name="attention_back",
-    )(column, row, qkv, qkv, qkv, grad, lse)
+    )(column, row, qkv, qkv, qkv, lse, sent)
 
 
 def own_lift(lift_ref, j):
@@ -858,7 +972,7 @@
     total, width = backs[0].shape
     tile = 512
     weights = [
-        pl.BlockSpec((tile, width), lambda i, part=part: (i, part)) for part in range(3)
+        pl.BlockSpec((tile, width), lambda i, part=part: (i, D // width + part)) for part in range(3)
     ]
     return pl.pallas_call(
         first_kernel,
@@ -911,7 +1025,7 @@
             VMEM,
             VMEM,
             pl.BlockSpec((RANK, width), lambda i: (0, i)),
-            pl.BlockSpec((D, width), lambda i: (0, i)),
+            pl.BlockSpec((D, width), lambda i: (0, D // width + i)),
         ],
         out_specs=[
             all_of(total, D),
@@ -1203,7 +1317,7 @@
     small = jnp.concatenate(
         [columns(router_weight, 32), columns(adapter_router, 32), columns(norm_gains.T, 64)], axis=1
     )
-    dense_line, out_line, chosen_line = gather_weights(qkv_blocks, out_weight, small, chosen, 0)
+    dense_line, chosen_line = gather_weights(qkv_blocks, out_weight, small, chosen, 0)
     chosen_all = lax.all_to_all(
         chosen_line.reshape(parts * share, groups, LANES).transpose(1, 0, 2),
         "dp",
@@ -1211,14 +1325,13 @@
         concat_axis=0,
         tiled=True,
     ).reshape(D, LANES)
-    dense_line, out_line, expert_input, matrix_out, chosen_all, pairs = lax.optimization_barrier(
-        (dense_line, out_line, expert_input, matrix_out, chosen_all, pairs)
+    dense_line, expert_input, matrix_out, chosen_all, pairs = lax.optimization_barrier(
+        (dense_line, expert_input, matrix_out, chosen_all, pairs)
     )
     dense_all = lax.all_gather(dense_line, "dp", axis=0, tiled=True)
     (tokens_all,) = line_gather([tokens], 1, 2)
-    out_matrix = lax.all_gather(out_line, "dp", axis=0, tiled=True)
     matrix_in = lax.all_gather(expert_input, "dp", axis=1, tiled=True)
-    small_at = 3 * width
+    small_at = D + 3 * width
 
     picked, router_rows, gain_rows = pick_rows(chosen_all, dense_all, small_at, experts)
     down_query, down_mix, down_route = picked[:16], picked[16:32], picked[32:48]
@@ -1248,8 +1361,7 @@
     )
     segments = segments_of(cont_lengths[0], jnp.arange(total, dtype=jnp.int32))
     segment_column, segment_row = segments[:, None], segments[None, :]
-    mixed_heads, log_mass = run_attention(segment_column, segment_row, qkv_low)
-    (mixed_low,) = exchange([mixed_heads], 3)
+    mixed_low, log_mass = run_attention(segment_column, segment_row, qkv_low, 3)
 
     middle, rank_mix, inverse_second, second_low, rank_route, router_probs, gates = finish_attention(
         experts,
@@ -1262,7 +1374,7 @@
         router_rows,
         lift_route,
         routed,
-        out_matrix,
+        dense_all,
     )
     held = lax.optimization_barrier([second_low] + [moved[s] for s in early_shifts])
     second_low = held[0]
@@ -1311,12 +1423,11 @@
         down_route,
         lift_mix,
         down_mix,
-        out_matrix,
-    )
-
-    (mixed_back,) = exchange([mixed_grad], 6, stack=True)
+        dense_all,
+    )
+
     back_query, back_key, back_value = run_attention_back(
-        segment_column, segment_row, qkv_low, mixed_back, log_mass
+        segment_column, segment_row, qkv_low, mixed_grad, log_mass, 6
     )
     qkv_back = jnp.concatenate([back_query, back_key, back_value], axis=1)
     rank_query_grad = dot_right(qkv_back, lift_query).astype(low)

time: 868 us -> 852 us (0.982)
  Pallas kernels: 650 us -> 626 us
    pallas_call x4 -> x2, Pallas kernels: 92 us -> 68 us  [the longest x1 35 us: run_attention(): pl.pallas_call(functools.partial(attention_kernel, parts), grid=(heads,),...]
  transfers between devices with their start and end apart: 13 -> 12, of which waited for: 4 -> 4; matrix products, arithmetic and copies ran while one was open for 6% -> 7% of each run, Pallas kernels for 67% -> 67%
where the time goes in v5:
time: 852 us; the launch traced here: 846 us
  Pallas kernels  626 us (73%)
  waiting for transfers between devices  87.3 us (10%)
  local copies, waits for them, and re-layouts  43.9 us (5%)
  starting transfers between devices  33.8 us (4%)
  other arithmetic  16.9 us (2%)
  matrix products  16.3 us (2%)
  between operations  15.7 us (2%)
    pallas_call x2, Pallas kernels, line_gather(): pl.pallas_call(functools.partial(gather_kernel, parts, pieces, n), out_sh...  176 us
    pallas_call x1, Pallas kernels, experts_backward(): pl.pallas_call(functools.partial(backward_kernel, parts), grid=(EXP_DEV,...  99.5 us
    pallas_call x1, Pallas kernels, line_reduce(): pl.pallas_call(functools.partial(reduce_kernel, parts, pieces), out_shape...  93.3 us
    pallas_call x1, Pallas kernels, experts_forward(): pl.pallas_call(forward_kernel, grid=(EXP_DEV, FF // TILE), in_specs=[VMEM...  87.2 us
    pallas_call x1, Pallas kernels, gather_weights(): pl.pallas_call(functools.partial(weights_kernel, parts), out_shape=[jax.S...  43.2 us
    pallas_call x1, Pallas kernels, run_attention(): pl.pallas_call(functools.partial(attention_kernel, parts), grid=(heads,),...  35 us
    reduce_scatter x1, waiting for transfers between devices, body(): lax.psum_scatter(first_terms, 'expert', scatter_dimension=0, tiled=True)  33.3 us
    pallas_call x1, Pallas kernels, run_attention_back(): pl.pallas_call(functools.partial(attention_back_kernel, parts), grid=(hea...  32.9 us
  transfers between devices with their start and end apart: 12, of which 4 were waited for; matrix products, arithmetic and copies ran while one was open for 7% of the time, Pallas kernels for 67%

profile of v5, /device:TPU:9, one launch (start us, length us, event | category | flops | bytes accessed | tf_op | source)
XLA Modules:
  0.0 846.2 jit_solution(8218514579955290182)
XLA Ops:
  10.6 6.5 all-reduce.5
  19.7 5.7 all-to-all-start.1
  30.2 43.2 %gather_weights.1 = (bf16[256,3712]{1,0:T(8,128)(2,1)}, bf16[256,1024]{1,0:T(8,128)(2,1)}) custom-call(bf16[256,1536]{1,0:T(8,128)(2,1)} %bitcast.104, bf16[64,2048]{1,0:T(8,128)(2,1)} %out.1, bf16[64,128]{1,0:T(8,128)(2,1)} %fusion.24.small, bf16[64,1024]{1,0:T(8,128)(2,1)} %fusion.9.chosen), custom_call_target="tpu_custom_call" | custom-call | bytes 169738240 | tf_op jit(solution)/shard_map/gather_weights/pallas_call | solution.py:426
  75.4 5.8 all-to-all-start
  81.8 11.3 %all-to-all-done = bf16[8,256,128]{2,1,0:T(8,128)(2,1)S(1)} async-done(((bf16[8,256,128]{2,1,0:T(8,128)(2,1)}), bf16[8,256,128]{2,1,0:T(8,128)(2,1)S(1)}, u32[]{:S(2)}, u32[]{:S(2)}) %all-to-all-start) | async-done | bytes 524320 | tf_op jit(solution)/shard_map/all_to_all | solution.py:1321
  93.1 19.5 %all-gather.4.cloned.1.call-done.out_ref = bf16[4,1024,2048]{2,1,0:T(8,128)(2,1)} async-done(((bf16[4,128,2048]{2,1,0:T(8,128)(2,1)}), bf16[4,1024,2048]{2,1,0:T(8,128)(2,1)}) %all-gather.4.cloned.1.call-update) | async-done | bytes 16777232 | tf_op jit(solution)/shard_map/all_gather | solution.py:1273
  113.5 85.9 %line_gather_1.1.tokens_ref = bf16[1280,2048]{1,0:T(8,128)(2,1)} custom-call(bf16[320,2048]{1,0:T(8,128)(2,1)} %tokens_ref.1), custom_call_target="tpu_custom_call" | custom-call | bytes 367001600 | tf_op jit(solution)/shard_map/line_gather_1/pallas_call | solution.py:148
  214.3 17.9 %project_qkv.1 = (bf16[1280,2048]{1,0:T(8,128)(2,1)}, bf16[1280,16]{1,0:T(8,128)(2,1)}, bf16[1280,1536]{1,0:T(8,128)(2,1)}) custom-call(bf16[1280,2048]{1,0:T(8,128)(2,1)} %line_gather_1.1.tokens_ref, f32[1,2048]{1,0:T(1,128)} %get-tuple-element.121.gain_ref, bf16[16,2048]{1,0:T(8,128)(2,1)} %get-tuple-element.119.down_ref, bf16[16,1536]{1,0:T(8,128)(2,1)} %bitcast.128, ...), custom_call_target="tpu_custom_call" | custom-call | flops 8053063680 | bytes 27262976 | tf_op jit(solution)/shard_map/project_qkv/pallas_call | solution.py:1020
  232.2 35.0 %attention.1 = (bf16[320,2048]{1,0:T(8,128)(2,1)S(1)}, f32[4,1280,1]{2,1,0:T(8,128)S(1)}) custom-call(s32[1280,1]{1,0:T(8,128)S(1)} %reshape_select_fusion.column_ref, s32[1,1280]{1,0:T(1,128)S(1)} %compare_select_fusion.row_ref, bf16[1280,1536]{1,0:T(8,128)(2,1)} %get-tuple-element.66.query_ref.key_ref.value_ref, ...), custom_call_target="tpu_custom_call" | custom-call | bytes 131072000 | tf_op jit(solution)/shard_map/attention/pallas_call | solution.py:529
  270.1 12.6 %finish_attention.1 = (f32[320,2048]{1,0:T(8,128)}, bf16[320,16]{1,0:T(8,128)(2,1)}, f32[320,1]{1,0:T(8,128)}, bf16[320,2048]{1,0:T(8,128)(2,1)}, bf16[320,16]{1...) custom-call(bf16[320,2048]{1,0:T(8,128)(2,1)} %copy-done.1, bf16[320,2048]{1,0:T(8,128)(2,1)} %tokens_ref.1, ...), custom_call_target="tpu_custom_call" | custom-call | flops 2684354560 | bytes 16252928 | tf_op jit(solution)/shard_map/finish_attention/pallas_call | solution.py:1100
  282.7 90.5 %line_gather_4.1 = (bf16[1280,2048]{1,0:T(8,128)(2,1)}, bf16[1280,128]{1,0:T(8,128)(2,1)}) custom-call(bf16[320,2048]{1,0:T(8,128)(2,1)} %get-tuple-element.73.refs_0_, bf16[320,128]{1,0:T(8,128)(2,1)} %get-tuple-element.74.refs_1_), custom_call_target="tpu_custom_call" | custom-call | bytes 389939200 | tf_op jit(solution)/shard_map/line_gather_4/pallas_call | solution.py:148
  376.1 87.2 %experts_forward.1 = (bf16[1280,2048]{1,0:T(8,128)(2,1)}, bf16[1280,128]{1,0:T(8,128)(2,1)}, bf16[4,1280,1024]{2,1,0:T(8,128)(2,1)}, bf16[4,1280,1024]{2,1,0:T(8,128)(2,1)}) custom-call(bf16[1280,2048]{1,0:T(8,128)(2,1)} %get-tuple-element.77.rows_ref, bf16[1280,128]{1,0:T(8,128)(2,1)} %get-tuple-element.75.gates_ref, ...), custom_call_target="tpu_custom_call" | custom-call | flops 107374182400 | bytes 71303168 | tf_op jit(solution)/shard_map/experts_forward/pallas_call | solution.py:769
  464.6 99.5 %experts_backward.1 = (bf16[1280,2176]{1,0:T(8,128)(2,1)}, bf16[1280,128]{1,0:T(8,128)(2,1)}, f32[4,16,1024]{2,1,0:T(8,128)}, f32[4,16,1024]{2,1,0:T(8,128)}) custom-call(bf16[1280,128]{1,0:T(8,128)(2,1)} %get-tuple-element.75.gates_ref, bf16[1280,128]{1,0:T(8,128)(2,1)} %get-tuple-element.81.ranks_ref, bf16[128,2048]{1,0:T(8,128)(2,1)} %get-tuple-element.115.down_ref, ...), custom_call_target="tpu_custom_call" | custom-call | flops 128849018880 | bytes 71303168 | tf_op jit(solution)/shard_map/experts_backward/pallas_call | solution.py:902
  564.2 93.3 %line_reduce_5.1.slot_ref = f32[320,2176]{1,0:T(8,128)S(1)} custom-call(bf16[1280,2176]{1,0:T(8,128)(2,1)} %get-tuple-element.86.src), custom_call_target="tpu_custom_call" | custom-call | bytes 389939200 | tf_op jit(solution)/shard_map/line_reduce_5/pallas_call | solution.py:315
  659.0 12.5 %middle_backward.1 = (bf16[1280,512]{1,0:T(8,128)(2,1)}, f32[320,2048]{1,0:T(8,128)}, bf16[320,2048]{1,0:T(8,128)(2,1)}, bf16[320,128]{1,0:T(8,128)(2,1)}, bf16[...) custom-call(f32[320,2176]{1,0:T(8,128)} %copy-done, f32[320,128]{1,0:T(8,128)} %get-tuple-element.89.probs_ref, ...), custom_call_target="tpu_custom_call" | custom-call | flops 2684354560 | bytes 24117248 | tf_op jit(solution)/shard_map/middle_backward/pallas_call | solution.py:1189
  672.8 32.9 %attention_back.1 = (bf16[1280,512]{1,0:T(8,128)(2,1)S(1)}, bf16[1280,512]{1,0:T(8,128)(2,1)S(1)}, bf16[1280,512]{1,0:T(8,128)(2,1)S(1)}) custom-call(s32[1280,1]{1,0:T(8,128)S(1)} %reshape_select_fusion.column_ref, s32[1,1280]{1,0:T(1,128)S(1)} %compare_select_fusion.row_ref, bf16[1280,1536]{1,0:T(8,128)(2,1)} %get-tuple-element.66.query_ref.key_ref.value_ref, ...), custom_call_target="tpu_custom_call" | custom-call | bytes 131072000 | tf_op jit(solution)/shard_map/attention_back/pallas_call | solution.py:643
  708.5 12.9 %first_products.1 = bf16[1280,2048]{1,0:T(8,128)(2,1)} custom-call(bf16[1280,512]{1,0:T(8,128)(2,1)S(1)} %get-tuple-element.92.query_ref, bf16[1280,512]{1,0:T(8,128)(2,1)S(1)} %get-tuple-element.93.key_ref, bf16[1280,512]{1,0:T(8,128)(2,1)S(1)} %get-tuple-element.94.value_ref, bf16[1280,16]{1,0:T(8,128)(2,1)S(1)} %convolution_convert_fusion.1.rank_ref, ...), custom_call_target="tpu_custom_call" | custom-call | flops 8053063680 | bytes 11534336 | tf_op jit(solution)/shard_map/first_products/pallas_call | solution.py:977
  722.3 3.6 convolution_convert_fusion.2
  727.0 10.8 %all-to-all-start.3 = ((bf16[8,128,256]{2,1,0:T(8,128)(2,1)}), bf16[8,128,256]{2,1,0:T(8,128)(2,1)S(1)}, u32[]{:S(2)}, u32[]{:S(2)}) async-start(bf16[8,128,256]{2,1,0:T(8,128)(2,1)} %maximum_bitcast_fusion.1), calls=%async_computation.5 | async-start | bytes 1048576 | tf_op jit(solution)/shard_map/all_to_all | solution.py:1405
  753.4 3.3 convolution_convert_fusion.6
  760.7 6.8 all-to-all-start.2
  771.4 21.7 %all-to-all-done.2 = bf16[32,2,3712]{2,1,0:T(2,128)(2,1)S(1)} async-done(((bf16[32,2,3712]{2,1,0:T(2,128)(2,1)}), bf16[32,2,3712]{2,1,0:T(2,128)(2,1)S(1)}, u32[]{:S(2)}, u32[]{:S(2)}) %all-to-all-start.2) | async-done | bytes 475168 | tf_op jit(solution)/shard_map/all_to_all | solution.py:1458
  800.2 33.3 %reduce-scatter.5.cloned.1.call-done = bf16[320,2048]{1,0:T(8,128)(2,1)} async-done(((bf16[1280,2048]{1,0:T(8,128)(2,1)}), bf16[320,2048]{1,0:T(8,128)(2,1)}) %reduce-scatter.5.cloned.1.call-update) | async-done | bytes 1310736 | tf_op jit(solution)/shard_map/reduce_scatter | solution.py:1457
  835.7 3.6 fusion.5
  (199 shorter events, 75.2 us)
Async XLA Ops:
  7.2 105.5 %all-gather.4.cloned.1.call-start = ((), (), s32[]{:S(2)}) async-start(), calls=%async_computation.6 | async-start | bytes 18874368 | tf_op jit(solution)/shard_map/all_gather | solution.py:1273
  17.0 11.6 %copy-start.28 = (s32[8]{0:T(128)}, s32[8]{0:T(128)S(1)}, u32[]{:S(2)}) copy-start(s32[8]{0:T(128)S(1)} %all-reduce.5) | copy-start | bytes 100
  19.7 55.7 %all-to-all-start.1 = ((bf16[8,128,256]{2,1,0:T(8,128)(2,1)}), bf16[8,128,256]{2,1,0:T(8,128)(2,1)S(1)}, u32[]{:S(2)}, u32[]{:S(2)}) async-start(bf16[8,128,256]{2,1,0:T(8,128)(2,1)} %copy.100), calls=%async_computation.1 | async-start | bytes 1048576 | tf_op jit(solution)/shard_map/all_to_all | solution.py:1282
  75.4 17.7 %all-to-all-start = ((bf16[8,256,128]{2,1,0:T(8,128)(2,1)}), bf16[8,256,128]{2,1,0:T(8,128)(2,1)S(1)}, u32[]{:S(2)}, u32[]{:S(2)}) async-start(bf16[8,256,128]{2,1,0:T(8,128)(2,1)} %bitcast_bitcast_fusion), calls=%async_computation | async-start | bytes 1048576 | tf_op jit(solution)/shard_map/all_to_all | solution.py:1321
  81.1 123.6 %all-gather.6.cloned.1.call-start = ((), (), s32[]{:S(2)}) async-start(), calls=%async_computation.7 | async-start | bytes 17104896 | tf_op jit(solution)/shard_map/all_gather | solution.py:1331
  93.1 20.3 %copy-start.11 = (bf16[8,256,128]{2,1,0:T(8,128)(2,1)}, bf16[8,256,128]{2,1,0:T(8,128)(2,1)S(1)}, u32[]{:S(2)}) copy-start(bf16[8,256,128]{2,1,0:T(8,128)(2,1)S(1)} %all-to-all-done) | copy-start | bytes 1572868
  112.6 263.5 %all-gather.8.cloned.1.call-start = ((), (), s32[]{:S(2)}) async-start(), calls=%async_computation.8 | async-start | bytes 37748736 | tf_op jit(solution)/shard_map/all_gather | solution.py:1333
  113.4 86.0 %copy-start.12 = (bf16[320,2048]{1,0:T(8,128)(2,1)S(1)}, bf16[320,2048]{1,0:T(8,128)(2,1)}, u32[]{:S(2)}) copy-start(bf16[320,2048]{1,0:T(8,128)(2,1)} %cotangent_ref.1) | copy-start | bytes 3932164
  113.4 87.5 %copy-start.27 = (s32[320,8]{0,1:T(8,128)S(1)}, s32[320,8]{0,1:T(8,128)}, u32[]{:S(2)}) copy-start(s32[320,8]{0,1:T(8,128)} %param.31) | copy-start | bytes 30724
  113.4 90.0 %copy-start.36 = (s32[1,8]{1,0:T(1,128)S(1)}, s32[1,8]{1,0:T(1,128)}, u32[]{:S(2)}) copy-start(s32[1,8]{1,0:T(1,128)} %param.33) | copy-start | bytes 100
  113.4 545.6 %reduce-scatter.3.cloned.1.call-start = ((), (), s32[]{:S(2)}) async-start(), calls=%async_computation.9 | async-start | bytes 6553600 | tf_op jit(solution)/shard_map/reduce_scatter | solution.py:1390
  199.4 83.3 %collective-permute-start = (bf16[320,2048]{1,0:T(8,128)(2,1)S(1)}, bf16[320,2048]{1,0:T(8,128)(2,1)}, u32[]{:S(2)}, u32[]{:S(2)}) collective-permute-start(bf16[320,2048]{1,0:T(8,128)(2,1)S(1)} %copy-done.12), channel_id=1, source_target_pairs={{0,1},{1,2},{2,3},{3,0},{4,5},{5,6},{6,7},{7,4},{8,9},{9,10},{10,1... | collective-permute-start | bytes 3932168 | tf_op jit(solution)/shard_map/ppermute | solution.py:1353
  373.2 90.3 %collective-permute-start.1 = (bf16[320,2048]{1,0:T(8,128)(2,1)S(1)}, bf16[320,2048]{1,0:T(8,128)(2,1)S(1)}, u32[]{:S(2)}, u32[]{:S(2)}) collective-permute-start(bf16[320,2048]{1,0:T(8,128)(2,1)S(1)} %copy-done.12), channel_id=1, source_target_pairs={{0,2},{1,3},{2,0},{3,1},{4,6},{5,7},{6,4},{7,5},{8,10},{9,11},{10,... | collective-permute-start | bytes 3932168 | tf_op jit(solution)/shard_map/ppermute | solution.py:1353
  375.7 87.9 %collective-permute-start.2 = (bf16[320,2048]{1,0:T(8,128)(2,1)S(1)}, bf16[320,2048]{1,0:T(8,128)(2,1)}, u32[]{:S(2)}, u32[]{:S(2)}) collective-permute-start(bf16[320,2048]{1,0:T(8,128)(2,1)S(1)} %copy-done.12), channel_id=1, source_target_pairs={{0,3},{1,0},{2,1},{3,2},{4,7},{5,4},{6,5},{7,6},{8,11},{9,8},{10,9... | collective-permute-start | bytes 3932168 | tf_op jit(solution)/shard_map/ppermute | solution.py:1353
  463.3 370.2 %reduce-scatter.5.cloned.1.call-start = ((), (), s32[]{:S(2)}) async-start(), calls=%async_computation.10 | async-start | bytes 6553600 | tf_op jit(solution)/shard_map/reduce_scatter | solution.py:1457
  725.9 11.9 %copy-start.17 = (bf16[1280,16]{1,0:T(8,128)(2,1)S(1)}, bf16[1280,16]{1,0:T(8,128)(2,1)}, u32[]{:S(2)}) copy-start(bf16[1280,16]{1,0:T(8,128)(2,1)} %get-tuple-element.104) | copy-start | bytes 122884
  727.0 33.7 %all-to-all-start.3 = ((bf16[8,128,256]{2,1,0:T(8,128)(2,1)}), bf16[8,128,256]{2,1,0:T(8,128)(2,1)S(1)}, u32[]{:S(2)}, u32[]{:S(2)}) async-start(bf16[8,128,256]{2,1,0:T(8,128)(2,1)} %maximum_bitcast_fusion.1), calls=%async_computation.5 | async-start | bytes 1048576 | tf_op jit(solution)/shard_map/all_to_all | solution.py:1405
  737.9 12.7 %copy-start.9 = (bf16[320,2048]{1,0:T(8,128)(2,1)S(1)}, bf16[320,2048]{1,0:T(8,128)(2,1)}, u32[]{:S(2)}) copy-start(bf16[320,2048]{1,0:T(8,128)(2,1)} %get-tuple-element.73.refs_0_) | copy-start | bytes 3932164
  740.7 11.2 %copy-start.2 = (bf16[320,2048]{1,0:T(8,128)(2,1)S(1)}, bf16[320,2048]{1,0:T(8,128)(2,1)}, u32[]{:S(2)}) copy-start(bf16[320,2048]{1,0:T(8,128)(2,1)} %copy-done.1) | copy-start | bytes 3932164
  741.4 11.7 %copy-start.21 = (bf16[320,16]{1,0:T(8,128)(2,1)S(1)}, bf16[320,16]{1,0:T(8,128)(2,1)}, u32[]{:S(2)}) copy-start(bf16[320,16]{1,0:T(8,128)(2,1)} %get-tuple-element.102) | copy-start | bytes 30724
  757.5 10.0 %copy-start.29 = (s32[8]{0:T(128)S(1)}, s32[8]{0:T(128)}, u32[]{:S(2)}) copy-start(s32[8]{0:T(128)} %copy-done.28) | copy-start | bytes 100
  760.7 32.4 %all-to-all-start.2 = ((bf16[32,2,3712]{2,1,0:T(2,128)(2,1)}), bf16[32,2,3712]{2,1,0:T(2,128)(2,1)S(1)}, u32[]{:S(2)}, u32[]{:S(2)}) async-start(bf16[32,2,3712]{2,1,0:T(2,128)(2,1)} %reshape.428), calls=%async_computation.4 | async-start | bytes 950272 | tf_op jit(solution)/shard_map/all_to_all | solution.py:1458
  796.2 37.3 %copy-start.6 = (bf16[320,2048]{1,0:T(8,128)(2,1)S(1)}, bf16[320,2048]{1,0:T(8,128)(2,1)}, u32[]{:S(2)}) copy-start(bf16[320,2048]{1,0:T(8,128)(2,1)} %tokens_ref.1) | copy-start | bytes 3932164
  796.2 37.3 %copy-start.24 = (f32[1,2048]{1,0:T(1,128)S(1)}, f32[1,2048]{1,0:T(1,128)}, u32[]{:S(2)}) copy-start(f32[1,2048]{1,0:T(1,128)} %get-tuple-element.121.gain_ref) | copy-start | bytes 24580
  (26 other events, 59.3 us)
Sparse Core Ops, SparseCore 0:
  9.9 102.6 all-gather.3
  114.5 83.1 all-gather.5
  199.7 160.7 all-gather.7
  463.5 96.5 reduce-scatter.2
  721.5 111.9 reduce-scatter.4

commit v6 on v5

--- a/solution.py
+++ b/solution.py
@@ -698,7 +698,7 @@
     out_ref,
     *refs,
 ):
-    output_ref, ranks_ref, gate_ref, up_ref, output_acc, stage, sems = refs
+    output_ref, output_rest_ref, ranks_ref, gate_ref, up_ref, output_acc, stage, sems = refs
     j, f = pl.program_id(0), pl.program_id(1)
     total = rows_ref.shape[0]
 
@@ -726,25 +726,35 @@
 
     @pl.when((j == EXP_DEV - 1) & (f == FF // TILE - 1))
     def _():
-        def copy(b):
+        def copies(b):
             slot = lax.rem(b, 2)
             here = row_chunk(b, stage.shape[1])
-            return pltpu.make_async_copy(stage.at[slot], output_ref.at[here], sems.at[slot])
-
+            half = D // 2
+            return [
+                pltpu.make_async_copy(
+                    stage.at[slot, :, h * half : (h + 1) * half], refs_out[h].at[here], sems.at[slot, h]
+                )
+                for h in range(2)
+            ]
+
+        refs_out = (output_ref, output_rest_ref)
         steps = total // stage.shape[1]
 
         @pl.loop(0, steps)
         def _(b):
             @pl.when(b >= 2)
             def _():
-                copy(b - 2).wait()
+                for copy in copies(b - 2):
+                    copy.wait()
 
             here = row_chunk(b, stage.shape[1])
             stage[lax.rem(b, 2)] = output_acc[here, :].astype(jnp.bfloat16)
-            copy(b).start()
+            for copy in copies(b):
+                copy.start()
 
         for b in range(steps - 2, steps):
-            copy(b).wait()
+            for copy in copies(b):
+                copy.wait()
 
 
 def weight_specs():
@@ -772,12 +782,14 @@
         in_specs=[VMEM] * 3 + weight_specs(),
         out_specs=[
             ANY,
+            ANY,
             pl.BlockSpec((total, LANES), lambda j, f: (0, 0), pipeline_mode=pl.Buffered(1)),
             kept,
             kept,
         ],
         out_shape=[
-            jax.ShapeDtypeStruct((total, D), jnp.bfloat16),
+            jax.ShapeDtypeStruct((total, D // 2), jnp.bfloat16),
+            jax.ShapeDtypeStruct((total, D // 2), jnp.bfloat16),
             jax.ShapeDtypeStruct((total, LANES), jnp.bfloat16),
             jax.ShapeDtypeStruct((EXP_DEV, total, FF), jnp.bfloat16),
             jax.ShapeDtypeStruct((EXP_DEV, total, FF), jnp.bfloat16),
@@ -785,7 +797,7 @@
         scratch_shapes=[
             pltpu.VMEM((total, D), jnp.float32),
             pltpu.VMEM((2, 160, D), jnp.bfloat16),
-            pltpu.SemaphoreType.DMA((2,)),
+            pltpu.SemaphoreType.DMA((2, 2)),
         ],
         compiler_params=EXPERT_PARAMS,
         cost_estimate=pl.CostEstimate(
@@ -807,126 +819,262 @@
     in_gate_ref,
     in_up_ref,
     out_ref,
-    gate_ref,
-    up_ref,
+    gate_hbm,
+    up_hbm,
     *refs,
 ):
     blocks, refs = refs[:parts], refs[parts:]
-    slot_ref, rank_ref, lift_grad_gate_ref, lift_grad_up_ref, upstream, slot_acc, rank_acc, gate_acc, lift_acc, stage, sems = refs
-    j, f = pl.program_id(0), pl.program_id(1)
+    sum_ref, rank_ref, lift_grad_ref, upstream, slot_acc, rank_acc, gate_acc, terms, gates, ups, load_sems, kept_sems = refs[:12]
+    slot_up, slot_down, send_up, recv_up, send_down, recv_down = refs[12:]
+    q, j, f = pl.program_id(0), pl.program_id(1), pl.program_id(2)
+    tiles = FF // TILE
+    me = lax.axis_index("expert")
     total = upstream.shape[0]
-
-    @pl.when((j == 0) & (f == 0))
-    def _():
-        piece = total // parts
+    piece, rows = total // parts, total // 2
+    part = piece // 2
+    own_half = jnp.where(me < parts // 2, 1 - q, q)
+    begin = pl.multiple_of(own_half * rows, rows)
+    here = pl.ds(begin, rows)
+    inner = j * tiles + f
+    step = q * EXP_DEV * tiles + inner
+    slot_now = lax.rem(step, 2)
+
+    def fetches(at):
+        half = at // (EXP_DEV * tiles)
+        first = pl.multiple_of(jnp.where(me < parts // 2, 1 - half, half) * rows, rows)
+        source = (
+            lax.rem(at // tiles, EXP_DEV),
+            pl.ds(first, rows),
+            pl.ds(pl.multiple_of(lax.rem(at, tiles) * TILE, TILE), TILE),
+        )
+        slot = lax.rem(at, 2)
+        return (
+            pltpu.make_async_copy(gate_hbm.at[source], gates.at[slot], kept_sems.at[slot, 0]),
+            pltpu.make_async_copy(up_hbm.at[source], ups.at[slot], kept_sems.at[slot, 1]),
+        )
+
+    def hop(ref, slot, at, n, to, send, recv):
+        return pltpu.make_async_remote_copy(
+            src_ref=ref,
+            dst_ref=slot.at[at, n * part : (n + 1) * part],
+            send_sem=send.at[at, n],
+            recv_sem=recv.at[at, n],
+            device_id={"expert": to},
+            device_id_type=MESH,
+        )
+
+    def landed(slot, at, n, send, recv):
+        return hop(slot.at[at, n * part : (n + 1) * part], slot, at, n, me, send, recv)
+
+    streams = ((True, slot_up, send_up, recv_up), (False, slot_down, send_down, recv_down))
+
+    def where_to(up, at):
+        line = me if up else parts - 1 - me
+        dest_line = parts - 1 - at + line
+        return line, (me + 1 if up else me - 1), (dest_line if up else parts - 1 - dest_line)
+
+    def send_first(up, slot, send, recv, at):
+        line, to, dest = where_to(up, at)
+
+        @pl.when(line == 0)
+        def _():
+            for n in range(2):
+                there = pl.ds(pl.multiple_of(dest * piece + n * part, part), part)
+                hop(terms.at[there], slot, at, n, to, send, recv).start()
+
+    def pass_on(up, slot, send, recv, at, n):
+        _, to, dest = where_to(up, at)
+        landed(slot, at - 1, n, send, recv).wait_recv()
+        chunk = 16
+
+        @pl.loop(0, part // chunk)
+        def _(r):
+            local = pl.ds(pl.multiple_of(n * part + r * chunk, chunk), chunk)
+            there = pl.ds(pl.multiple_of(dest * piece + n * part + r * chunk, chunk), chunk)
+            both = slot[at - 1, local, :].astype(jnp.float32) + terms[there, :].astype(jnp.float32)
+            slot[at - 1, local, :] = both.astype(jnp.bfloat16)
+
+        hop(slot.at[at - 1, n * part : (n + 1) * part], slot, at, n, to, send, recv).start()
+
+    @pl.when(step == 0)
+    def _():
+        greet_line(me, parts)
         copies = []
         for shift in range(parts):
-            owner = lax.rem(lax.axis_index("expert") + parts - shift, parts)
-            there = row_chunk(owner, piece)
-            copies.append(pltpu.make_async_copy(blocks[shift], upstream.at[there], sems.at[shift]))
+            there = row_chunk(lax.rem(me + parts - shift, parts), piece)
+            copies.append(pltpu.make_async_copy(blocks[shift], upstream.at[there], load_sems.at[shift]))
         for copy in copies:
             copy.start()
-
-        @pl.loop(0, total // ROWS)
-        def _(b):
-            here = row_chunk(b)
-            slot_acc[here, :] = jnp.zeros((ROWS, D), jnp.float32)
-            rank_acc[here, :] = jnp.zeros((ROWS, LANES), jnp.float32)
-            gate_acc[here, :] = jnp.zeros((ROWS, LANES), jnp.float32)
-
+        for copy in fetches(step):
+            copy.start()
+        lift_grad_ref[...] = jnp.zeros_like(lift_grad_ref)
         for copy in copies:
             copy.wait()
 
-    lift_acc[...] = jnp.zeros_like(lift_acc)
+    @pl.when(step + 1 < 2 * EXP_DEV * tiles)
+    def _():
+        for copy in fetches(step + 1):
+            copy.start()
+
+    @pl.when(inner == 0)
+    def _():
+        slot_acc[...] = jnp.zeros_like(slot_acc)
+        rank_acc[...] = jnp.zeros_like(rank_acc)
+        gate_acc[...] = jnp.zeros_like(gate_acc)
+
     lift_gate, lift_up = own_lift(lift_gate_ref, j), own_lift(lift_up_ref, j)
-
-    @pl.loop(0, total // ROWS)
-    def _(b):
-        here = row_chunk(b)
-        mine, column = gate_column(gates_ref, here, j)
-        raw = dot_right(upstream[here, :], out_ref[0])
-        gate = gate_ref[0, here, :].astype(jnp.float32)
-        up = up_ref[0, here, :].astype(jnp.float32)
-        sigma = jax.nn.sigmoid(gate)
-        silu = gate * sigma
-        gate_grad = jnp.sum(raw * (silu * up), axis=1, keepdims=True)
-        back = raw * column
-        to_gate = (back * up * (sigma + silu * (1.0 - sigma))).astype(jnp.bfloat16)
-        to_up = (back * silu).astype(jnp.bfloat16)
-        slot_acc[here, :] += dot_right(to_gate, in_gate_ref[0]) + dot_right(
-            to_up, in_up_ref[0]
+    for copy in fetches(step):
+        copy.wait()
+    mine = lax.broadcasted_iota(jnp.int32, (rows, LANES), 1) == me * EXP_DEV + j
+    column = jnp.sum(jnp.where(mine, gates_ref[here, :].astype(jnp.float32), 0.0), axis=1, keepdims=True)
+    raw = dot_right(upstream[here, :], out_ref[0])
+    gate = gates[slot_now].astype(jnp.float32)
+    up_part = ups[slot_now].astype(jnp.float32)
+    sigma = jax.nn.sigmoid(gate)
+    silu = gate * sigma
+    gate_grad = jnp.sum(raw * (silu * up_part), axis=1, keepdims=True)
+    back = raw * column
+    to_gate = (back * up_part * (sigma + silu * (1.0 - sigma))).astype(jnp.bfloat16)
+    to_up = (back * silu).astype(jnp.bfloat16)
+    slot_acc[...] += dot_right(to_gate, in_gate_ref[0]) + dot_right(to_up, in_up_ref[0])
+    rank_acc[...] += dot_right(to_gate, lift_gate) + dot_right(to_up, lift_up)
+    gate_acc[...] += jnp.where(mine, gate_grad, 0.0)
+    ranks = ranks_ref[here, :]
+    for side, grad in enumerate((to_gate, to_up)):
+        lanes = pl.ds(pl.multiple_of(side * FF + f * TILE, TILE), TILE)
+        lift_grad_ref[:, lanes] += jnp.where(
+            lax.broadcasted_iota(jnp.int32, (LANES, TILE), 0) // RANK == j, dot_left(ranks, grad), 0.0
         )
-        rank_acc[here, :] += dot_right(to_gate, lift_gate) + dot_right(to_up, lift_up)
-        gate_acc[here, :] += jnp.where(mine, gate_grad, 0.0)
-        lift_acc[0] += dot_left(ranks_ref[here, :], to_gate)
-        lift_acc[1] += dot_left(ranks_ref[here, :], to_up)
-
-    own = row_chunk(j, RANK)
-    lift_grad_gate_ref[0] = lift_acc[0, own, :]
-    lift_grad_up_ref[0] = lift_acc[1, own, :]
-
-    @pl.when((j == EXP_DEV - 1) & (f == FF // TILE - 1))
-    def _():
-        def copy(b):
-            slot = lax.rem(b, 2)
-            here = row_chunk(b, stage.shape[1])
-            return pltpu.make_async_copy(stage.at[slot], slot_ref.at[here], sems.at[slot])
-
-        steps = total // stage.shape[1]
-
-        @pl.loop(0, steps)
+
+    @pl.when(inner == EXP_DEV * tiles - 1)
+    def _():
+        size = rows // 4
+
+        @pl.loop(0, 4)
         def _(b):
-            @pl.when(b >= 2)
-            def _():
-                copy(b - 2).wait()
-
-            here = row_chunk(b, stage.shape[1])
-            rank_low = rank_acc[here, :].astype(jnp.bfloat16)
-            rank_ref[here, :] = rank_low
-            slot = slot_acc[here, :] + dot_plain(rank_low, down_ref[...])
-            wide = gate_acc[here, :]
+            local = row_chunk(b, size)
+            there = pl.ds(pl.multiple_of(begin + b * size, size), size)
+            rank_low = rank_acc[local, :].astype(jnp.bfloat16)
+            rank_ref[there, :] = rank_low
+            slot = slot_acc[local, :] + dot_plain(rank_low, down_ref[...])
+            terms[there, :D] = slot.astype(jnp.bfloat16)
+            wide = gate_acc[local, :]
             high = wide.astype(jnp.bfloat16).astype(jnp.float32)
             both = high + pltpu.roll(wide - high, LANES // 2, 1)
-            stage[lax.rem(b, 2), :, :D] = slot.astype(jnp.bfloat16)
-            stage[lax.rem(b, 2), :, D:] = both.astype(jnp.bfloat16)
-            copy(b).start()
-
-        for b in range(steps - 2, steps):
-            copy(b).wait()
-
-
-def experts_backward(blocks, gates, ranks, down, lift, matrix_in, matrix_out, gate, up):
+            terms[there, D:] = both.astype(jnp.bfloat16)
+
+    @pl.when((q == 0) & (inner == EXP_DEV * tiles - 1))
+    def _():
+        for at in range(parts // 2):
+            for stream in streams:
+                send_first(*stream, at)
+
+    @pl.when((q == 1) & (inner == EXP_DEV * tiles - 3))
+    def _():
+        for stream in streams:
+            line, _, _ = where_to(stream[0], 1)
+
+            @pl.when(line == 1)
+            def _(stream=stream):
+                for n in range(2):
+                    pass_on(*stream, 1, n)
+
+    @pl.when((q == 1) & (inner == EXP_DEV * tiles - 1))
+    def _():
+        for at in range(1, parts - 1):
+            if at >= parts // 2:
+                for stream in streams:
+                    send_first(*stream, at)
+            for n in range(2):
+                for stream in streams:
+                    line, _, _ = where_to(stream[0], at)
+                    early = (line == 1) & (at == 1)
+
+                    @pl.when((line > 0) & (at >= line) & (line < parts - 1) & jnp.logical_not(early))
+                    def _(stream=stream, at=at, n=n):
+                        pass_on(*stream, at, n)
+
+        chunk = 16
+        last = parts - 2
+
+        @pl.loop(0, piece // chunk)
+        def _(r):
+            local = row_chunk(r, chunk)
+            there = pl.ds(pl.multiple_of(me * piece + r * chunk, chunk), chunk)
+            sum_ref[local, :] = terms[there, :].astype(jnp.float32)
+
+        for n in range(2):
+            for up, slot, send, recv in streams:
+                line, _, _ = where_to(up, 0)
+
+                @pl.when(line > 0)
+                def _(slot=slot, n=n, send=send, recv=recv):
+                    landed(slot, last, n, send, recv).wait_recv()
+
+                    @pl.loop(0, part // chunk)
+                    def _(r):
+                        local = pl.ds(pl.multiple_of(n * part + r * chunk, chunk), chunk)
+                        sum_ref[local, :] = sum_ref[local, :] + slot[last, local, :].astype(jnp.float32)
+
+        for up, slot, send, recv in streams:
+            line, _, _ = where_to(up, 0)
+            for at in range(parts - 1):
+                for n in range(2):
+
+                    @pl.when((at >= line) & (line < parts - 1))
+                    def _(slot=slot, at=at, n=n, send=send, recv=recv):
+                        landed(slot, at, n, send, recv).wait_send()
+
+
+def experts_backward(blocks, gates, ranks, down, lift, matrix_in, matrix_out, gate, up, cid):
     total, parts = gates.shape[0], len(blocks)
-    grad = pl.BlockSpec((1, RANK, TILE), lambda j, f: (j, 0, f))
-    kept = pl.BlockSpec((1, total, TILE), lambda j, f: (j, 0, f))
+    rows, piece, tiles = total // 2, total // parts, FF // TILE
+    once = dict(pipeline_mode=pl.Buffered(1))
+    sem = pltpu.SemaphoreType.DMA
+    weights = [
+        pl.BlockSpec((LANES, TILE), lambda q, j, f: (0, f)),
+        pl.BlockSpec((LANES, TILE), lambda q, j, f: (0, f + tiles)),
+        pl.BlockSpec((1, D, TILE), lambda q, j, f: (j, 0, f)),
+        pl.BlockSpec((1, D, TILE), lambda q, j, f: (j, 0, f + tiles)),
+        pl.BlockSpec((1, TILE, D), lambda q, j, f: (j, f, 0)),
+    ]
+    whole = lambda q, j, f: (0, 0)
     return pl.pallas_call(
         functools.partial(backward_kernel, parts),
-        grid=(EXP_DEV, FF // TILE),
-        in_specs=[VMEM] * 3 + weight_specs() + [kept, kept] + [ANY] * parts,
+        grid=(2, EXP_DEV, tiles),
+        in_specs=[VMEM] * 3 + weights + [ANY] * (2 + parts),
         out_specs=[
-            ANY,
-            pl.BlockSpec((total, LANES), lambda j, f: (0, 0), pipeline_mode=pl.Buffered(1)),
-            grad,
-            grad,
+            pl.BlockSpec((piece, D + LANES), whole, **once),
+            pl.BlockSpec((total, LANES), whole, **once),
+            pl.BlockSpec((LANES, 2 * FF), whole, **once),
         ],
         out_shape=[
-            jax.ShapeDtypeStruct((total, D + LANES), jnp.bfloat16),
+            jax.ShapeDtypeStruct((piece, D + LANES), jnp.float32),
             jax.ShapeDtypeStruct((total, LANES), jnp.bfloat16),
-            jax.ShapeDtypeStruct((EXP_DEV, RANK, FF), jnp.float32),
-            jax.ShapeDtypeStruct((EXP_DEV, RANK, FF), jnp.float32),
+            jax.ShapeDtypeStruct((LANES, 2 * FF), jnp.float32),
         ],
         scratch_shapes=[
             pltpu.VMEM((total, D), jnp.bfloat16),
-            pltpu.VMEM((total, D), jnp.float32),
-            pltpu.VMEM((total, LANES), jnp.float32),
-            pltpu.VMEM((total, LANES), jnp.float32),
-            pltpu.VMEM((2, LANES, TILE), jnp.float32),
-            pltpu.VMEM((2, 160, D + LANES), jnp.bfloat16),
-            pltpu.SemaphoreType.DMA((parts,)),
-        ],
-        compiler_params=EXPERT_PARAMS,
+            pltpu.VMEM((rows, D), jnp.float32),
+            pltpu.VMEM((rows, LANES), jnp.float32),
+            pltpu.VMEM((rows, LANES), jnp.float32),
+            pltpu.VMEM((total, D + LANES), jnp.bfloat16),
+            pltpu.VMEM((2, rows, TILE), jnp.bfloat16),
+            pltpu.VMEM((2, rows, TILE), jnp.bfloat16),
+            sem((parts,)),
+            sem((2, 2)),
+            pltpu.VMEM((parts - 1, piece, D + LANES), jnp.bfloat16),
+            pltpu.VMEM((parts - 1, piece, D + LANES), jnp.bfloat16),
+        ]
+        + [sem((parts - 1, 2))] * 4,
+        compiler_params=pltpu.CompilerParams(
+            dimension_semantics=("arbitrary",) * 3,
+            vmem_limit_bytes=60 * 1024 * 1024,
+            collective_id=cid,
+            has_side_effects=True,
+        ),
         cost_estimate=pl.CostEstimate(
-            flops=12 * EXP_DEV * total * D * FF,
+            flops=32 * EXP_DEV * total * D * FF,
             bytes_accessed=EXP_DEV * 6 * D * FF + 8 * total * D,
             transcendentals=EXP_DEV * total * FF,
         ),
@@ -1384,17 +1532,21 @@
     late, second_all = lax.optimization_barrier((cotangent, second_all))
     moved.update({s: shifted(late, s) for s in late_shifts})
     cotangents = [cotangent] + [moved[s] for s in range(1, parts)]
-    output_terms, ranks, gate, up = experts_forward(
+    output_left, output_right, ranks, gate, up = experts_forward(
         second_all, gates_all, pairs[0], pairs[1], matrix_in, matrix_out
     )
-    output_sum = lax.psum_scatter(output_terms, "expert", scatter_dimension=0, tiled=True)
-    slot_terms, rank_expert_grad, lift_gate_grad, lift_up_grad = experts_backward(
-        cotangents, gates_all, ranks, pairs[0], pairs[1], matrix_in, matrix_out, gate, up
-    )
-    slot_sum = line_reduce(slot_terms, 5, 2)
-    slot_sum, output_sum = lax.optimization_barrier((slot_sum, output_sum))
-
-    lift_sent = jnp.concatenate([lift_gate_grad, lift_up_grad], axis=2).reshape(EXP_DEV * RANK, D)
+    output_left = lax.psum_scatter(output_left, "expert", scatter_dimension=0, tiled=True)
+    slot_sum, rank_expert_grad, lift_expert_grad = experts_backward(
+        cotangents, gates_all, ranks, pairs[0], pairs[1], matrix_in, matrix_out, gate, up, 5
+    )
+    output_left, output_right, slot_sum = lax.optimization_barrier(
+        (output_left, output_right, slot_sum)
+    )
+    output_right = lax.psum_scatter(output_right, "expert", scatter_dimension=0, tiled=True)
+    output_sum = jnp.concatenate([output_left, output_right], axis=1)
+    layer_output = (middle + output_sum.astype(jnp.float32)).astype(low)
+
+    lift_sent = lift_expert_grad[: EXP_DEV * RANK]
     down_sent = dot_left(rank_expert_grad[:, : EXP_DEV * RANK], second_all)
     expert_sent = (
         jnp.concatenate([lift_sent, down_sent], axis=0)
@@ -1453,7 +1605,6 @@
         ],
         axis=1,
     ).astype(low)
-    first_terms, output_sum = lax.optimization_barrier((first_terms, output_sum))
     first_grad = lax.psum_scatter(first_terms, "expert", scatter_dimension=0, tiled=True).astype(jnp.float32)
     got = lax.all_to_all(owned, ("dp", "expert"), split_axis=0, concat_axis=0, tiled=True)
     inputs = tokens.astype(jnp.float32)
@@ -1478,7 +1629,6 @@
         route_rows,
         0,
     )
-    layer_output = (middle + output_sum.astype(jnp.float32)).astype(low)
     return (
         layer_output,
         input_grad,

time: 852 us -> 835 us (0.980)
  Pallas kernels: 626 us -> 611 us
    pallas_call x2 -> x1, Pallas kernels: 193 us -> 148 us  [experts_backward(): pl.pallas_call(functools.partial(backward_kernel, parts), grid=(2, EXP_DE...]
    pallas_call x1, Pallas kernels: 32.9 us -> 62.6 us  [run_attention_back(): pl.pallas_call(functools.partial(attention_back_kernel, parts), grid=(hea...]
  transfers between devices with their start and end apart: 12 -> 13, of which waited for: 4 -> 4; matrix products, arithmetic and copies ran while one was open for 7% -> 8% of each run, Pallas kernels for 67% -> 74%
where the time goes in v6:
time: 835 us; the launch traced here: 829 us
  Pallas kernels  611 us (73%)
  waiting for transfers between devices  84.3 us (10%)
  local copies, waits for them, and re-layouts  43.4 us (5%)
  starting transfers between devices  33.3 us (4%)
  other arithmetic  18.8 us (2%)
  matrix products  16.2 us (2%)
  between operations  15.7 us (2%)
    pallas_call x2, Pallas kernels, line_gather(): pl.pallas_call(functools.partial(gather_kernel, parts, pieces, n), out_sh...  176 us
    pallas_call x1, Pallas kernels, experts_backward(): pl.pallas_call(functools.partial(backward_kernel, parts), grid=(2, EXP_DE...  148 us
    pallas_call x1, Pallas kernels, experts_forward(): pl.pallas_call(forward_kernel, grid=(EXP_DEV, FF // TILE), in_specs=[VMEM...  87.2 us
    pallas_call x1, Pallas kernels, run_attention_back(): pl.pallas_call(functools.partial(attention_back_kernel, parts), grid=(hea...  62.6 us
    pallas_call x1, Pallas kernels, gather_weights(): pl.pallas_call(functools.partial(weights_kernel, parts), out_shape=[jax.S...  43.2 us
    pallas_call x1, Pallas kernels, run_attention(): pl.pallas_call(functools.partial(attention_kernel, parts), grid=(heads,),...  35.1 us
    reduce_scatter x1, waiting for transfers between devices, body(): lax.psum_scatter(first_terms, 'expert', scatter_dimension=0, tiled=True)  29.1 us
    all_to_all x1, waiting for transfers between devices, body(): lax.all_to_all(owned, ('dp', 'expert'), split_axis=0, concat_axis=0, tile...  22.9 us
  transfers between devices with their start and end apart: 13, of which 4 were waited for; matrix products, arithmetic and copies ran while one was open for 8% of the time, Pallas kernels for 74%

profile of v6, /device:TPU:9, one launch (start us, length us, event | category | flops | bytes accessed | tf_op | source)
XLA Modules:
  0.0 828.9 jit_solution(12577020488664153164)
XLA Ops:
  10.6 6.5 all-reduce.5
  19.7 5.7 all-to-all-start.1
  30.2 43.2 %gather_weights.1 = (bf16[256,3712]{1,0:T(8,128)(2,1)}, bf16[256,1024]{1,0:T(8,128)(2,1)}) custom-call(bf16[256,1536]{1,0:T(8,128)(2,1)} %bitcast.105, bf16[64,2048]{1,0:T(8,128)(2,1)} %out.1, bf16[64,128]{1,0:T(8,128)(2,1)} %fusion.24.small, bf16[64,1024]{1,0:T(8,128)(2,1)} %fusion.9.chosen), custom_call_target="tpu_custom_call" | custom-call | bytes 169738240 | tf_op jit(solution)/shard_map/gather_weights/pallas_call | solution.py:426
  75.4 5.8 all-to-all-start
  81.8 11.3 %all-to-all-done = bf16[8,256,128]{2,1,0:T(8,128)(2,1)S(1)} async-done(((bf16[8,256,128]{2,1,0:T(8,128)(2,1)}), bf16[8,256,128]{2,1,0:T(8,128)(2,1)S(1)}, u32[]{:S(2)}, u32[]{:S(2)}) %all-to-all-start) | async-done | bytes 524320 | tf_op jit(solution)/shard_map/all_to_all | solution.py:1469
  93.1 19.5 %all-gather.4.cloned.1.call-done.out_ref = bf16[4,1024,2048]{2,1,0:T(8,128)(2,1)} async-done(((bf16[4,128,2048]{2,1,0:T(8,128)(2,1)}), bf16[4,1024,2048]{2,1,0:T(8,128)(2,1)}) %all-gather.4.cloned.1.call-update) | async-done | bytes 16777232 | tf_op jit(solution)/shard_map/all_gather | solution.py:1421
  113.5 85.9 %line_gather_1.1.tokens_ref = bf16[1280,2048]{1,0:T(8,128)(2,1)} custom-call(bf16[320,2048]{1,0:T(8,128)(2,1)} %tokens_ref.1), custom_call_target="tpu_custom_call" | custom-call | bytes 367001600 | tf_op jit(solution)/shard_map/line_gather_1/pallas_call | solution.py:148
  214.3 17.9 %project_qkv.1 = (bf16[1280,2048]{1,0:T(8,128)(2,1)}, bf16[1280,16]{1,0:T(8,128)(2,1)}, bf16[1280,1536]{1,0:T(8,128)(2,1)}) custom-call(bf16[1280,2048]{1,0:T(8,128)(2,1)} %line_gather_1.1.tokens_ref, f32[1,2048]{1,0:T(1,128)} %get-tuple-element.119.gain_ref, bf16[16,2048]{1,0:T(8,128)(2,1)} %get-tuple-element.117.down_ref, bf16[16,1536]{1,0:T(8,128)(2,1)} %bitcast.129, ...), custom_call_target="tpu_custom_call" | custom-call | flops 8053063680 | bytes 27262976 | tf_op jit(solution)/shard_map/project_qkv/pallas_call | solution.py:1168
  232.2 35.1 %attention.1 = (bf16[320,2048]{1,0:T(8,128)(2,1)S(1)}, f32[4,1280,1]{2,1,0:T(8,128)S(1)}) custom-call(s32[1280,1]{1,0:T(8,128)S(1)} %reshape_select_fusion.column_ref, s32[1,1280]{1,0:T(1,128)S(1)} %compare_select_fusion.row_ref, bf16[1280,1536]{1,0:T(8,128)(2,1)} %get-tuple-element.65.query_ref.key_ref.value_ref, ...), custom_call_target="tpu_custom_call" | custom-call | bytes 131072000 | tf_op jit(solution)/shard_map/attention/pallas_call | solution.py:529
  270.0 12.7 %finish_attention.1 = (f32[320,2048]{1,0:T(8,128)}, bf16[320,16]{1,0:T(8,128)(2,1)}, f32[320,1]{1,0:T(8,128)}, bf16[320,2048]{1,0:T(8,128)(2,1)}, bf16[320,16]{1...) custom-call(bf16[320,2048]{1,0:T(8,128)(2,1)} %copy-done, bf16[320,2048]{1,0:T(8,128)(2,1)} %tokens_ref.1, ...), custom_call_target="tpu_custom_call" | custom-call | flops 2684354560 | bytes 16252928 | tf_op jit(solution)/shard_map/finish_attention/pallas_call | solution.py:1248
  282.7 90.5 %line_gather_4.1 = (bf16[1280,2048]{1,0:T(8,128)(2,1)}, bf16[1280,128]{1,0:T(8,128)(2,1)}) custom-call(bf16[320,2048]{1,0:T(8,128)(2,1)} %get-tuple-element.71.refs_0_, bf16[320,128]{1,0:T(8,128)(2,1)} %get-tuple-element.72.refs_1_), custom_call_target="tpu_custom_call" | custom-call | bytes 389939200 | tf_op jit(solution)/shard_map/line_gather_4/pallas_call | solution.py:148
  376.1 87.2 %experts_forward.1 = (bf16[1280,1024]{1,0:T(8,128)(2,1)}, bf16[1280,1024]{1,0:T(8,128)(2,1)}, bf16[1280,128]{1,0:T(8,128)(2,1)}, bf16[4,1280,1024]{2,1,0:T(8,128)(2,1)}, bf16[4,1280,1024]{2,1,0:T(8,128)(2,1)}) custom-call(bf16[1280,2048]{1,0:T(8,128)(2,1)} %get-tuple-element.74.rows_ref, bf16[1280,128]{1,0:T(8,128)(2,1)} %get-tuple-element.75.gates_ref, ...), custom_call_target="tpu_custom_call" | custom-call | flops 107374182400 | bytes 71303168 | tf_op jit(solution)/shard_map/experts_forward/pallas_call | solution.py:779
  464.5 147.5 %experts_backward.1 = (f32[320,2176]{1,0:T(8,128)}, bf16[1280,128]{1,0:T(8,128)(2,1)}, f32[128,2048]{1,0:T(8,128)}) custom-call(bf16[1280,128]{1,0:T(8,128)(2,1)} %get-tuple-element.75.gates_ref, bf16[1280,128]{1,0:T(8,128)(2,1)} %get-tuple-element.81.ranks_ref, bf16[128,2048]{1,0:T(8,128)(2,1)} %get-tuple-element.113.down_ref, ...), custom_call_target="tpu_custom_call" | custom-call | flops 343597383680 | bytes 71303168 | tf_op jit(solution)/shard_map/experts_backward/pallas_call | solution.py:1042
  612.3 12.7 %middle_backward.1 = (bf16[1280,512]{1,0:T(8,128)(2,1)}, f32[320,2048]{1,0:T(8,128)}, bf16[320,2048]{1,0:T(8,128)(2,1)}, bf16[320,128]{1,0:T(8,128)(2,1)}, bf16[...) custom-call(f32[320,2176]{1,0:T(8,128)} %get-tuple-element.89.slot_ref, f32[320,128]{1,0:T(8,128)} %get-tuple-element.90.probs_ref, ...), custom_call_target="tpu_custom_call" | custom-call | flops 2684354560 | bytes 24117248 | tf_op jit(solution)/shard_map/middle_backward/pallas_call | solution.py:1337
  626.3 62.6 %attention_back.1 = (bf16[1280,512]{1,0:T(8,128)(2,1)S(1)}, bf16[1280,512]{1,0:T(8,128)(2,1)S(1)}, bf16[1280,512]{1,0:T(8,128)(2,1)S(1)}) custom-call(s32[1280,1]{1,0:T(8,128)S(1)} %reshape_select_fusion.column_ref, s32[1,1280]{1,0:T(1,128)S(1)} %compare_select_fusion.row_ref, bf16[1280,1536]{1,0:T(8,128)(2,1)} %get-tuple-element.65.query_ref.key_ref.value_ref, ...), custom_call_target="tpu_custom_call" | custom-call | bytes 131072000 | tf_op jit(solution)/shard_map/attention_back/pallas_call | solution.py:643
  691.6 12.9 %first_products.1 = bf16[1280,2048]{1,0:T(8,128)(2,1)} custom-call(bf16[1280,512]{1,0:T(8,128)(2,1)S(1)} %get-tuple-element.95.query_ref, bf16[1280,512]{1,0:T(8,128)(2,1)S(1)} %get-tuple-element.96.key_ref, bf16[1280,512]{1,0:T(8,128)(2,1)S(1)} %get-tuple-element.97.value_ref, bf16[1280,16]{1,0:T(8,128)(2,1)S(1)} %convolution_convert_fusion.1.rank_ref, ...), custom_call_target="tpu_custom_call" | custom-call | flops 8053063680 | bytes 11534336 | tf_op jit(solution)/shard_map/first_products/pallas_call | solution.py:1125
  705.5 3.5 convolution_convert_fusion.2
  711.0 10.0 %all-to-all-start.3 = ((bf16[8,128,256]{2,1,0:T(8,128)(2,1)}), bf16[8,128,256]{2,1,0:T(8,128)(2,1)S(1)}, u32[]{:S(2)}, u32[]{:S(2)}) async-start(bf16[8,128,256]{2,1,0:T(8,128)(2,1)} %maximum_bitcast_fusion.1), calls=%async_computation.6 | async-start | bytes 1048576 | tf_op jit(solution)/shard_map/all_to_all | solution.py:1557
  736.7 3.3 convolution_convert_fusion.6
  744.0 7.2 all-to-all-start.2
  753.6 22.9 %all-to-all-done.2 = bf16[32,2,3712]{2,1,0:T(2,128)(2,1)S(1)} async-done(((bf16[32,2,3712]{2,1,0:T(2,128)(2,1)}), bf16[32,2,3712]{2,1,0:T(2,128)(2,1)S(1)}, u32[]{:S(2)}, u32[]{:S(2)}) %all-to-all-start.2) | async-done | bytes 475168 | tf_op jit(solution)/shard_map/all_to_all | solution.py:1609
  783.6 3.4 add_convert_fusion
  787.0 29.1 %reduce-scatter.8.cloned.1.call-done = bf16[320,2048]{1,0:T(8,128)(2,1)} async-done(((bf16[1280,2048]{1,0:T(8,128)(2,1)}), bf16[320,2048]{1,0:T(8,128)(2,1)}) %reduce-scatter.8.cloned.1.call-update) | async-done | bytes 1310736 | tf_op jit(solution)/shard_map/reduce_scatter | solution.py:1608
  818.2 3.6 fusion.5
  (190 shorter events, 73.1 us)
Async XLA Ops:
  7.2 105.5 %all-gather.4.cloned.1.call-start = ((), (), s32[]{:S(2)}) async-start(), calls=%async_computation.7 | async-start | bytes 18874368 | tf_op jit(solution)/shard_map/all_gather | solution.py:1421
  17.0 11.6 %copy-start.24 = (s32[8]{0:T(128)}, s32[8]{0:T(128)S(1)}, u32[]{:S(2)}) copy-start(s32[8]{0:T(128)S(1)} %all-reduce.5) | copy-start | bytes 100
  19.7 55.7 %all-to-all-start.1 = ((bf16[8,128,256]{2,1,0:T(8,128)(2,1)}), bf16[8,128,256]{2,1,0:T(8,128)(2,1)S(1)}, u32[]{:S(2)}, u32[]{:S(2)}) async-start(bf16[8,128,256]{2,1,0:T(8,128)(2,1)} %copy.100), calls=%async_computation.1 | async-start | bytes 1048576 | tf_op jit(solution)/shard_map/all_to_all | solution.py:1430
  75.4 17.7 %all-to-all-start = ((bf16[8,256,128]{2,1,0:T(8,128)(2,1)}), bf16[8,256,128]{2,1,0:T(8,128)(2,1)S(1)}, u32[]{:S(2)}, u32[]{:S(2)}) async-start(bf16[8,256,128]{2,1,0:T(8,128)(2,1)} %bitcast_bitcast_fusion), calls=%async_computation | async-start | bytes 1048576 | tf_op jit(solution)/shard_map/all_to_all | solution.py:1469
  81.1 123.6 %all-gather.6.cloned.1.call-start = ((), (), s32[]{:S(2)}) async-start(), calls=%async_computation.8 | async-start | bytes 17104896 | tf_op jit(solution)/shard_map/all_gather | solution.py:1479
  93.1 20.3 %copy-start.9 = (bf16[8,256,128]{2,1,0:T(8,128)(2,1)}, bf16[8,256,128]{2,1,0:T(8,128)(2,1)S(1)}, u32[]{:S(2)}) copy-start(bf16[8,256,128]{2,1,0:T(8,128)(2,1)S(1)} %all-to-all-done) | copy-start | bytes 1572868
  112.6 263.4 %all-gather.8.cloned.1.call-start = ((), (), s32[]{:S(2)}) async-start(), calls=%async_computation.9 | async-start | bytes 37748736 | tf_op jit(solution)/shard_map/all_gather | solution.py:1481
  113.4 86.0 %copy-start.10 = (bf16[320,2048]{1,0:T(8,128)(2,1)S(1)}, bf16[320,2048]{1,0:T(8,128)(2,1)}, u32[]{:S(2)}) copy-start(bf16[320,2048]{1,0:T(8,128)(2,1)} %cotangent_ref.1) | copy-start | bytes 3932164
  113.4 87.4 %copy-start.23 = (s32[320,8]{0,1:T(8,128)S(1)}, s32[320,8]{0,1:T(8,128)}, u32[]{:S(2)}) copy-start(s32[320,8]{0,1:T(8,128)} %param.31) | copy-start | bytes 30724
  113.4 90.0 %copy-start.32 = (s32[1,8]{1,0:T(1,128)S(1)}, s32[1,8]{1,0:T(1,128)}, u32[]{:S(2)}) copy-start(s32[1,8]{1,0:T(1,128)} %param.33) | copy-start | bytes 100
  113.4 498.6 %reduce-scatter.4.cloned.1.call-start = ((), (), s32[]{:S(2)}) async-start(), calls=%async_computation.10 | async-start | bytes 3276800 | tf_op jit(solution)/shard_map/reduce_scatter | solution.py:1538
  199.4 83.3 %collective-permute-start = (bf16[320,2048]{1,0:T(8,128)(2,1)S(1)}, bf16[320,2048]{1,0:T(8,128)(2,1)}, u32[]{:S(2)}, u32[]{:S(2)}) collective-permute-start(bf16[320,2048]{1,0:T(8,128)(2,1)S(1)} %copy-done.10), channel_id=1, source_target_pairs={{0,1},{1,2},{2,3},{3,0},{4,5},{5,6},{6,7},{7,4},{8,9},{9,10},{10,1... | collective-permute-start | bytes 3932168 | tf_op jit(solution)/shard_map/ppermute | solution.py:1501
  373.2 90.2 %collective-permute-start.1 = (bf16[320,2048]{1,0:T(8,128)(2,1)S(1)}, bf16[320,2048]{1,0:T(8,128)(2,1)S(1)}, u32[]{:S(2)}, u32[]{:S(2)}) collective-permute-start(bf16[320,2048]{1,0:T(8,128)(2,1)S(1)} %copy-done.10), channel_id=1, source_target_pairs={{0,2},{1,3},{2,0},{3,1},{4,6},{5,7},{6,4},{7,5},{8,10},{9,11},{10,... | collective-permute-start | bytes 3932168 | tf_op jit(solution)/shard_map/ppermute | solution.py:1501
  375.6 87.8 %collective-permute-start.2 = (bf16[320,2048]{1,0:T(8,128)(2,1)S(1)}, bf16[320,2048]{1,0:T(8,128)(2,1)}, u32[]{:S(2)}, u32[]{:S(2)}) collective-permute-start(bf16[320,2048]{1,0:T(8,128)(2,1)S(1)} %copy-done.10), channel_id=1, source_target_pairs={{0,3},{1,0},{2,1},{3,2},{4,7},{5,4},{6,5},{7,6},{8,11},{9,8},{10,9... | collective-permute-start | bytes 3932168 | tf_op jit(solution)/shard_map/ppermute | solution.py:1501
  463.3 320.2 %reduce-scatter.6.cloned.1.call-start = ((), (), s32[]{:S(2)}) async-start(), calls=%async_computation.11 | async-start | bytes 3276800 | tf_op jit(solution)/shard_map/reduce_scatter | solution.py:1545
  612.0 204.0 %reduce-scatter.8.cloned.1.call-start = ((), (), s32[]{:S(2)}) async-start(), calls=%async_computation.12 | async-start | bytes 6553600 | tf_op jit(solution)/shard_map/reduce_scatter | solution.py:1608
  709.0 12.1 %copy-start.15 = (bf16[1280,16]{1,0:T(8,128)(2,1)S(1)}, bf16[1280,16]{1,0:T(8,128)(2,1)}, u32[]{:S(2)}) copy-start(bf16[1280,16]{1,0:T(8,128)(2,1)} %get-tuple-element.103) | copy-start | bytes 122884
  711.0 32.9 %all-to-all-start.3 = ((bf16[8,128,256]{2,1,0:T(8,128)(2,1)}), bf16[8,128,256]{2,1,0:T(8,128)(2,1)S(1)}, u32[]{:S(2)}, u32[]{:S(2)}) async-start(bf16[8,128,256]{2,1,0:T(8,128)(2,1)} %maximum_bitcast_fusion.1), calls=%async_computation.6 | async-start | bytes 1048576 | tf_op jit(solution)/shard_map/all_to_all | solution.py:1557
  721.1 12.7 %copy-start.7 = (bf16[320,2048]{1,0:T(8,128)(2,1)S(1)}, bf16[320,2048]{1,0:T(8,128)(2,1)}, u32[]{:S(2)}) copy-start(bf16[320,2048]{1,0:T(8,128)(2,1)} %get-tuple-element.71.refs_0_) | copy-start | bytes 3932164
  724.0 11.2 %copy-start.1 = (bf16[320,2048]{1,0:T(8,128)(2,1)S(1)}, bf16[320,2048]{1,0:T(8,128)(2,1)}, u32[]{:S(2)}) copy-start(bf16[320,2048]{1,0:T(8,128)(2,1)} %copy-done) | copy-start | bytes 3932164
  724.6 11.7 %copy-start.17 = (bf16[320,16]{1,0:T(8,128)(2,1)S(1)}, bf16[320,16]{1,0:T(8,128)(2,1)}, u32[]{:S(2)}) copy-start(bf16[320,16]{1,0:T(8,128)(2,1)} %get-tuple-element.101) | copy-start | bytes 30724
  744.0 32.5 %all-to-all-start.2 = ((bf16[32,2,3712]{2,1,0:T(2,128)(2,1)}), bf16[32,2,3712]{2,1,0:T(2,128)(2,1)S(1)}, u32[]{:S(2)}, u32[]{:S(2)}) async-start(bf16[32,2,3712]{2,1,0:T(2,128)(2,1)} %reshape.426), calls=%async_computation.5 | async-start | bytes 950272 | tf_op jit(solution)/shard_map/all_to_all | solution.py:1609
  783.6 32.5 %copy-start.5 = (bf16[320,2048]{1,0:T(8,128)(2,1)S(1)}, bf16[320,2048]{1,0:T(8,128)(2,1)}, u32[]{:S(2)}) copy-start(bf16[320,2048]{1,0:T(8,128)(2,1)} %tokens_ref.1) | copy-start | bytes 3932164
  783.6 32.5 %copy-start.20 = (f32[1,2048]{1,0:T(1,128)S(1)}, f32[1,2048]{1,0:T(1,128)}, u32[]{:S(2)}) copy-start(f32[1,2048]{1,0:T(1,128)} %get-tuple-element.119.gain_ref) | copy-start | bytes 24580
  (23 other events, 60.1 us)
Sparse Core Ops, SparseCore 0:
  9.9 102.6 all-gather.3
  114.5 83.1 all-gather.5
  199.7 160.7 all-gather.7
  463.5 53.9 reduce-scatter.3
  612.2 82.6 reduce-scatter.5
  704.7 111.3 reduce-scatter.7

commit v7 on v6

--- a/solution.py
+++ b/solution.py
@@ -1473,8 +1473,14 @@
         concat_axis=0,
         tiled=True,
     ).reshape(D, LANES)
-    dense_line, expert_input, matrix_out, chosen_all, pairs = lax.optimization_barrier(
-        (dense_line, expert_input, matrix_out, chosen_all, pairs)
+    def shifted(array, by):
+        return lax.ppermute(array, "expert", [(i, (i + by) % parts) for i in range(parts)])
+
+    there = chosen_line[0, 0]
+    late_shifts = list(range(2, parts))
+    moved = {1: shifted(jnp.where(there == there, cotangent, 0), 1)}
+    dense_line, expert_input, matrix_out, chosen_all, pairs, moved[1] = lax.optimization_barrier(
+        (dense_line, expert_input, matrix_out, chosen_all, pairs, moved[1])
     )
     dense_all = lax.all_gather(dense_line, "dp", axis=0, tiled=True)
     (tokens_all,) = line_gather([tokens], 1, 2)
@@ -1497,13 +1503,6 @@
     )
     lift_route = jnp.pad(lift_route, ((0, 0), (0, LANES - experts)))
     routed = jnp.any(routes[:, :, None] == jnp.arange(LANES, dtype=jnp.int32), axis=1).astype(jnp.float32)
-    def shifted(array, by):
-        return lax.ppermute(array, "expert", [(i, (i + by) % parts) for i in range(parts)])
-
-    early, tokens_all = lax.optimization_barrier((cotangent, tokens_all))
-    early_shifts, late_shifts = [1], list(range(2, parts))
-    moved = {s: shifted(early, s) for s in early_shifts}
-
     normed_low, rank_query, qkv_low = project_qkv(
         tokens_all, gain_rows[0:1], down_query, lift_query, dense_all
     )
@@ -1524,9 +1523,6 @@
         routed,
         dense_all,
     )
-    held = lax.optimization_barrier([second_low] + [moved[s] for s in early_shifts])
-    second_low = held[0]
-    moved.update(zip(early_shifts, held[1:]))
     second_all, gates_all = line_gather([second_low, gates], 4, 2)
 
     late, second_all = lax.optimization_barrier((cotangent, second_all))

time: 835 us -> 833 us (level)
    all_gather x1, waiting for transfers between devices: 19.5 us -> 5.8 us  [body(): matrix_out = lax.all_gather(expert_output, 'dp', axis=1, tiled=True)]
    all_to_all x1, waiting for transfers between devices: 0.01 us -> 11.1 us  [body(): lax.all_to_all(pairs.reshape(groups, 2 * EXP_DEV * RANK, adapter_cols), '...]
  transfers between devices with their start and end apart: 13 -> 13, of which waited for: 4 -> 5; matrix products, arithmetic and copies ran while one was open for 8% -> 8% of each run, Pallas kernels for 74% -> 74%
where the time goes in v7:
time: 833 us; the launch traced here: 828 us
  Pallas kernels  610 us (73%)
  waiting for transfers between devices  81.6 us (10%)
  local copies, waits for them, and re-layouts  42.5 us (5%)
  starting transfers between devices  34.6 us (4%)
  other arithmetic  18.9 us (2%)
  between operations  17.1 us (2%)
  matrix products  16.2 us (2%)
    pallas_call x2, Pallas kernels, line_gather(): pl.pallas_call(functools.partial(gather_kernel, parts, pieces, n), out_sh...  177 us
    pallas_call x1, Pallas kernels, experts_backward(): pl.pallas_call(functools.partial(backward_kernel, parts), grid=(2, EXP_DE...  148 us
    pallas_call x1, Pallas kernels, experts_forward(): pl.pallas_call(forward_kernel, grid=(EXP_DEV, FF // TILE), in_specs=[VMEM...  87.2 us
    pallas_call x1, Pallas kernels, run_attention_back(): pl.pallas_call(functools.partial(attention_back_kernel, parts), grid=(hea...  64.5 us
    pallas_call x1, Pallas kernels, gather_weights(): pl.pallas_call(functools.partial(weights_kernel, parts), out_shape=[jax.S...  38.6 us
    pallas_call x1, Pallas kernels, run_attention(): pl.pallas_call(functools.partial(attention_kernel, parts), grid=(heads,),...  35.3 us
    reduce_scatter x1, waiting for transfers between devices, body(): lax.psum_scatter(first_terms, 'expert', scatter_dimension=0, tiled=True)  29.1 us
    all_to_all x1, waiting for transfers between devices, body(): lax.all_to_all(owned, ('dp', 'expert'), split_axis=0, concat_axis=0, tile...  22.9 us
  transfers between devices with their start and end apart: 13, of which 5 were waited for; matrix products, arithmetic and copies ran while one was open for 8% of the time, Pallas kernels for 74%

profile of v7, /device:TPU:9, one launch (start us, length us, event | category | flops | bytes accessed | tf_op | source)
XLA Modules:
  0.0 827.6 jit_solution(4757138150054814432)
XLA Ops:
  10.6 6.5 all-reduce.5
  21.9 38.6 %gather_weights.1 = (bf16[256,3712]{1,0:T(8,128)(2,1)}, bf16[256,1024]{1,0:T(8,128)(2,1)}) custom-call(bf16[256,1536]{1,0:T(8,128)(2,1)} %bitcast.106, bf16[64,2048]{1,0:T(8,128)(2,1)} %out.1, bf16[64,128]{1,0:T(8,128)(2,1)} %fusion.24.small, bf16[64,1024]{1,0:T(8,128)(2,1)} %fusion.9.chosen), custom_call_target="tpu_custom_call" | custom-call | bytes 169738240 | tf_op jit(solution)/shard_map/gather_weights/pallas_call | solution.py:426
  66.9 8.8 %all-to-all-start.1 = ((bf16[8,128,256]{2,1,0:T(8,128)(2,1)}), bf16[8,128,256]{2,1,0:T(8,128)(2,1)S(1)}, u32[]{:S(2)}, u32[]{:S(2)}) async-start(bf16[8,128,256]{2,1,0:T(8,128)(2,1)} %copy.100), calls=%async_computation.1 | async-start | bytes 1048576 | tf_op jit(solution)/shard_map/all_to_all | solution.py:1430
  76.5 11.1 %all-to-all-done.1 = bf16[8,128,256]{2,1,0:T(8,128)(2,1)S(1)} async-done(((bf16[8,128,256]{2,1,0:T(8,128)(2,1)}), bf16[8,128,256]{2,1,0:T(8,128)(2,1)S(1)}, u32[]{:S(2)}, u32[]{:S(2)}) %all-to-all-start.1) | async-done | bytes 524320 | tf_op jit(solution)/shard_map/all_to_all | solution.py:1430
  87.6 7.2 all-to-all-start
  95.4 11.3 %all-to-all-done = bf16[8,256,128]{2,1,0:T(8,128)(2,1)S(1)} async-done(((bf16[8,256,128]{2,1,0:T(8,128)(2,1)}), bf16[8,256,128]{2,1,0:T(8,128)(2,1)S(1)}, u32[]{:S(2)}, u32[]{:S(2)}) %all-to-all-start) | async-done | bytes 524320 | tf_op jit(solution)/shard_map/all_to_all | solution.py:1469
  106.7 5.8 all-gather.4.cloned.1.call-done.out_ref
  113.4 85.3 %line_gather_1.1.tokens_ref = bf16[1280,2048]{1,0:T(8,128)(2,1)} custom-call(bf16[320,2048]{1,0:T(8,128)(2,1)} %tokens_ref.1), custom_call_target="tpu_custom_call" | custom-call | bytes 367001600 | tf_op jit(solution)/shard_map/line_gather_1/pallas_call | solution.py:148
  212.0 18.6 %project_qkv.1 = (bf16[1280,2048]{1,0:T(8,128)(2,1)}, bf16[1280,16]{1,0:T(8,128)(2,1)}, bf16[1280,1536]{1,0:T(8,128)(2,1)}) custom-call(bf16[1280,2048]{1,0:T(8,128)(2,1)} %line_gather_1.1.tokens_ref, f32[1,2048]{1,0:T(1,128)} %get-tuple-element.113.gain_ref, bf16[16,2048]{1,0:T(8,128)(2,1)} %get-tuple-element.111.down_ref, bf16[16,1536]{1,0:T(8,128)(2,1)} %bitcast.130, ...), custom_call_target="tpu_custom_call" | custom-call | flops 8053063680 | bytes 27262976 | tf_op jit(solution)/shard_map/project_qkv/pallas_call | solution.py:1168
  230.7 35.3 %attention.1 = (bf16[320,2048]{1,0:T(8,128)(2,1)S(1)}, f32[4,1280,1]{2,1,0:T(8,128)S(1)}) custom-call(s32[1280,1]{1,0:T(8,128)S(1)} %reshape_select_fusion.column_ref, s32[1,1280]{1,0:T(1,128)S(1)} %compare_select_fusion.row_ref, bf16[1280,1536]{1,0:T(8,128)(2,1)} %get-tuple-element.61.query_ref.key_ref.value_ref, ...), custom_call_target="tpu_custom_call" | custom-call | bytes 131072000 | tf_op jit(solution)/shard_map/attention/pallas_call | solution.py:529
  268.7 13.0 %finish_attention.1 = (f32[320,2048]{1,0:T(8,128)}, bf16[320,16]{1,0:T(8,128)(2,1)}, f32[320,1]{1,0:T(8,128)}, bf16[320,2048]{1,0:T(8,128)(2,1)}, bf16[320,16]{1...) custom-call(bf16[320,2048]{1,0:T(8,128)(2,1)} %copy-done, bf16[320,2048]{1,0:T(8,128)(2,1)} %tokens_ref.1, ...), custom_call_target="tpu_custom_call" | custom-call | flops 2684354560 | bytes 16252928 | tf_op jit(solution)/shard_map/finish_attention/pallas_call | solution.py:1248
  281.8 91.6 %line_gather_4.1 = (bf16[1280,2048]{1,0:T(8,128)(2,1)}, bf16[1280,128]{1,0:T(8,128)(2,1)}) custom-call(bf16[320,2048]{1,0:T(8,128)(2,1)} %get-tuple-element.65.refs_0_, bf16[320,128]{1,0:T(8,128)(2,1)} %get-tuple-element.66.refs_1_), custom_call_target="tpu_custom_call" | custom-call | bytes 389939200 | tf_op jit(solution)/shard_map/line_gather_4/pallas_call | solution.py:148
  376.1 87.2 %experts_forward.1 = (bf16[1280,1024]{1,0:T(8,128)(2,1)}, bf16[1280,1024]{1,0:T(8,128)(2,1)}, bf16[1280,128]{1,0:T(8,128)(2,1)}, bf16[4,1280,1024]{2,1,0:T(8,128)(2,1)}, bf16[4,1280,1024]{2,1,0:T(8,128)(2,1)}) custom-call(bf16[1280,2048]{1,0:T(8,128)(2,1)} %get-tuple-element.68.rows_ref, bf16[1280,128]{1,0:T(8,128)(2,1)} %get-tuple-element.69.gates_ref, ...), custom_call_target="tpu_custom_call" | custom-call | flops 107374182400 | bytes 71303168 | tf_op jit(solution)/shard_map/experts_forward/pallas_call | solution.py:779
  463.4 148.1 %experts_backward.1 = (f32[320,2176]{1,0:T(8,128)}, bf16[1280,128]{1,0:T(8,128)(2,1)}, f32[128,2048]{1,0:T(8,128)}) custom-call(bf16[1280,128]{1,0:T(8,128)(2,1)} %get-tuple-element.69.gates_ref, bf16[1280,128]{1,0:T(8,128)(2,1)} %get-tuple-element.75.ranks_ref, bf16[128,2048]{1,0:T(8,128)(2,1)} %get-tuple-element.107.down_ref, ...), custom_call_target="tpu_custom_call" | custom-call | flops 343597383680 | bytes 71303168 | tf_op jit(solution)/shard_map/experts_backward/pallas_call | solution.py:1042
  611.7 12.8 %middle_backward.1 = (bf16[1280,512]{1,0:T(8,128)(2,1)}, f32[320,2048]{1,0:T(8,128)}, bf16[320,2048]{1,0:T(8,128)(2,1)}, bf16[320,128]{1,0:T(8,128)(2,1)}, bf16[...) custom-call(f32[320,2176]{1,0:T(8,128)} %get-tuple-element.83.slot_ref, f32[320,128]{1,0:T(8,128)} %get-tuple-element.84.probs_ref, ...), custom_call_target="tpu_custom_call" | custom-call | flops 2684354560 | bytes 24117248 | tf_op jit(solution)/shard_map/middle_backward/pallas_call | solution.py:1337
  625.9 64.5 %attention_back.1 = (bf16[1280,512]{1,0:T(8,128)(2,1)S(1)}, bf16[1280,512]{1,0:T(8,128)(2,1)S(1)}, bf16[1280,512]{1,0:T(8,128)(2,1)S(1)}) custom-call(s32[1280,1]{1,0:T(8,128)S(1)} %reshape_select_fusion.column_ref, s32[1,1280]{1,0:T(1,128)S(1)} %compare_select_fusion.row_ref, bf16[1280,1536]{1,0:T(8,128)(2,1)} %get-tuple-element.61.query_ref.key_ref.value_ref, ...), custom_call_target="tpu_custom_call" | custom-call | bytes 131072000 | tf_op jit(solution)/shard_map/attention_back/pallas_call | solution.py:643
  693.1 12.9 %first_products.1 = bf16[1280,2048]{1,0:T(8,128)(2,1)} custom-call(bf16[1280,512]{1,0:T(8,128)(2,1)S(1)} %get-tuple-element.89.query_ref, bf16[1280,512]{1,0:T(8,128)(2,1)S(1)} %get-tuple-element.90.key_ref, bf16[1280,512]{1,0:T(8,128)(2,1)S(1)} %get-tuple-element.91.value_ref, bf16[1280,16]{1,0:T(8,128)(2,1)S(1)} %convolution_convert_fusion.1.rank_ref, ...), custom_call_target="tpu_custom_call" | custom-call | flops 8053063680 | bytes 11534336 | tf_op jit(solution)/shard_map/first_products/pallas_call | solution.py:1125
  707.0 3.5 convolution_convert_fusion.2
  712.5 7.2 all-to-all-start.3
  742.6 7.2 all-to-all-start.2
  752.3 22.9 %all-to-all-done.2 = bf16[32,2,3712]{2,1,0:T(2,128)(2,1)S(1)} async-done(((bf16[32,2,3712]{2,1,0:T(2,128)(2,1)}), bf16[32,2,3712]{2,1,0:T(2,128)(2,1)S(1)}, u32[]{:S(2)}, u32[]{:S(2)}) %all-to-all-start.2) | async-done | bytes 475168 | tf_op jit(solution)/shard_map/all_to_all | solution.py:1605
  782.3 3.4 add_convert_fusion
  785.7 29.1 %reduce-scatter.8.cloned.1.call-done = bf16[320,2048]{1,0:T(8,128)(2,1)} async-done(((bf16[1280,2048]{1,0:T(8,128)(2,1)}), bf16[320,2048]{1,0:T(8,128)(2,1)}) %reduce-scatter.8.cloned.1.call-update) | async-done | bytes 1310736 | tf_op jit(solution)/shard_map/reduce_scatter | solution.py:1604
  816.9 3.6 fusion.5
  (196 shorter events, 75.2 us)
Async XLA Ops:
  7.2 105.4 %all-gather.4.cloned.1.call-start = ((), (), s32[]{:S(2)}) async-start(), calls=%async_computation.7 | async-start | bytes 18874368 | tf_op jit(solution)/shard_map/all_gather | solution.py:1421
  17.0 48.6 %copy-start.27 = (s32[8]{0:T(128)}, s32[8]{0:T(128)S(1)}, u32[]{:S(2)}) copy-start(s32[8]{0:T(128)S(1)} %all-reduce.5) | copy-start | bytes 100
  18.1 44.8 %copy-start.7 = (bf16[320,2048]{1,0:T(8,128)(2,1)S(1)}, bf16[320,2048]{1,0:T(8,128)(2,1)}, u32[]{:S(2)}) copy-start(bf16[320,2048]{1,0:T(8,128)(2,1)} %cotangent_ref.1) | copy-start | bytes 3932164
  20.4 44.8 %copy-start.18 = (bf16[4,8,16,256]{3,2,1,0:T(8,128)(2,1)S(1)}, bf16[4,8,16,256]{3,2,1,0:T(8,128)(2,1)}, u32[]{:S(2)}) copy-start(bf16[4,8,16,256]{3,2,1,0:T(8,128)(2,1)} %param.30) | copy-start | bytes 786436
  20.4 44.8 %copy-start.19 = (bf16[4,256,8,16]{1,3,2,0:T(8,128)(2,1)S(1)}, bf16[4,256,8,16]{1,3,2,0:T(8,128)(2,1)}, u32[]{:S(2)}) copy-start(bf16[4,256,8,16]{1,3,2,0:T(8,128)(2,1)} %param.29) | copy-start | bytes 786436
  64.1 42.6 %collective-permute-start = (bf16[320,2048]{1,0:T(8,128)(2,1)}, bf16[320,2048]{1,0:T(8,128)(2,1)}, u32[]{:S(2)}, u32[]{:S(2)}) collective-permute-start(bf16[320,2048]{1,0:T(8,128)(2,1)} %broadcast_select_fusion), channel_id=1, source_target_pairs={{0,1},{1,2},{2,3},{3,0},{4,5},{5,6},{6,7},{7,4},{8,9},{9,10},{10,1... | collective-permute-start | bytes 3932168 | tf_op jit(solution)/shard_map/ppermute | solution.py:1477
  66.9 20.7 %all-to-all-start.1 = ((bf16[8,128,256]{2,1,0:T(8,128)(2,1)}), bf16[8,128,256]{2,1,0:T(8,128)(2,1)S(1)}, u32[]{:S(2)}, u32[]{:S(2)}) async-start(bf16[8,128,256]{2,1,0:T(8,128)(2,1)} %copy.100), calls=%async_computation.1 | async-start | bytes 1048576 | tf_op jit(solution)/shard_map/all_to_all | solution.py:1430
  87.6 19.1 %all-to-all-start = ((bf16[8,256,128]{2,1,0:T(8,128)(2,1)}), bf16[8,256,128]{2,1,0:T(8,128)(2,1)S(1)}, u32[]{:S(2)}, u32[]{:S(2)}) async-start(bf16[8,256,128]{2,1,0:T(8,128)(2,1)} %bitcast_bitcast_fusion), calls=%async_computation | async-start | bytes 1048576 | tf_op jit(solution)/shard_map/all_to_all | solution.py:1469
  94.8 107.8 %all-gather.6.cloned.1.call-start = ((), (), s32[]{:S(2)}) async-start(), calls=%async_computation.8 | async-start | bytes 17104896 | tf_op jit(solution)/shard_map/all_gather | solution.py:1485
  112.6 263.5 %all-gather.8.cloned.1.call-start = ((), (), s32[]{:S(2)}) async-start(), calls=%async_computation.9 | async-start | bytes 37748736 | tf_op jit(solution)/shard_map/all_gather | solution.py:1487
  113.3 85.4 %copy-start.26 = (s32[320,8]{0,1:T(8,128)S(1)}, s32[320,8]{0,1:T(8,128)}, u32[]{:S(2)}) copy-start(s32[320,8]{0,1:T(8,128)} %param.31) | copy-start | bytes 30724
  113.3 87.9 %copy-start.34 = (s32[1,8]{1,0:T(1,128)S(1)}, s32[1,8]{1,0:T(1,128)}, u32[]{:S(2)}) copy-start(s32[1,8]{1,0:T(1,128)} %param.33) | copy-start | bytes 100
  113.3 498.1 %reduce-scatter.4.cloned.1.call-start = ((), (), s32[]{:S(2)}) async-start(), calls=%async_computation.10 | async-start | bytes 3276800 | tf_op jit(solution)/shard_map/reduce_scatter | solution.py:1534
  373.3 90.0 %collective-permute-start.1 = (bf16[320,2048]{1,0:T(8,128)(2,1)S(1)}, bf16[320,2048]{1,0:T(8,128)(2,1)}, u32[]{:S(2)}, u32[]{:S(2)}) collective-permute-start(bf16[320,2048]{1,0:T(8,128)(2,1)S(1)} %copy-done.7), channel_id=1, source_target_pairs={{0,2},{1,3},{2,0},{3,1},{4,6},{5,7},{6,4},{7,5},{8,10},{9,11},{10,... | collective-permute-start | bytes 3932168 | tf_op jit(solution)/shard_map/ppermute | solution.py:1477
  374.1 89.2 %collective-permute-start.2 = (bf16[320,2048]{1,0:T(8,128)(2,1)S(1)}, bf16[320,2048]{1,0:T(8,128)(2,1)}, u32[]{:S(2)}, u32[]{:S(2)}) collective-permute-start(bf16[320,2048]{1,0:T(8,128)(2,1)S(1)} %copy-done.7), channel_id=1, source_target_pairs={{0,3},{1,0},{2,1},{3,2},{4,7},{5,4},{6,5},{7,6},{8,11},{9,8},{10,9... | collective-permute-start | bytes 3932168 | tf_op jit(solution)/shard_map/ppermute | solution.py:1477
  463.3 319.0 %reduce-scatter.6.cloned.1.call-start = ((), (), s32[]{:S(2)}) async-start(), calls=%async_computation.11 | async-start | bytes 3276800 | tf_op jit(solution)/shard_map/reduce_scatter | solution.py:1541
  611.5 203.3 %reduce-scatter.8.cloned.1.call-start = ((), (), s32[]{:S(2)}) async-start(), calls=%async_computation.12 | async-start | bytes 6553600 | tf_op jit(solution)/shard_map/reduce_scatter | solution.py:1604
  712.5 30.1 %all-to-all-start.3 = ((bf16[8,128,256]{2,1,0:T(8,128)(2,1)}), bf16[8,128,256]{2,1,0:T(8,128)(2,1)S(1)}, u32[]{:S(2)}, u32[]{:S(2)}) async-start(bf16[8,128,256]{2,1,0:T(8,128)(2,1)} %maximum_bitcast_fusion.1), calls=%async_computation.6 | async-start | bytes 1048576 | tf_op jit(solution)/shard_map/all_to_all | solution.py:1553
  719.8 12.7 %copy-start.8 = (bf16[320,2048]{1,0:T(8,128)(2,1)S(1)}, bf16[320,2048]{1,0:T(8,128)(2,1)}, u32[]{:S(2)}) copy-start(bf16[320,2048]{1,0:T(8,128)(2,1)} %get-tuple-element.65.refs_0_) | copy-start | bytes 3932164
  722.6 11.2 %copy-start.1 = (bf16[320,2048]{1,0:T(8,128)(2,1)S(1)}, bf16[320,2048]{1,0:T(8,128)(2,1)}, u32[]{:S(2)}) copy-start(bf16[320,2048]{1,0:T(8,128)(2,1)} %copy-done) | copy-start | bytes 3932164
  723.3 11.7 %copy-start.20 = (bf16[320,16]{1,0:T(8,128)(2,1)S(1)}, bf16[320,16]{1,0:T(8,128)(2,1)}, u32[]{:S(2)}) copy-start(bf16[320,16]{1,0:T(8,128)(2,1)} %get-tuple-element.95) | copy-start | bytes 30724
  742.6 32.5 %all-to-all-start.2 = ((bf16[32,2,3712]{2,1,0:T(2,128)(2,1)}), bf16[32,2,3712]{2,1,0:T(2,128)(2,1)S(1)}, u32[]{:S(2)}, u32[]{:S(2)}) async-start(bf16[32,2,3712]{2,1,0:T(2,128)(2,1)} %reshape.427), calls=%async_computation.5 | async-start | bytes 950272 | tf_op jit(solution)/shard_map/all_to_all | solution.py:1605
  782.3 32.5 %copy-start.5 = (bf16[320,2048]{1,0:T(8,128)(2,1)S(1)}, bf16[320,2048]{1,0:T(8,128)(2,1)}, u32[]{:S(2)}) copy-start(bf16[320,2048]{1,0:T(8,128)(2,1)} %tokens_ref.1) | copy-start | bytes 3932164
  782.3 32.5 %copy-start.23 = (f32[1,2048]{1,0:T(1,128)S(1)}, f32[1,2048]{1,0:T(1,128)}, u32[]{:S(2)}) copy-start(f32[1,2048]{1,0:T(1,128)} %get-tuple-element.113.gain_ref) | copy-start | bytes 24580
  (25 other events, 87.7 us)
Sparse Core Ops, SparseCore 0:
  9.9 102.5 all-gather.3
  114.4 83.3 all-gather.5
  199.7 160.7 all-gather.7
  463.4 53.9 reduce-scatter.3
  611.6 81.8 reduce-scatter.5
  706.2 108.5 reduce-scatter.7
